TPU v7x, 128 devices: a whole 4x4x4 slice. The times are simulated.
128 devices in a mesh: gx: 16 (over z, y), gy: 8 (over x, core).
Axes of the slice: x: 4, y: 4, z: 4, core: 2. Of those that a mesh axis runs over, the one named last changes fastest.
Arguments:
- inputs: bfloat16 [2, 64, 64, 64, 512], P(None, 'gx', 'gy'), may hold values from -6 to 6
- cotangent: bfloat16 [2, 64, 64, 64, 512], P(None, 'gx', 'gy'), may hold values from -6 to 6
- pre_activation: bfloat16 [2, 64, 64, 64, 512], P(None, 'gx', 'gy'), may hold values from -6 to 6
- pointwise: bfloat16 [32, 32], replicated, may hold values from -1 to 1
- spectral: bfloat16 [24, 24, 192, 1024], P(None, 'gy', 'gx'), may hold values from -4 to 4
Outputs:
- input_grad: bfloat16 [2, 64, 64, 64, 512], P(None, 'gx', 'gy')
- spectral_grad: float32 [24, 24, 192, 1024], P(None, 'gy', 'gx')
All inputs are finite; a program needn't handle non-finite values.
Results may differ from a plain program's by a relative error of at most 0.0083.
Values sent between devices are 32-bit elements; how exact they have to be, the bound alone decides.
No kernel may reach another device: no remote copies, remote signals or barrier semaphores. Data moves between devices by JAX's collectives and lax.ppermute only.
A program may use at most 192 MiB of HBM per device.

v0:
```python
import math

import jax
import jax.numpy as jnp
from jax import lax
from jax.sharding import PartitionSpec as P

X = 64
Y = 64
Z = 64
NT = 16
MS = 12
MT = 8
KS = 24


def fourier(length, frequencies):
    points = jnp.arange(length, dtype=jnp.float32)[:, None]
    orders = jnp.arange(frequencies, dtype=jnp.float32)[None, :]
    scales = jnp.where(orders == 0.0, math.sqrt(1.0 / length), math.sqrt(2.0 / length))
    cosines = scales * jnp.cos(2.0 * math.pi * points * orders / length)
    sines = math.sqrt(2.0 / length) * jnp.sin(2.0 * math.pi * points * (orders + 1.0) / length)
    return jnp.concatenate([cosines, sines], axis=1)


def cosine(length, modes):
    points = jnp.arange(length, dtype=jnp.float32)[:, None]
    orders = jnp.arange(modes, dtype=jnp.float32)[None, :]
    scales = jnp.where(orders == 0.0, math.sqrt(1.0 / length), math.sqrt(2.0 / length))
    return scales * jnp.cos(math.pi * orders * (points + 0.5) / length)


def gelu_slope(values):
    normal_cdf = 0.5 * (1.0 + jax.scipy.special.erf(values * 0.7071067811865476))
    density = 0.3989422804014327 * jnp.exp(-0.5 * values * values)
    return normal_cdf + values * density


def time_table(time_short, channels):
    identity = jnp.eye(channels, dtype=jnp.float32)
    table = time_short.astype(jnp.float32)[:, None, :, None] * identity[None, :, None, :]
    return table.reshape(time_short.shape[0] * channels, time_short.shape[1] * channels).astype(
        jnp.bfloat16
    )


def analyse_local(stacked, third_basis, table):
    high = lax.Precision.HIGHEST
    leading = stacked.shape[:3]
    depth = stacked.shape[3]
    timed = jnp.dot(
        stacked.reshape(-1, stacked.shape[4]), table, preferred_element_type=jnp.float32
    )
    timed = timed.reshape(-1, depth, table.shape[1])
    sectioned = jnp.einsum("nzs,zk->nks", timed, third_basis, precision=high)
    return sectioned.reshape(leading + (-1,))


def synthesise_local(modes, third_basis, table_wide):
    high = lax.Precision.HIGHEST
    leading = modes.shape[:3]
    blocks = modes.reshape(-1, third_basis.shape[1], table_wide.shape[1])
    sectioned = jnp.einsum("nks,zk->nzs", blocks, third_basis, precision=high)
    flat = jnp.dot(
        sectioned.reshape(-1, table_wide.shape[1]),
        table_wide.T,
        precision=high,
        preferred_element_type=jnp.float32,
    )
    return flat.reshape(leading + (third_basis.shape[0], -1))


def body(inputs, cotangent, pre_activation, pointwise, spectral):
    high = lax.Precision.HIGHEST
    first_count = lax.axis_size("gx")
    second_index = lax.axis_index("gy")
    samples = inputs.shape[0]
    first_local = inputs.shape[1]
    second_local = inputs.shape[2]
    channels = pointwise.shape[0]
    mode_rows = spectral.shape[1]
    block_modes = spectral.shape[2]
    local_columns = block_modes * channels
    first_basis = fourier(X, MS)
    second_basis = fourier(Y, MS)
    third_short = fourier(Z, MS).astype(jnp.bfloat16)
    time_short = cosine(NT, MT).astype(jnp.bfloat16)
    third_basis = third_short.astype(jnp.float32)
    table = time_table(time_short, channels)
    table_wide = table.astype(jnp.float32)
    second_local_basis = lax.dynamic_slice_in_dim(
        second_basis, second_index * second_local, second_local, 0
    )
    values = pre_activation.astype(jnp.float32)
    grad_pre = (cotangent.astype(jnp.float32) * gelu_slope(values)).astype(jnp.bfloat16)
    stacked = jnp.concatenate([inputs, grad_pre], axis=0)
    partial_modes = analyse_local(stacked, third_basis, table)
    turned = lax.all_to_all(
        partial_modes.reshape(2 * samples, first_local, second_local, first_count, local_columns),
        "gx",
        split_axis=3,
        concat_axis=1,
        tiled=True,
    )
    turned = turned.reshape(2 * samples, first_count * first_local, second_local, local_columns)
    first_modes = jnp.einsum("bxyn,xm->bmyn", turned, first_basis, precision=high)
    basis_part = second_local_basis
    coefficients = lax.psum_scatter(
        jnp.einsum("bmyn,yk->kbmn", first_modes, basis_part, precision=high),
        "gy",
        scatter_dimension=0,
        tiled=True,
    )
    shaped = coefficients.reshape(mode_rows, 2 * samples, KS, block_modes, channels)
    input_modes = shaped[:, :samples]
    grad_modes = shaped[:, samples:]
    spectral_grad = jnp.einsum("kbmqc,kbmqo->mkqco", input_modes, grad_modes, precision=high)
    spectral_grad = spectral_grad.reshape(KS, mode_rows, block_modes, channels * channels)
    weights = spectral.astype(jnp.float32).reshape(KS, mode_rows, block_modes, channels, channels)
    mode_grad = jnp.einsum("mkqco,kbmqo->kbmqc", weights, grad_modes, precision=high)
    mode_grad = mode_grad.reshape(mode_rows, samples, KS, local_columns)
    basis_part = second_local_basis
    lateral = jnp.einsum(
        "kbmn,yk->bmyn",
        lax.all_gather(mode_grad, "gy", axis=0, tiled=True),
        basis_part,
        precision=high,
    )
    first_back = jnp.einsum("bmyn,xm->bxyn", lateral, first_basis, precision=high)
    first_back = first_back.reshape(samples, first_count, first_local, second_local, local_columns)
    returned = lax.all_to_all(first_back, "gx", split_axis=1, concat_axis=4, tiled=True)
    returned = returned.reshape(samples, first_local, second_local, first_count * local_columns)
    synthesized = synthesise_local(returned, third_basis, table_wide)
    direct = jnp.dot(
        grad_pre.reshape(-1, channels), pointwise.T, preferred_element_type=jnp.float32
    )
    direct = direct.reshape(inputs.shape)
    input_grad = (direct + synthesized).astype(jnp.bfloat16)
    return (input_grad, spectral_grad)


def solution(mesh):
    in_specs = (
        P(None, "gx", "gy", None, None),
        P(None, "gx", "gy", None, None),
        P(None, "gx", "gy", None, None),
        P(),
        P(None, "gy", "gx", None),
    )
    out_specs = (P(None, "gx", "gy", None, None), P(None, "gy", "gx", None))
    return jax.shard_map(body, mesh=mesh, in_specs=in_specs, out_specs=out_specs, check_vma=False)
```

profile of v0, /device:TPU:8, one launch (start us, length us, event | category | flops | bytes accessed | tf_op | source)
XLA Modules:
  0.0 306.0 jit_solution(12966443726839419774)
XLA Ops:
  8.4 7.6 %fusion.7 = bf16[2,4,8,64,512]{4,3,2,1,0:T(8,128)(2,1)} fusion(bf16[2,4,8,64,512]{4,3,2,1,0:T(8,128)(2,1)} %param.7, bf16[2,4,8,64,512]{4,3,2,1,0:T(8,128)(2,1)} %param.6), kind=kLoop, calls=%fused_computation.13 | loop fusion | flops 25165824 | bytes 12582912 | tf_op jit(solution)/shard_map/convert_element_type | solution.py:95
  16.0 7.4 %pad_maximum_fusion = bf16[4,4,8,64,512]{4,3,2,1,0:T(8,128)(2,1)} fusion(bf16[2,4,8,64,512]{4,3,2,1,0:T(8,128)(2,1)} %fusion.7, bf16[2,4,8,64,512]{4,3,2,1,0:T(8,128)(2,1)} %param.5), kind=kLoop, calls=%fused_computation.11 | loop fusion | flops 4194304 | bytes 16777216 | tf_op jit(solution)/shard_map/concatenate | solution.py:96
  23.5 5.7 %fusion.53 = f32[128,64,256]{2,1,0:T(8,128)S(1)} fusion(bf16[128,64,512]{2,1,0:T(8,128)(2,1)} %bitcast.73, bf16[512,256,1]{1,0,2:T(8,128)(2,1)S(1)} %reshape.147), kind=kOutput, calls=%fused_computation.65 | convolution fusion | flops 2147483648 | bytes 17039360 | tf_op jit(solution)/shard_map/dot_general | solution.py:51
  29.3 4.6 %convolution_bitcast_fusion = f32[128,24,256]{2,1,0:T(8,128)} fusion(f32[128,64,256]{2,1,0:T(8,128)S(1)} %fusion.53, f32[64,12]{0,1:T(8,128)S(1)} %get-tuple-element.7, f32[64,12]{0,1:T(8,128)S(1)} %get-tuple-element.6), kind=kOutput, calls=%fused_computation.19 | convolution fusion | flops 603985920 | bytes 11540480 | tf_op jit(solution)/shard_map/nzs,zk->nks/dot_general | solution.py:55
  34.0 3.0 reshape_reshape.6
  37.0 2.6 copy.45
  39.6 8.4 %all-to-all-start = ((f32[4,4,8,16,384]{4,2,1,0,3:T(8,128)}), f32[4,4,8,16,384]{4,2,1,0,3:T(8,128)S(1)}, u32[]{:S(2)}, u32[]{:S(2)}) async-start(f32[4,4,8,16,384]{4,2,1,0,3:T(8,128)} %copy.45), calls=%async_computation | async-start | bytes 6291456 | tf_op jit(solution)/shard_map/all_to_all | solution.py:98
  48.3 42.9 %all-to-all-done = f32[4,4,8,16,384]{4,2,1,0,3:T(8,128)S(1)} async-done(((f32[4,4,8,16,384]{4,2,1,0,3:T(8,128)}), f32[4,4,8,16,384]{4,2,1,0,3:T(8,128)S(1)}, u32[]{:S(2)}, u32[]{:S(2)}) %all-to-all-start) | async-done | bytes 3145760 | tf_op jit(solution)/shard_map/all_to_all | solution.py:98
  93.4 3.1 %fusion.23 = f32[24,4,24,384]{3,0,2,1:T(8,128)S(1)} fusion(f32[4,24,8,384]{3,1,2,0:T(8,128)S(1)} %fusion.14, s32[]{:T(128)S(6)} %select_n.26, f32[64,12]{0,1:T(8,128)S(1)} %get-tuple-element.6, f32[64,12]{0,1:T(8,128)S(1)} %get-tuple-element.7), kind=kOutput, calls=%fused_computation.26 | convolution fusion | flops 84934848 | bytes 4724740 | tf_op jit(solution)/shard_map/bmyn,yk->kbmn/dot_general | solution.py:109
  96.5 2.4 copy.50
  99.0 6.7 %reshape.143 = bf16[24,3,12,32,32]{4,3,0,2,1:T(8,128)(2,1)} reshape(bf16[24,3,12,1024]{3,0,2,1:T(8,128)(2,1)S(1)} %copy-done.5) | data formatting | bytes 3538944 | tf_op jit(solution)/shard_map/reshape | solution.py:119
  105.7 32.6 %reduce-scatter.2.cloned.1.call-done = f32[3,4,24,384]{3,2,1,0:T(8,128)} async-done(((f32[24,4,24,384]{3,2,1,0:T(8,128)}), f32[3,4,24,384]{3,2,1,0:T(8,128)}) %reduce-scatter.2.cloned.1.call-update) | async-done | bytes 442384 | tf_op jit(solution)/shard_map/reduce_scatter | solution.py:108
  141.2 13.2 %fusion.17 = f32[3,2,24,12,32]{4,1,3,2,0:T(2,128)S(1)} fusion(bf16[24,3,12,32,32]{4,3,0,2,1:T(8,128)(2,1)} %reshape.143, f32[3,2,24,12,32]{4,3,2,1,0:T(8,128)S(1)} %get-tuple-element.5), kind=kOutput, calls=%fused_computation.24 | convolution fusion | flops 21233664 | bytes 2211840 | tf_op jit(solution)/shard_map/mkqco,kbmqo->kbmqc/dot_general | solution.py:120
  155.7 19.2 %reshape.139 = bf16[65536,32]{1,0:T(8,128)(2,1)} reshape(bf16[2,4,8,64,512]{4,3,2,1,0:T(8,128)(2,1)} %fusion.7) | data formatting | bytes 8388608 | tf_op jit(solution)/shard_map/reshape | solution.py:135
  174.8 4.4 %all-gather.2.cloned.1.call-done = f32[24,2,24,384]{3,2,1,0:T(8,128)} async-done(((f32[3,2,24,384]{3,2,1,0:T(8,128)}), f32[24,2,24,384]{3,2,1,0:T(8,128)}) %all-gather.2.cloned.1.call-update) | async-done | bytes 1769488 | tf_op jit(solution)/shard_map/all_gather | solution.py:125
  179.2 3.0 fusion.20
  185.3 3.0 copy.57
  188.3 16.1 %all-to-all-start.1 = ((f32[2,16,4,8,384]{4,2,3,0,1:T(4,128)}), f32[2,16,4,8,384]{4,2,3,0,1:T(4,128)}, u32[]{:S(2)}, u32[]{:S(2)}) async-start(f32[2,16,4,8,384]{4,2,3,0,1:T(4,128)} %copy.57), calls=%async_computation.2 | async-start | bytes 3145728 | tf_op jit(solution)/shard_map/all_to_all | solution.py:131
  204.4 19.5 %fusion.52 = f32[65536,32]{1,0:T(8,128)} fusion(bf16[65536,32]{1,0:T(8,128)(2,1)} %reshape.139, bf16[32,32]{1,0:T(8,128)(2,1)S(1)} %copy-done), kind=kOutput, calls=%fused_computation.64 | convolution fusion | flops 134217728 | bytes 12584960 | tf_op jit(solution)/shard_map/dot_general | solution.py:134
  225.3 24.8 %reshape.140 = f32[2,4,8,64,512]{4,3,2,1,0:T(8,128)} reshape(f32[65536,32]{1,0:T(8,128)} %fusion.52) | data formatting | bytes 16777216 | tf_op jit(solution)/shard_map/reshape | solution.py:137
  250.1 24.8 %fusion.25 = f32[24,3,12,32,32]{4,3,0,2,1:T(8,128)} fusion(f32[3,2,24,12,32]{4,3,2,1,0:T(8,128)S(1)} %get-tuple-element.5, f32[3,2,24,12,32]{4,3,2,1,0:T(8,128)S(1)} %copy-done.4), kind=kOutput, calls=%fused_computation.28 | convolution fusion | flops 21233664 | bytes 3981312 | tf_op jit(solution)/shard_map/kbmqc,kbmqo->mkqco/dot_general | solution.py:117
  274.9 11.9 %reshape.146 = f32[24,3,12,1024]{3,0,2,1:T(8,128)} reshape(f32[24,3,12,32,32]{4,3,0,2,1:T(8,128)} %fusion.25) | data formatting | bytes 7077888 | tf_op jit(solution)/shard_map/reshape | solution.py:118
  286.8 2.3 copy.58
  291.6 7.4 %add_convert_fusion = bf16[2,4,8,64,512]{4,3,2,1,0:T(8,128)(2,1)} fusion(f32[2,4,8,64,512]{4,3,2,1,0:T(8,128)} %reshape.140, f32[2,4,8,64,256]{4,3,2,1,0:T(8,128)S(1)} %bitcast.74, bf16[512,256,1,1,1]{1,0,2,3,4:T(8,128)(2,1)S(1)} %copy-done.6), kind=kOutput, calls=%fused_computation.12 | convolution fusion | flops 6446645248 | bytes 17039360 | tf_op jit(solution)/shard_map/dot_general | solution.py:64
  (46 shorter events, 14.9 us)
Async XLA Ops:
  7.2 197.2 %copy-start = (bf16[32,32]{1,0:T(8,128)(2,1)S(1)}, bf16[32,32]{1,0:T(8,128)(2,1)}, u32[]{:S(2)}) copy-start(bf16[32,32]{1,0:T(8,128)(2,1)} %param.8) | copy-start | bytes 6148
  7.7 8.3 %copy-start.2 = (bf16[16,32,8,32]{3,2,1,0:T(8,128)(2,1)}, bf16[16,32,8,32]{3,2,1,0:T(8,128)(2,1)S(1)}, u32[]{:S(2)}) copy-start(bf16[16,32,8,32]{3,2,1,0:T(8,128)(2,1)S(1)} %multiply_convert_fusion) | copy-start | bytes 786436
  29.3 64.1 %copy-start.7 = (f32[64,12]{0,1:T(8,128)}, f32[64,12]{0,1:T(8,128)S(1)}, u32[]{:S(2)}) copy-start(f32[64,12]{0,1:T(8,128)S(1)} %get-tuple-element.7) | copy-start | bytes 9220
  39.6 51.6 %all-to-all-start = ((f32[4,4,8,16,384]{4,2,1,0,3:T(8,128)}), f32[4,4,8,16,384]{4,2,1,0,3:T(8,128)S(1)}, u32[]{:S(2)}, u32[]{:S(2)}) async-start(f32[4,4,8,16,384]{4,2,1,0,3:T(8,128)} %copy.45), calls=%async_computation | async-start | bytes 6291456 | tf_op jit(solution)/shard_map/all_to_all | solution.py:98
  48.0 90.3 %reduce-scatter.2.cloned.1.call-start = ((), (), s32[]{:S(2)}) async-start(), calls=%async_computation.3 | async-start | bytes 3981312 | tf_op jit(solution)/shard_map/reduce_scatter | solution.py:108
  96.5 2.5 copy-start.5
  98.9 80.3 %all-gather.2.cloned.1.call-start = ((), (), s32[]{:S(2)}) async-start(), calls=%async_computation.4 | async-start | bytes 1990656 | tf_op jit(solution)/shard_map/all_gather | solution.py:125
  155.6 23.5 %copy-start.8 = (f32[64,12]{0,1:T(8,128)S(1)}, f32[64,12]{0,1:T(8,128)}, u32[]{:S(2)}) copy-start(f32[64,12]{0,1:T(8,128)} %copy-done.7) | copy-start | bytes 9220
  188.3 98.6 %all-to-all-start.1 = ((f32[2,16,4,8,384]{4,2,3,0,1:T(4,128)}), f32[2,16,4,8,384]{4,2,3,0,1:T(4,128)}, u32[]{:S(2)}, u32[]{:S(2)}) async-start(f32[2,16,4,8,384]{4,2,3,0,1:T(4,128)} %copy.57), calls=%async_computation.2 | async-start | bytes 3145728 | tf_op jit(solution)/shard_map/all_to_all | solution.py:131
  204.4 19.5 %copy-start.3 = (bf16[16,32,8,32]{3,2,1,0:T(8,128)(2,1)S(1)}, bf16[16,32,8,32]{3,2,1,0:T(8,128)(2,1)}, u32[]{:S(2)}) copy-start(bf16[16,32,8,32]{3,2,1,0:T(8,128)(2,1)} %copy-done.2) | copy-start | bytes 786436
  225.3 24.8 %copy-start.4 = (f32[3,2,24,12,32]{4,3,2,1,0:T(8,128)S(1)}, f32[3,2,24,12,32]{4,3,2,1,0:T(8,128)}, u32[]{:S(2)}) copy-start(f32[3,2,24,12,32]{4,3,2,1,0:T(8,128)} %get-tuple-element.4) | copy-start | bytes 663556
  286.8 2.8 copy-start.9
  289.2 2.4 copy-start.6
  291.5 7.4 %copy-start.1 = (bf16[32,32]{1,0:T(8,128)(2,1)S(1)}, bf16[32,32]{1,0:T(8,128)(2,1)}, u32[]{:S(2)}) copy-start(bf16[32,32]{1,0:T(8,128)(2,1)} %param.8) | copy-start | bytes 6148
Sparse Core Ops, SparseCore 0:
  99.1 39.1 reduce-scatter.1
  155.8 23.3 all-gather.1
where the time goes:
time: 311 us; the launch traced here: 306 us
  matrix products  86.6 us (28%)
  local copies, waits for them, and re-layouts  84.6 us (27%)
  waiting for transfers between devices  79.9 us (26%)
  starting transfers between devices  24.8 us (8%)
  other arithmetic  15.6 us (5%)
  between operations  14.5 us (5%)
    all_to_all x1, waiting for transfers between devices, body(): lax.all_to_all(partial_modes.reshape(2 * samples, first_local, second_loc...  42.9 us
    reduce_scatter x1, waiting for transfers between devices, body(): lax.psum_scatter(jnp.einsum('bmyn,yk->kbmn', first_modes, basis_part, pre...  32.6 us
    reshape x1, local copies, waits for them, and re-layouts, body(): direct = direct.reshape(inputs.shape)  24.8 us
    dot_general x1, matrix products, body(): jnp.einsum('kbmqc,kbmqo->mkqco', input_modes, grad_modes, precision=high)  24.8 us
    dot_general x1, matrix products, body(): jnp.dot(grad_pre.reshape(-1, channels), pointwise.T, preferred_element_ty...  19.5 us
    reshape x1, local copies, waits for them, and re-layouts, body(): grad_pre.reshape(-1, channels)  19.2 us
    all_to_all x1, starting transfers between devices, body(): lax.all_to_all(first_back, 'gx', split_axis=1, concat_axis=4, tiled=True)  16.1 us
    dot_general x1, matrix products, body(): jnp.einsum('mkqco,kbmqo->kbmqc', weights, grad_modes, precision=high)  13.2 us
  transfers between devices with their start and end apart: 4, of which 3 were waited for; matrix products, arithmetic and copies ran while one was open for 35% of the time, Pallas kernels for 0%

commit v1 on v0

v1 whole, which is shorter than its diff:
```python
import functools
import math

import jax
import jax.numpy as jnp
import ml_dtypes
import numpy as np
from jax import lax
from jax.experimental import pallas as pl
from jax.experimental.pallas import tpu as pltpu
from jax.sharding import PartitionSpec as P

N = 64
NT = 16
MS = 12
MT = 8
KS = 24
C = 32
BF = ml_dtypes.bfloat16
F32 = jnp.float32
BF16 = jnp.bfloat16
MIB = 1 << 20


def fourier(length, frequencies):
    points = np.arange(length, dtype=np.float64)[:, None]
    orders = np.arange(frequencies, dtype=np.float64)[None, :]
    scales = np.where(orders == 0.0, math.sqrt(1.0 / length), math.sqrt(2.0 / length))
    cosines = scales * np.cos(2.0 * math.pi * points * orders / length)
    sines = math.sqrt(2.0 / length) * np.sin(2.0 * math.pi * points * (orders + 1.0) / length)
    return np.concatenate([cosines, sines], axis=1).astype(np.float32)


def cosine(length, modes):
    points = np.arange(length, dtype=np.float64)[:, None]
    orders = np.arange(modes, dtype=np.float64)[None, :]
    scales = np.where(orders == 0.0, math.sqrt(1.0 / length), math.sqrt(2.0 / length))
    return (scales * np.cos(math.pi * orders * (points + 0.5) / length)).astype(np.float32)


def constants():
    basis = fourier(N, MS)
    third = basis.astype(BF).astype(np.float32)
    time = cosine(NT, MT).astype(BF).astype(np.float32)
    eye_c = np.eye(C, dtype=np.float32)
    eye_r = np.eye(8, dtype=np.float32)
    out = {}
    tables = np.zeros((4, NT, C, 2, 4, C), np.float32)
    for pair in range(4):
        for kt in range(MT):
            half, q = divmod(kt, 4)
            tables[pair, :, :, half, (q + pair) % 4, :] = time[:, kt][:, None, None] * eye_c[None]
    tables = tables.reshape(4, NT * C, MT * C)
    out["tables"] = tables.astype(BF)
    out["tables_t"] = np.swapaxes(tables, 1, 2).copy().astype(BF)
    zl = np.einsum("zk,rs->krsz", third, eye_r).reshape(KS * 8, 8 * N)
    out["zl"] = zl.astype(BF)
    out["zl_t"] = np.concatenate([zl.T, np.zeros((8 * N, 64), np.float32)], axis=1).astype(BF)
    high = basis.astype(BF).astype(np.float32)
    low = (basis - high).astype(BF).astype(np.float32)
    eye_h = np.eye(2, dtype=np.float32)
    forms = [np.einsum("xk,hg->hkxg", part, eye_h).reshape(2 * KS, 2 * N) for part in (high, low)]
    out["xl"] = np.concatenate(forms, axis=1).astype(BF)
    out["xl_t"] = np.concatenate([form.T for form in forms], axis=1).astype(BF)
    padded = np.zeros((N, 8, 4), np.float32)
    padded[:, :, :3] = basis.reshape(N, 8, 3)
    y = padded.reshape(8, 4, 2, 32)
    yb = np.einsum("slhk,cd->hslckd", y, eye_c).reshape(2, 8 * 4 * C, 32 * C)
    out["yb"] = yb.astype(BF)
    spread = np.zeros((3, 4, C, 4, C), np.float32)
    gather = np.zeros((3, C, C, 4, C), np.float32)
    wide = np.zeros((3, 4, C, C, C), np.float32)
    for ky in range(3):
        spread[ky, ky] = eye_c[:, None, :]
        gather[ky, :, :, ky, :] = eye_c[:, None, :]
        wide[ky, ky] = eye_c[:, :, None]
    out["spread"] = spread.reshape(3, 128, 128).astype(BF)
    out["gather"] = gather.reshape(3, C * C, 128).astype(BF)
    out["wide"] = wide.reshape(3, 128, C * C).astype(BF)
    return out


def dot(a, b):
    return jnp.dot(a, b, preferred_element_type=F32)


def dot_t(a, b):
    return lax.dot_general(a, b, (((1,), (1,)), ((), ())), preferred_element_type=F32)


def gelu_slope(v):
    cdf = 0.5 * (1.0 + lax.erf(v * 0.7071067811865476))
    return cdf + v * (0.3989422804014327 * jnp.exp(-0.5 * v * v))


def lane_group(rows):
    return lax.broadcasted_iota(jnp.int32, (rows, 128), 1) // C


def analyse_field(field, table_ref, zl_ref, parts, sent_ref):
    pair = pl.program_id(1)
    timed = dot(field, table_ref[0]).astype(BF16)
    parts[pair] = dot(zl_ref[...], timed)

    @pl.when(pair == 3)
    def _():
        group = lane_group(8 * KS)
        for half in range(2):
            lanes = slice(half * 128, half * 128 + 128)
            for q in range(4):
                value = parts[(-q) % 4, :, lanes]
                for p in range(1, 4):
                    value = jnp.where(group == p, parts[(p - q) % 4, :, lanes], value)
                if q:
                    value = pltpu.roll(value, 128 - q * C, 1)
                for kz in range(KS):
                    block, slot = divmod(2 * kz + half, 3)
                    sent_ref[block, q, slot] = value[kz * 8 : kz * 8 + 8]


def analyse_grad_kernel(cot_ref, pre_ref, table_ref, zl_ref, sent_ref, grad_ref, flat, parts):
    cot = cot_ref.at[0]
    pre = pre_ref.at[0]

    def slope(i, carry):
        x, y = i // 2, i % 2
        for j in range(4):
            rows = pl.ds(j * 16, 16)
            v = pre[x, y, rows, :].astype(F32)
            g = cot[x, y, rows, :].astype(F32)
            grad = (g * gelu_slope(v)).astype(BF16)
            grad_ref[0, x, y, rows, :] = grad
            flat[pl.ds(pl.multiple_of(i * N + j * 16, 16), 16), :] = grad
        return carry

    lax.fori_loop(0, 8, slope, 0)
    analyse_field(flat[...], table_ref, zl_ref, parts, sent_ref)


def analyse_input_kernel(field_ref, table_ref, zl_ref, sent_ref, parts):
    analyse_field(field_ref[0].reshape(8 * N, NT * C), table_ref, zl_ref, parts, sent_ref)


FIELD = pl.BlockSpec((1, 4, 2, N, NT * C), lambda b, p: (b, 0, p, 0, 0))
TABLE = pl.BlockSpec((1, NT * C, MT * C), lambda b, p: (p, 0, 0))
TABLE_T = pl.BlockSpec((1, MT * C, NT * C), lambda b, p: (p, 0, 0))
SENT = pl.BlockSpec((16, 4, 3, 8, 128), lambda b, p: (0, b, 0, 0, 0))
SENT_SHAPE = jax.ShapeDtypeStruct((16, 8, 3, 8, 128), F32)
PART_SHAPE = jax.ShapeDtypeStruct((72, 128), F32)


def whole(shape):
    return pl.BlockSpec(shape, lambda *ids: (0,) * len(shape))


def params(limit):
    return pltpu.CompilerParams(vmem_limit_bytes=limit * MIB)


def analyse_grad(cotangent, pre_activation, k):
    return pl.pallas_call(
        analyse_grad_kernel,
        grid=(2, 4),
        in_specs=[FIELD, FIELD, TABLE, whole((8 * KS, 8 * N))],
        out_specs=[SENT, FIELD],
        out_shape=[SENT_SHAPE, jax.ShapeDtypeStruct(cotangent.shape, BF16)],
        scratch_shapes=[pltpu.VMEM((8 * N, NT * C), BF16), pltpu.VMEM((4, 8 * KS, MT * C), F32)],
        compiler_params=params(24),
        cost_estimate=pl.CostEstimate(flops=4 * 10**9, bytes_accessed=14 * 10**6, transcendentals=4 * 10**6),
        name="analyse_grad",
    )(cotangent, pre_activation, k["tables"], k["zl"])


def analyse_input(inputs, k):
    return pl.pallas_call(
        analyse_input_kernel,
        grid=(2, 4),
        in_specs=[FIELD, TABLE, whole((8 * KS, 8 * N))],
        out_specs=SENT,
        out_shape=SENT_SHAPE,
        scratch_shapes=[pltpu.VMEM((4, 8 * KS, MT * C), F32)],
        compiler_params=params(24),
        cost_estimate=pl.CostEstimate(flops=4 * 10**9, bytes_accessed=6 * 10**6, transcendentals=0),
        name="analyse_input",
    )(inputs, k["tables"], k["zl"])


def planes_forward_kernel(got_ref, xl_ref, yb_ref, *rest):
    outs, blocks = rest[:8], rest[8]
    me = lax.axis_index("gy")
    firsts = []
    for slot in range(3):
        field = jnp.concatenate(
            [got_ref[:, s, slot].reshape(128, 128).astype(BF16) for s in range(8)], axis=1
        )
        firsts.append(dot(xl_ref[...], jnp.concatenate([field, field], axis=0)))
    total = None
    for half in range(2):
        rows = jnp.concatenate([f[half * KS : half * KS + KS] for f in firsts], axis=0)
        term = dot(rows.astype(BF16), yb_ref[half])
        total = term if total is None else total + term
    for s in range(8):
        blocks[s] = total[:, s * 128 : s * 128 + 128]
    for s in range(8):
        outs[s][...] = blocks[me ^ s]


def planes_forward(got, k):
    return pl.pallas_call(
        planes_forward_kernel,
        out_shape=[PART_SHAPE] * 8,
        scratch_shapes=[pltpu.VMEM((8, 72, 128), F32)],
        compiler_params=params(32),
        cost_estimate=pl.CostEstimate(flops=10**9, bytes_accessed=6 * 10**6, transcendentals=0),
        name="planes_forward",
    )(got, k["xl"], k["yb"])


def planes_back_kernel(*refs):
    parts, (xl_ref, yb_ref, sent_ref, blocks) = refs[:8], refs[8:]
    me = lax.axis_index("gy")
    for s in range(8):
        blocks[me ^ s] = parts[s][...]
    field = jnp.concatenate([blocks[s] for s in range(8)], axis=1).astype(BF16)
    halves = [dot_t(field, yb_ref[half]) for half in range(2)]
    for slot in range(3):
        rows = slice(slot * KS, slot * KS + KS)
        both = jnp.concatenate([half[rows] for half in halves], axis=0).astype(BF16)
        wide = dot(xl_ref[...], jnp.concatenate([both, both], axis=0))
        for s in range(8):
            sent_ref[:, s, slot] = wide[:, s * 128 : s * 128 + 128].reshape(16, 8, 128)


def planes_back(parts, k):
    return pl.pallas_call(
        planes_back_kernel,
        out_shape=SENT_SHAPE,
        scratch_shapes=[pltpu.VMEM((8, 72, 128), F32)],
        compiler_params=params(32),
        cost_estimate=pl.CostEstimate(flops=10**9, bytes_accessed=6 * 10**6, transcendentals=0),
        name="planes_back",
    )(*parts, k["xl_t"], k["yb"])


def mode_grad_kernel(*refs):
    parts, (weight_ref, spread_ref, gather_ref), outs, products = refs[:8], refs[8:11], refs[11:19], refs[19]
    me = lax.axis_index("gy")
    field = jnp.concatenate([part[...] for part in parts], axis=0).astype(BF16)
    total = None
    for ky in range(3):
        copies = dot(field, spread_ref[ky])
        for s in range(8):
            q = (me ^ s) & 3
            for slot in range(3):
                at = s * 72 + slot * KS
                weight = weight_ref[ky, slot * 4 + q].astype(F32)
                copy = copies[at : at + KS]
                products[at : at + KS, :] = weight * jnp.concatenate([copy] * 8, axis=1)
        term = dot(products[...].astype(BF16), gather_ref[ky])
        total = term if total is None else total + term
    for s in range(8):
        outs[s][...] = total[s * 72 : s * 72 + 72]


def mode_grad(parts, weights, k):
    return pl.pallas_call(
        mode_grad_kernel,
        out_shape=[PART_SHAPE] * 8,
        scratch_shapes=[pltpu.VMEM((576, C * C), F32)],
        compiler_params=params(32),
        cost_estimate=pl.CostEstimate(flops=10**9, bytes_accessed=4 * 10**6, transcendentals=0),
        name="mode_grad",
    )(*parts, weights, k["spread"], k["gather"])


def spectral_grad_kernel(*refs):
    grads, fields, (spread_ref, wide_ref, out_ref) = refs[:8], refs[8:16], refs[16:]
    me = lax.axis_index("gy")
    grad = jnp.concatenate([part[...] for part in grads], axis=0).astype(BF16)
    field = jnp.concatenate([part[...] for part in fields], axis=0).astype(BF16)
    copies = dot(grad, spread_ref[0])
    wide = dot(field, wide_ref[0])
    for s in range(4):
        q = (me ^ s) & 3
        for slot in range(3):
            total = None
            for at in (s * 72 + slot * KS, (s + 4) * 72 + slot * KS):
                term = wide[at : at + KS] * jnp.concatenate([copies[at : at + KS]] * 8, axis=1)
                total = term if total is None else total + term
            out_ref[0, slot * 4 + q] = total


def spectral_grad(grads, fields, k):
    return pl.pallas_call(
        spectral_grad_kernel,
        grid=(3,),
        in_specs=[whole((72, 128))] * 16
        + [
            pl.BlockSpec((1, 128, 128), lambda i: (i, 0, 0)),
            pl.BlockSpec((1, 128, C * C), lambda i: (i, 0, 0)),
        ],
        out_specs=pl.BlockSpec((1, 12, KS, C * C), lambda i: (i, 0, 0, 0)),
        out_shape=jax.ShapeDtypeStruct((3, 12, KS, C * C), F32),
        compiler_params=params(32),
        cost_estimate=pl.CostEstimate(flops=10**9, bytes_accessed=4 * 10**6, transcendentals=0),
        name="spectral_grad",
    )(*grads, *fields, k["spread"], k["wide"])


def synthesise_kernel(got_ref, grad_ref, table_ref, zl_ref, mix_ref, out_ref, parts):
    pair = pl.program_id(1)

    @pl.when(pair == 0)
    def _():
        group = lane_group(8 * KS)
        for half in range(2):
            turned = []
            for q in range(4):
                tiles = []
                for kz in range(KS):
                    block, slot = divmod(2 * kz + half, 3)
                    tiles.append(got_ref[block, q, slot])
                value = jnp.concatenate(tiles, axis=0)
                turned.append(pltpu.roll(value, q * C, 1) if q else value)
            for p in range(4):
                value = turned[(-p) % 4]
                for g in range(1, 4):
                    value = jnp.where(group == g, turned[(g - p) % 4], value)
                parts[p, :, half * 128 : half * 128 + 128] = value

    timed = dot(parts[pair].astype(BF16), table_ref[0]).astype(BF16)
    timed = jnp.concatenate([timed, jnp.zeros((64, NT * C), BF16)], axis=0)
    grad = grad_ref[0].reshape(8 * N, NT * C)
    for side in range(2):
        lanes = slice(side * 256, side * 256 + 256)
        left = jnp.concatenate([zl_ref[...], grad[:, lanes]], axis=1)
        right = jnp.concatenate([timed[:, lanes], mix_ref[...]], axis=0)
        out_ref[0, :, :, :, lanes] = dot(left, right).astype(BF16).reshape(4, 2, N, 256)


def synthesise(got, grad, mix, k):
    return pl.pallas_call(
        synthesise_kernel,
        grid=(2, 4),
        in_specs=[SENT, FIELD, TABLE_T, whole((8 * N, 256)), whole((256, 256))],
        out_specs=FIELD,
        out_shape=jax.ShapeDtypeStruct(grad.shape, BF16),
        scratch_shapes=[pltpu.VMEM((4, 8 * KS, MT * C), F32)],
        compiler_params=params(24),
        cost_estimate=pl.CostEstimate(flops=4 * 10**9, bytes_accessed=10 * 10**6, transcendentals=0),
        name="synthesise",
    )(got, grad, k["tables_t"], k["zl_t"], mix)


def exchange_all(block):
    flat = block.reshape(128, 24, 128)
    return lax.all_to_all(flat, ("gx", "gy"), 0, 0, tiled=True).reshape(block.shape)


def exchange_second(parts):
    out = [parts[0]]
    for s in range(1, 8):
        out.append(lax.ppermute(parts[s], "gy", [(i, i ^ s) for i in range(8)]))
    return out


def body(inputs, cotangent, pre_activation, pointwise, spectral):
    k = constants()
    weights = jnp.transpose(spectral, (1, 2, 0, 3))
    mix = jnp.kron(jnp.eye(8, dtype=BF16), pointwise.T)
    sent, grad_pre = analyse_grad(cotangent, pre_activation, k)
    got = exchange_all(sent)
    sent_input = analyse_input(inputs, k)
    got_input = exchange_all(sent_input)
    grads = exchange_second(planes_forward(got, k))
    modes = exchange_second(mode_grad(grads, weights, k))
    back = exchange_all(planes_back(modes, k))
    fields = exchange_second(planes_forward(got_input, k))
    weight_grad = jnp.transpose(spectral_grad(grads, fields, k), (2, 0, 1, 3))
    return synthesise(back, grad_pre, mix, k), weight_grad


def solution(mesh):
    in_specs = (
        P(None, "gx", "gy", None, None),
        P(None, "gx", "gy", None, None),
        P(None, "gx", "gy", None, None),
        P(),
        P(None, "gy", "gx", None),
    )
    out_specs = (P(None, "gx", "gy", None, None), P(None, "gy", "gx", None))
    return jax.shard_map(body, mesh=mesh, in_specs=in_specs, out_specs=out_specs, check_vma=False)
```

time: 311 us -> 154 us (0.50)
  matrix products: 86.6 us -> 0 us
  local copies, waits for them, and re-layouts: 84.6 us -> 28.7 us
  waiting for transfers between devices: 79.9 us -> 37.3 us
  Pallas kernels: 0 us -> 34.7 us
  starting transfers between devices: 24.8 us -> 49.5 us
  other arithmetic: 15.6 us -> 0.9 us
  between operations: 14.5 us -> 0.85 us
    dot_general x11 -> x0, matrix products: 86.6 us -> none  [the longest x1 24.8 us: body(): jnp.einsum('kbmqc,kbmqo->mkqco', input_modes, grad_modes, precision=high)]
    reshape x8 -> x0, local copies, waits for them, and re-layouts: 70 us -> none  [the longest x1 24.8 us: body(): direct = direct.reshape(inputs.shape)]
    pallas_call x0 -> x8, Pallas kernels: none -> 34.7 us  [the longest x1 11.6 us: analyse_grad(): pl.pallas_call(analyse_grad_kernel, grid=(2, 4), in_specs=[FIELD, FIELD,...]
    reduce_scatter x1 -> x0, waiting for transfers between devices: 32.6 us -> none  [body(): lax.psum_scatter(jnp.einsum('bmyn,yk->kbmn', first_modes, basis_part, pre...]
    all_to_all x2 -> x3, waiting for transfers between devices: 42.9 us -> 15.4 us  [exchange_all(): lax.all_to_all(flat, ('gx', 'gy'), 0, 0, tiled=True).reshape(block.shape)]
    unnamed x20 -> x62, local copies, waits for them, and re-layouts: 0.05 us -> 27.2 us
    ppermute x0 -> x21, starting transfers between devices: none -> 25.7 us  [exchange_second(): out.append(lax.ppermute(parts[s], 'gy', [(i, i ^ s) for i in range(8)]))]
    ppermute x0 -> x21, waiting for transfers between devices: none -> 21.9 us  [exchange_second(): out.append(lax.ppermute(parts[s], 'gy', [(i, i ^ s) for i in range(8)]))]
  transfers between devices with their start and end apart: 4 -> 24, of which waited for: 3 -> 9; matrix products, arithmetic and copies ran while one was open for 35% -> 2% of each run, Pallas kernels for 0% -> 11%
where the time goes in v1:
time: 154 us; the launch traced here: 152 us
  starting transfers between devices  49.5 us (32%)
  waiting for transfers between devices  37.3 us (24%)
  Pallas kernels  34.7 us (23%)
  local copies, waits for them, and re-layouts  28.7 us (19%)
    unnamed x62, local copies, waits for them, and re-layouts  27.2 us
    ppermute x21, starting transfers between devices, exchange_second(): out.append(lax.ppermute(parts[s], 'gy', [(i, i ^ s) for i in range(8)]))  25.7 us
    all_to_all x3, starting transfers between devices, exchange_all(): lax.all_to_all(flat, ('gx', 'gy'), 0, 0, tiled=True).reshape(block.shape)  23.8 us
    ppermute x21, waiting for transfers between devices, exchange_second(): out.append(lax.ppermute(parts[s], 'gy', [(i, i ^ s) for i in range(8)]))  21.9 us
    all_to_all x3, waiting for transfers between devices, exchange_all(): lax.all_to_all(flat, ('gx', 'gy'), 0, 0, tiled=True).reshape(block.shape)  15.4 us
    pallas_call x1, Pallas kernels, analyse_grad(): pl.pallas_call(analyse_grad_kernel, grid=(2, 4), in_specs=[FIELD, FIELD,...  11.6 us
    pallas_call x1, Pallas kernels, synthesise(): pl.pallas_call(synthesise_kernel, grid=(2, 4), in_specs=[SENT, FIELD, TAB...  7.06 us
    pallas_call x1, Pallas kernels, analyse_input(): pl.pallas_call(analyse_input_kernel, grid=(2, 4), in_specs=[FIELD, TABLE,...  5.18 us
  transfers between devices with their start and end apart: 24, of which 9 were waited for; matrix products, arithmetic and copies ran while one was open for 2% of the time, Pallas kernels for 11%

profile of v1, /device:TPU:8, one launch (start us, length us, event | category | flops | bytes accessed | tf_op | source)
XLA Modules:
  0.0 151.9 jit_solution(404929201545099185)
XLA Ops:
  0.6 2.2 %copy-done.12 = bf16[2,4,8,64,512]{4,3,2,1,0:T(8,128)(2,1)S(1)} copy-done((bf16[2,4,8,64,512]{4,3,2,1,0:T(8,128)(2,1)S(1)}, bf16[2,4,8,64,512]{4,3,2,1,0:T(8,128)(2,1)}, u32[]{:S(2)}) %copy-start.12) | copy-done | bytes 4194328
  2.8 2.2 %copy-done.13 = bf16[2,4,8,64,512]{4,3,2,1,0:T(8,128)(2,1)S(1)} copy-done((bf16[2,4,8,64,512]{4,3,2,1,0:T(8,128)(2,1)S(1)}, bf16[2,4,8,64,512]{4,3,2,1,0:T(8,128)(2,1)}, u32[]{:S(2)}) %copy-start.13) | copy-done | bytes 4194328
  7.2 11.6 %analyse_grad.1 = (f32[16,8,3,8,128]{4,3,2,1,0:T(8,128)}, bf16[2,4,8,64,512]{4,3,2,1,0:T(8,128)(2,1)S(1)}) custom-call(bf16[2,4,8,64,512]{4,3,2,1,0:T(8,128)(2,1)S(1)} %copy-done.12, bf16[2,4,8,64,512]{4,3,2,1,0:T(8,128)(2,1)S(1)} %copy-done.13, bf16[4,512,256]{2,1,0:T(8,128)(2,1)S(1)} %copy-done.22, bf16[192,512]{1,0:T(8,128)(2,1)S(1)} %copy-done.26), custom_call_target="tpu_custom_call" | custom-call | flops 4000000000 | bytes 14000000 | tf_op jit(solution)/shard_map/analyse_grad/pallas_call | solution.py:161
  18.7 2.0 %copy-done.28 = bf16[2,4,8,64,512]{4,3,2,1,0:T(8,128)(2,1)} copy-done((bf16[2,4,8,64,512]{4,3,2,1,0:T(8,128)(2,1)}, bf16[2,4,8,64,512]{4,3,2,1,0:T(8,128)(2,1)S(1)}, u32[]{:S(2)}) %copy-start.28) | copy-done | bytes 4194328
  20.8 10.4 %all-to-all-start = ((f32[128,24,128]{2,1,0:T(8,128)}), f32[128,24,128]{2,1,0:T(8,128)S(1)}, u32[]{:S(2)}, u32[]{:S(2)}) async-start(f32[128,24,128]{2,1,0:T(8,128)} %bitcast), calls=%async_computation | async-start | bytes 3145728 | tf_op jit(solution)/shard_map/all_to_all | solution.py:357
  31.2 2.2 %copy-done.14 = bf16[2,4,8,64,512]{4,3,2,1,0:T(8,128)(2,1)S(1)} copy-done((bf16[2,4,8,64,512]{4,3,2,1,0:T(8,128)(2,1)S(1)}, bf16[2,4,8,64,512]{4,3,2,1,0:T(8,128)(2,1)}, u32[]{:S(2)}) %copy-start.14) | copy-done | bytes 4194328
  33.4 5.2 %analyse_input.1 = f32[16,8,3,8,128]{4,3,2,1,0:T(8,128)S(1)} custom-call(bf16[2,4,8,64,512]{4,3,2,1,0:T(8,128)(2,1)S(1)} %copy-done.14, bf16[4,512,256]{2,1,0:T(8,128)(2,1)S(1)} %copy-done.23, bf16[192,512]{1,0:T(8,128)(2,1)S(1)} %copy-done.27), custom_call_target="tpu_custom_call" | custom-call | flops 4000000000 | bytes 6000000 | tf_op jit(solution)/shard_map/analyse_input/pallas_call | solution.py:175
  39.7 15.4 %all-to-all-done = f32[128,24,128]{2,1,0:T(8,128)S(1)} async-done(((f32[128,24,128]{2,1,0:T(8,128)}), f32[128,24,128]{2,1,0:T(8,128)S(1)}, u32[]{:S(2)}, u32[]{:S(2)}) %all-to-all-start) | async-done | bytes 1572896 | tf_op jit(solution)/shard_map/all_to_all | solution.py:357
  55.1 5.4 %all-to-all-start.2 = ((f32[128,24,128]{2,1,0:T(8,128)}), f32[128,24,128]{2,1,0:T(8,128)S(1)}, u32[]{:S(2)}, u32[]{:S(2)}) async-start(f32[128,24,128]{2,1,0:T(8,128)} %bitcast.13), calls=%async_computation.2 | async-start | bytes 3145728 | tf_op jit(solution)/shard_map/all_to_all | solution.py:357
  60.6 2.2 %copy-done = bf16[2,1024,1024]{2,1,0:T(8,128)(2,1)S(1)} copy-done((bf16[2,1024,1024]{2,1,0:T(8,128)(2,1)S(1)}, bf16[2,1024,1024]{2,1,0:T(8,128)(2,1)}, u32[]{:S(2)}) %copy-start) | copy-done | bytes 4194328
  65.9 3.0 %collective-permute-start.3 = (f32[72,128]{1,0:T(8,128)S(1)}, f32[72,128]{1,0:T(8,128)S(1)}, u32[]{:S(2)}, u32[]{:S(2)}) collective-permute-start(f32[72,128]{1,0:T(8,128)S(1)} %get-tuple-element.33), channel_id=1, source_target_pairs={{0,4},{1,5},{2,6},{3,7},{4,0},{5,1},{6,2},{7,3},{8,12},{9,13},{10,... | collective-permute-start | bytes 110600 | tf_op jit(solution)/shard_map/ppermute | solution.py:363
  69.2 2.7 %collective-permute-start.5 = (f32[72,128]{1,0:T(8,128)S(1)}, f32[72,128]{1,0:T(8,128)S(1)}, u32[]{:S(2)}, u32[]{:S(2)}) collective-permute-start(f32[72,128]{1,0:T(8,128)S(1)} %get-tuple-element.35), channel_id=1, source_target_pairs={{0,6},{1,7},{2,4},{3,5},{4,2},{5,3},{6,0},{7,1},{8,14},{9,15},{10,... | collective-permute-start | bytes 110600 | tf_op jit(solution)/shard_map/ppermute | solution.py:363
  71.9 8.6 %collective-permute-done.1.refs_2_ = f32[72,128]{1,0:T(8,128)S(1)} collective-permute-done((f32[72,128]{1,0:T(8,128)S(1)}, f32[72,128]{1,0:T(8,128)S(1)}, u32[]{:S(2)}, u32[]{:S(2)}) %collective-permute-start.1) | collective-permute-done | bytes 36896 | tf_op jit(solution)/shard_map/ppermute | solution.py:363
  81.3 2.2 %collective-permute-done.3.refs_4_ = f32[72,128]{1,0:T(8,128)S(1)} collective-permute-done((f32[72,128]{1,0:T(8,128)S(1)}, f32[72,128]{1,0:T(8,128)S(1)}, u32[]{:S(2)}, u32[]{:S(2)}) %collective-permute-start.3) | collective-permute-done | bytes 36896 | tf_op jit(solution)/shard_map/ppermute | solution.py:363
  93.7 2.1 %collective-permute-start.12 = (f32[72,128]{1,0:T(8,128)S(1)}, f32[72,128]{1,0:T(8,128)S(1)}, u32[]{:S(2)}, u32[]{:S(2)}) collective-permute-start(f32[72,128]{1,0:T(8,128)S(1)} %get-tuple-element.43), channel_id=1, source_target_pairs={{0,6},{1,7},{2,4},{3,5},{4,2},{5,3},{6,0},{7,1},{8,14},{9,15},{10,... | collective-permute-start | bytes 110600 | tf_op jit(solution)/shard_map/ppermute | solution.py:363
  100.4 2.9 %planes_back.1 = f32[16,8,3,8,128]{4,3,2,1,0:T(8,128)} custom-call(f32[72,128]{1,0:T(8,128)S(1)} %get-tuple-element.37.refs_0_, f32[72,128]{1,0:T(8,128)S(1)} %collective-permute-done.7.refs_1_, f32[72,128]{1,0:T(8,128)S(1)} %collective-permute-done.8.refs_2_, f32[72,128]{1,0:T(8,128)S(1)} %collective-permute-done.9.refs_3_, ...), custom_call_target="tpu_custom_call" | custom-call | flops 1000000000 | bytes 6000000 | tf_op jit(solution)/shard_map/planes_back/pallas_call | solution.py:235
  103.3 8.0 %all-to-all-start.1 = ((f32[128,24,128]{2,1,0:T(8,128)}), f32[128,24,128]{2,1,0:T(8,128)S(1)}, u32[]{:S(2)}, u32[]{:S(2)}) async-start(f32[128,24,128]{2,1,0:T(8,128)} %bitcast.3), calls=%async_computation.1 | async-start | bytes 3145728 | tf_op jit(solution)/shard_map/all_to_all | solution.py:357
  111.3 2.2 %copy-done.2 = bf16[2,1024,1024]{2,1,0:T(8,128)(2,1)S(1)} copy-done((bf16[2,1024,1024]{2,1,0:T(8,128)(2,1)S(1)}, bf16[2,1024,1024]{2,1,0:T(8,128)(2,1)}, u32[]{:S(2)}) %copy-start.2) | copy-done | bytes 4194328
  120.9 3.0 %collective-permute-start.17 = (f32[72,128]{1,0:T(8,128)}, f32[72,128]{1,0:T(8,128)S(1)}, u32[]{:S(2)}, u32[]{:S(2)}) collective-permute-start(f32[72,128]{1,0:T(8,128)} %copy-done.19), channel_id=1, source_target_pairs={{0,4},{1,5},{2,6},{3,7},{4,0},{5,1},{6,2},{7,3},{8,12},{9,13},{10,... | collective-permute-start | bytes 110600 | tf_op jit(solution)/shard_map/ppermute | solution.py:363
  124.3 2.7 %collective-permute-start.19 = (f32[72,128]{1,0:T(8,128)}, f32[72,128]{1,0:T(8,128)S(1)}, u32[]{:S(2)}, u32[]{:S(2)}) collective-permute-start(f32[72,128]{1,0:T(8,128)} %copy-done.17), channel_id=1, source_target_pairs={{0,6},{1,7},{2,4},{3,5},{4,2},{5,3},{6,0},{7,1},{8,14},{9,15},{10,... | collective-permute-start | bytes 110600 | tf_op jit(solution)/shard_map/ppermute | solution.py:363
  126.9 4.3 %collective-permute-done.15.refs_10_ = f32[72,128]{1,0:T(8,128)S(1)} collective-permute-done((f32[72,128]{1,0:T(8,128)}, f32[72,128]{1,0:T(8,128)S(1)}, u32[]{:S(2)}, u32[]{:S(2)}) %collective-permute-start.15) | collective-permute-done | bytes 36896 | tf_op jit(solution)/shard_map/ppermute | solution.py:363
  138.7 3.0 %spectral_grad.1 = f32[3,12,24,1024]{3,2,1,0:T(8,128)} custom-call(f32[72,128]{1,0:T(8,128)S(1)} %get-tuple-element.29.refs_0_, f32[72,128]{1,0:T(8,128)S(1)} %collective-permute-done.refs_1_, f32[72,128]{1,0:T(8,128)S(1)} %collective-permute-done.1.refs_2_, f32[72,128]{1,0:T(8,128)S(1)} %collective-permute-done.2.refs_3_, ...), custom_call_target="tpu_custom_call" | custom-call | flops 1000000000 | bytes 4000000 | tf_op jit(solution)/shard_map/spectral_grad/pallas_call | solution.py:294
  142.7 2.2 %copy-done.29 = bf16[2,4,8,64,512]{4,3,2,1,0:T(8,128)(2,1)S(1)} copy-done((bf16[2,4,8,64,512]{4,3,2,1,0:T(8,128)(2,1)S(1)}, bf16[2,4,8,64,512]{4,3,2,1,0:T(8,128)(2,1)}, u32[]{:S(2)}) %copy-start.29) | copy-done | bytes 4194328
  144.9 7.1 %synthesise.1 = bf16[2,4,8,64,512]{4,3,2,1,0:T(8,128)(2,1)} custom-call(f32[16,8,3,8,128]{4,3,2,1,0:T(8,128)S(1)} %bitcast.14, bf16[2,4,8,64,512]{4,3,2,1,0:T(8,128)(2,1)S(1)} %copy-done.29, bf16[4,256,512]{2,1,0:T(8,128)(2,1)S(1)} %copy-done.21, bf16[512,256]{1,0:T(8,128)(2,1)S(1)} %copy-done.25, bf16[256,256]{1,0:T(8,128)(2,1)S(1)} %mul.27.mix_ref), custom_call_target="tpu_custom_call" | custom-call | flops 4000000000 | bytes 10000000 | tf_op jit(solution)/shard_map/synthesise/pallas_call | solution.py:342
  (98 shorter events, 38.6 us)
Async XLA Ops:
  20.8 34.4 %all-to-all-start = ((f32[128,24,128]{2,1,0:T(8,128)}), f32[128,24,128]{2,1,0:T(8,128)S(1)}, u32[]{:S(2)}, u32[]{:S(2)}) async-start(f32[128,24,128]{2,1,0:T(8,128)} %bitcast), calls=%async_computation | async-start | bytes 3145728 | tf_op jit(solution)/shard_map/all_to_all | solution.py:357
  55.1 48.2 %all-to-all-start.2 = ((f32[128,24,128]{2,1,0:T(8,128)}), f32[128,24,128]{2,1,0:T(8,128)S(1)}, u32[]{:S(2)}, u32[]{:S(2)}) async-start(f32[128,24,128]{2,1,0:T(8,128)} %bitcast.13), calls=%async_computation.2 | async-start | bytes 3145728 | tf_op jit(solution)/shard_map/all_to_all | solution.py:357
  63.9 5.2 %collective-permute-start = (f32[72,128]{1,0:T(8,128)S(1)}, f32[72,128]{1,0:T(8,128)S(1)}, u32[]{:S(2)}, u32[]{:S(2)}) collective-permute-start(f32[72,128]{1,0:T(8,128)S(1)} %get-tuple-element.30), channel_id=1, source_target_pairs={{0,1},{1,0},{2,3},{3,2},{4,5},{5,4},{6,7},{7,6},{8,9},{9,8},{10,11... | collective-permute-start | bytes 110600 | tf_op jit(solution)/shard_map/ppermute | solution.py:363
  64.2 16.3 %collective-permute-start.1 = (f32[72,128]{1,0:T(8,128)S(1)}, f32[72,128]{1,0:T(8,128)S(1)}, u32[]{:S(2)}, u32[]{:S(2)}) collective-permute-start(f32[72,128]{1,0:T(8,128)S(1)} %get-tuple-element.31), channel_id=1, source_target_pairs={{0,2},{1,3},{2,0},{3,1},{4,6},{5,7},{6,4},{7,5},{8,10},{9,11},{10,... | collective-permute-start | bytes 110600 | tf_op jit(solution)/shard_map/ppermute | solution.py:363
  65.7 15.7 %collective-permute-start.2 = (f32[72,128]{1,0:T(8,128)S(1)}, f32[72,128]{1,0:T(8,128)S(1)}, u32[]{:S(2)}, u32[]{:S(2)}) collective-permute-start(f32[72,128]{1,0:T(8,128)S(1)} %get-tuple-element.32), channel_id=1, source_target_pairs={{0,3},{1,2},{2,1},{3,0},{4,7},{5,6},{6,5},{7,4},{8,11},{9,10},{10,... | collective-permute-start | bytes 110600 | tf_op jit(solution)/shard_map/ppermute | solution.py:363
  65.9 17.6 %collective-permute-start.3 = (f32[72,128]{1,0:T(8,128)S(1)}, f32[72,128]{1,0:T(8,128)S(1)}, u32[]{:S(2)}, u32[]{:S(2)}) collective-permute-start(f32[72,128]{1,0:T(8,128)S(1)} %get-tuple-element.33), channel_id=1, source_target_pairs={{0,4},{1,5},{2,6},{3,7},{4,0},{5,1},{6,2},{7,3},{8,12},{9,13},{10,... | collective-permute-start | bytes 110600 | tf_op jit(solution)/shard_map/ppermute | solution.py:363
  68.9 14.6 %collective-permute-start.4 = (f32[72,128]{1,0:T(8,128)S(1)}, f32[72,128]{1,0:T(8,128)S(1)}, u32[]{:S(2)}, u32[]{:S(2)}) collective-permute-start(f32[72,128]{1,0:T(8,128)S(1)} %get-tuple-element.34), channel_id=1, source_target_pairs={{0,5},{1,4},{2,7},{3,6},{4,1},{5,0},{6,3},{7,2},{8,13},{9,12},{10,... | collective-permute-start | bytes 110600 | tf_op jit(solution)/shard_map/ppermute | solution.py:363
  69.2 14.3 %collective-permute-start.5 = (f32[72,128]{1,0:T(8,128)S(1)}, f32[72,128]{1,0:T(8,128)S(1)}, u32[]{:S(2)}, u32[]{:S(2)}) collective-permute-start(f32[72,128]{1,0:T(8,128)S(1)} %get-tuple-element.35), channel_id=1, source_target_pairs={{0,6},{1,7},{2,4},{3,5},{4,2},{5,3},{6,0},{7,1},{8,14},{9,15},{10,... | collective-permute-start | bytes 110600 | tf_op jit(solution)/shard_map/ppermute | solution.py:363
  80.5 4.6 %collective-permute-start.6 = (f32[72,128]{1,0:T(8,128)S(1)}, f32[72,128]{1,0:T(8,128)S(1)}, u32[]{:S(2)}, u32[]{:S(2)}) collective-permute-start(f32[72,128]{1,0:T(8,128)S(1)} %get-tuple-element.36), channel_id=1, source_target_pairs={{0,7},{1,6},{2,5},{3,4},{4,3},{5,2},{6,1},{7,0},{8,15},{9,14},{10,... | collective-permute-start | bytes 110600 | tf_op jit(solution)/shard_map/ppermute | solution.py:363
  88.5 5.2 %collective-permute-start.7 = (f32[72,128]{1,0:T(8,128)S(1)}, f32[72,128]{1,0:T(8,128)S(1)}, u32[]{:S(2)}, u32[]{:S(2)}) collective-permute-start(f32[72,128]{1,0:T(8,128)S(1)} %get-tuple-element.38), channel_id=1, source_target_pairs={{0,1},{1,0},{2,3},{3,2},{4,5},{5,4},{6,7},{7,6},{8,9},{9,8},{10,11... | collective-permute-start | bytes 110600 | tf_op jit(solution)/shard_map/ppermute | solution.py:363
  88.6 7.2 %collective-permute-start.8 = (f32[72,128]{1,0:T(8,128)S(1)}, f32[72,128]{1,0:T(8,128)S(1)}, u32[]{:S(2)}, u32[]{:S(2)}) collective-permute-start(f32[72,128]{1,0:T(8,128)S(1)} %get-tuple-element.39), channel_id=1, source_target_pairs={{0,2},{1,3},{2,0},{3,1},{4,6},{5,7},{6,4},{7,5},{8,10},{9,11},{10,... | collective-permute-start | bytes 110600 | tf_op jit(solution)/shard_map/ppermute | solution.py:363
  88.7 8.0 %collective-permute-start.9 = (f32[72,128]{1,0:T(8,128)S(1)}, f32[72,128]{1,0:T(8,128)S(1)}, u32[]{:S(2)}, u32[]{:S(2)}) collective-permute-start(f32[72,128]{1,0:T(8,128)S(1)} %get-tuple-element.40), channel_id=1, source_target_pairs={{0,3},{1,2},{2,1},{3,0},{4,7},{5,6},{6,5},{7,4},{8,11},{9,10},{10,... | collective-permute-start | bytes 110600 | tf_op jit(solution)/shard_map/ppermute | solution.py:363
  90.4 6.2 %collective-permute-start.10 = (f32[72,128]{1,0:T(8,128)S(1)}, f32[72,128]{1,0:T(8,128)S(1)}, u32[]{:S(2)}, u32[]{:S(2)}) collective-permute-start(f32[72,128]{1,0:T(8,128)S(1)} %get-tuple-element.41), channel_id=1, source_target_pairs={{0,4},{1,5},{2,6},{3,7},{4,0},{5,1},{6,2},{7,3},{8,12},{9,13},{10,... | collective-permute-start | bytes 110600 | tf_op jit(solution)/shard_map/ppermute | solution.py:363
  92.3 5.2 %collective-permute-start.11 = (f32[72,128]{1,0:T(8,128)S(1)}, f32[72,128]{1,0:T(8,128)S(1)}, u32[]{:S(2)}, u32[]{:S(2)}) collective-permute-start(f32[72,128]{1,0:T(8,128)S(1)} %get-tuple-element.42), channel_id=1, source_target_pairs={{0,5},{1,4},{2,7},{3,6},{4,1},{5,0},{6,3},{7,2},{8,13},{9,12},{10,... | collective-permute-start | bytes 110600 | tf_op jit(solution)/shard_map/ppermute | solution.py:363
  93.7 5.2 %collective-permute-start.12 = (f32[72,128]{1,0:T(8,128)S(1)}, f32[72,128]{1,0:T(8,128)S(1)}, u32[]{:S(2)}, u32[]{:S(2)}) collective-permute-start(f32[72,128]{1,0:T(8,128)S(1)} %get-tuple-element.43), channel_id=1, source_target_pairs={{0,6},{1,7},{2,4},{3,5},{4,2},{5,3},{6,0},{7,1},{8,14},{9,15},{10,... | collective-permute-start | bytes 110600 | tf_op jit(solution)/shard_map/ppermute | solution.py:363
  95.8 4.6 %collective-permute-start.13 = (f32[72,128]{1,0:T(8,128)S(1)}, f32[72,128]{1,0:T(8,128)S(1)}, u32[]{:S(2)}, u32[]{:S(2)}) collective-permute-start(f32[72,128]{1,0:T(8,128)S(1)} %get-tuple-element.44), channel_id=1, source_target_pairs={{0,7},{1,6},{2,5},{3,4},{4,3},{5,2},{6,1},{7,0},{8,15},{9,14},{10,... | collective-permute-start | bytes 110600 | tf_op jit(solution)/shard_map/ppermute | solution.py:363
  103.3 38.4 %all-to-all-start.1 = ((f32[128,24,128]{2,1,0:T(8,128)}), f32[128,24,128]{2,1,0:T(8,128)S(1)}, u32[]{:S(2)}, u32[]{:S(2)}) async-start(f32[128,24,128]{2,1,0:T(8,128)} %bitcast.3), calls=%async_computation.1 | async-start | bytes 3145728 | tf_op jit(solution)/shard_map/all_to_all | solution.py:357
  119.0 5.3 %collective-permute-start.14 = (f32[72,128]{1,0:T(8,128)}, f32[72,128]{1,0:T(8,128)S(1)}, u32[]{:S(2)}, u32[]{:S(2)}) collective-permute-start(f32[72,128]{1,0:T(8,128)} %get-tuple-element.47), channel_id=1, source_target_pairs={{0,1},{1,0},{2,3},{3,2},{4,5},{5,4},{6,7},{7,6},{8,9},{9,8},{10,11... | collective-permute-start | bytes 110600 | tf_op jit(solution)/shard_map/ppermute | solution.py:363
  119.1 12.1 %collective-permute-start.15 = (f32[72,128]{1,0:T(8,128)}, f32[72,128]{1,0:T(8,128)S(1)}, u32[]{:S(2)}, u32[]{:S(2)}) collective-permute-start(f32[72,128]{1,0:T(8,128)} %get-tuple-element.48), channel_id=1, source_target_pairs={{0,2},{1,3},{2,0},{3,1},{4,6},{5,7},{6,4},{7,5},{8,10},{9,11},{10,... | collective-permute-start | bytes 110600 | tf_op jit(solution)/shard_map/ppermute | solution.py:363
  120.7 13.7 %collective-permute-start.16 = (f32[72,128]{1,0:T(8,128)}, f32[72,128]{1,0:T(8,128)S(1)}, u32[]{:S(2)}, u32[]{:S(2)}) collective-permute-start(f32[72,128]{1,0:T(8,128)} %copy-done.20), channel_id=1, source_target_pairs={{0,3},{1,2},{2,1},{3,0},{4,7},{5,6},{6,5},{7,4},{8,11},{9,10},{10,... | collective-permute-start | bytes 110600 | tf_op jit(solution)/shard_map/ppermute | solution.py:363
  120.9 13.5 %collective-permute-start.17 = (f32[72,128]{1,0:T(8,128)}, f32[72,128]{1,0:T(8,128)S(1)}, u32[]{:S(2)}, u32[]{:S(2)}) collective-permute-start(f32[72,128]{1,0:T(8,128)} %copy-done.19), channel_id=1, source_target_pairs={{0,4},{1,5},{2,6},{3,7},{4,0},{5,1},{6,2},{7,3},{8,12},{9,13},{10,... | collective-permute-start | bytes 110600 | tf_op jit(solution)/shard_map/ppermute | solution.py:363
  123.9 10.5 %collective-permute-start.18 = (f32[72,128]{1,0:T(8,128)}, f32[72,128]{1,0:T(8,128)S(1)}, u32[]{:S(2)}, u32[]{:S(2)}) collective-permute-start(f32[72,128]{1,0:T(8,128)} %copy-done.18), channel_id=1, source_target_pairs={{0,5},{1,4},{2,7},{3,6},{4,1},{5,0},{6,3},{7,2},{8,13},{9,12},{10,... | collective-permute-start | bytes 110600 | tf_op jit(solution)/shard_map/ppermute | solution.py:363
  124.3 10.2 %collective-permute-start.19 = (f32[72,128]{1,0:T(8,128)}, f32[72,128]{1,0:T(8,128)S(1)}, u32[]{:S(2)}, u32[]{:S(2)}) collective-permute-start(f32[72,128]{1,0:T(8,128)} %copy-done.17), channel_id=1, source_target_pairs={{0,6},{1,7},{2,4},{3,5},{4,2},{5,3},{6,0},{7,1},{8,14},{9,15},{10,... | collective-permute-start | bytes 110600 | tf_op jit(solution)/shard_map/ppermute | solution.py:363
  131.2 4.8 %collective-permute-start.20 = (f32[72,128]{1,0:T(8,128)}, f32[72,128]{1,0:T(8,128)S(1)}, u32[]{:S(2)}, u32[]{:S(2)}) collective-permute-start(f32[72,128]{1,0:T(8,128)} %copy-done.16), channel_id=1, source_target_pairs={{0,7},{1,6},{2,5},{3,4},{4,3},{5,2},{6,1},{7,0},{8,15},{9,14},{10,... | collective-permute-start | bytes 110600 | tf_op jit(solution)/shard_map/ppermute | solution.py:363
  (31 other events, 267.6 us)

commit v2 on v1

v2 whole, which is shorter than its diff:
```python
import functools
import math

import jax
import jax.numpy as jnp
import ml_dtypes
import numpy as np
from jax import lax
from jax.experimental import pallas as pl
from jax.experimental.pallas import tpu as pltpu
from jax.sharding import PartitionSpec as P

N = 64
NT = 16
MS = 12
MT = 8
KS = 24
C = 32
BF = ml_dtypes.bfloat16
F32 = jnp.float32
BF16 = jnp.bfloat16
MIB = 1 << 20


def fourier(length, frequencies):
    points = np.arange(length, dtype=np.float64)[:, None]
    orders = np.arange(frequencies, dtype=np.float64)[None, :]
    scales = np.where(orders == 0.0, math.sqrt(1.0 / length), math.sqrt(2.0 / length))
    cosines = scales * np.cos(2.0 * math.pi * points * orders / length)
    sines = math.sqrt(2.0 / length) * np.sin(2.0 * math.pi * points * (orders + 1.0) / length)
    return np.concatenate([cosines, sines], axis=1).astype(np.float32)


def cosine(length, modes):
    points = np.arange(length, dtype=np.float64)[:, None]
    orders = np.arange(modes, dtype=np.float64)[None, :]
    scales = np.where(orders == 0.0, math.sqrt(1.0 / length), math.sqrt(2.0 / length))
    return (scales * np.cos(math.pi * orders * (points + 0.5) / length)).astype(np.float32)


def constants():
    basis = fourier(N, MS)
    third = basis.astype(BF).astype(np.float32)
    time = cosine(NT, MT).astype(BF).astype(np.float32)
    eye_c = np.eye(C, dtype=np.float32)
    eye_r = np.eye(8, dtype=np.float32)
    out = {}
    tables = np.zeros((4, NT, C, 2, 4, C), np.float32)
    for pair in range(4):
        for kt in range(MT):
            half, q = divmod(kt, 4)
            tables[pair, :, :, half, (q + pair) % 4, :] = time[:, kt][:, None, None] * eye_c[None]
    tables = tables.reshape(4, NT * C, MT * C)
    out["tables"] = tables.astype(BF)
    out["tables_t"] = np.swapaxes(tables, 1, 2).copy().astype(BF)
    zl = np.einsum("zk,rs->krsz", third, eye_r).reshape(KS * 8, 8 * N)
    out["zl"] = zl.astype(BF)
    out["zl_t"] = np.concatenate([zl.T, np.zeros((8 * N, 64), np.float32)], axis=1).astype(BF)
    high = basis.astype(BF).astype(np.float32)
    low = (basis - high).astype(BF).astype(np.float32)
    eye_h = np.eye(2, dtype=np.float32)
    forms = [np.einsum("xk,hg->hkxg", part, eye_h).reshape(2 * KS, 2 * N) for part in (high, low)]
    out["xl"] = np.concatenate(forms, axis=1).astype(BF)
    out["xl_t"] = np.concatenate([form.T for form in forms], axis=1).astype(BF)
    second = basis.reshape(8, 4, 2, 8, 3)
    out["cy"] = np.repeat(np.einsum("slhdj->djhsl", second).reshape(8, 3, 16, 4), C, axis=3)
    spread = np.zeros((3, 4, C, 4, C), np.float32)
    gather = np.zeros((3, C, C, 4, C), np.float32)
    wide = np.zeros((3, 4, C, C, C), np.float32)
    for ky in range(3):
        spread[ky, ky] = eye_c[:, None, :]
        gather[ky, :, :, ky, :] = eye_c[:, None, :]
        wide[ky, ky] = eye_c[:, :, None]
    out["spread"] = spread.reshape(3, 128, 128).astype(BF)
    out["gather"] = gather.reshape(3, C * C, 128).astype(BF)
    out["wide"] = wide.reshape(3, 128, C * C).astype(BF)
    return out


def dot(a, b):
    return jnp.dot(a, b, preferred_element_type=F32)


def gelu_slope(v):
    cdf = 0.5 * (1.0 + lax.erf(v * 0.7071067811865476))
    return cdf + v * (0.3989422804014327 * jnp.exp(-0.5 * v * v))


def lane_group(rows):
    return lax.broadcasted_iota(jnp.int32, (rows, 128), 1) // C


def send_parts(parts, sent_ref):
    group = lane_group(8 * KS)
    for half in range(2):
        lanes = slice(half * 128, half * 128 + 128)
        for q in range(4):
            value = parts[(-q) % 4, :, lanes]
            for p in range(1, 4):
                value = jnp.where(group == p, parts[(p - q) % 4, :, lanes], value)
            if q:
                value = pltpu.roll(value, 128 - q * C, 1)
            for kz in range(KS):
                block, slot = divmod(2 * kz + half, 3)
                sent_ref[block, q, slot] = value[kz * 8 : kz * 8 + 8]


def analyse_grad_kernel(cot_ref, pre_ref, table_ref, zl_ref, sent_ref, grad_ref, flat, timed, parts):
    step = pl.program_id(1)

    def time(n, carry):
        timed[n] = dot(flat[n & 1], table_ref[n // 4]).astype(BF16)
        return carry

    def slope(n, carry):
        pair, x = n // 4, n % 4
        before = jnp.maximum(n - 1, 0)
        earlier = dot(flat[(n + 1) & 1], table_ref[before // 4])
        for y in range(2):
            for j in range(4):
                rows = pl.ds(j * 16, 16)
                v = pre_ref[0, x, 2 * pair + y, rows, :].astype(F32)
                g = cot_ref[0, x, 2 * pair + y, rows, :].astype(F32)
                grad = (g * gelu_slope(v)).astype(BF16)
                grad_ref[0, x, 2 * pair + y, rows, :] = grad
                flat[n & 1, y * N + j * 16 : y * N + j * 16 + 16, :] = grad
        timed[before] = earlier.astype(BF16)
        return carry

    lax.fori_loop(0, 8, slope, 0)
    time(7, 0)
    for pair in range(2):
        parts[2 * step + pair] = dot(zl_ref[...], timed[4 * pair : 4 * pair + 4].reshape(8 * N, MT * C))

    @pl.when(step == 1)
    def _():
        send_parts(parts, sent_ref)


def analyse_input_kernel(field_ref, table_ref, zl_ref, sent_ref, parts):
    step = pl.program_id(1)
    for pair in range(2):
        field = field_ref[0, :, 2 * pair : 2 * pair + 2].reshape(8 * N, NT * C)
        timed = dot(field, table_ref[pair]).astype(BF16)
        parts[2 * step + pair] = dot(zl_ref[...], timed)

    @pl.when(step == 1)
    def _():
        send_parts(parts, sent_ref)


FIELD = pl.BlockSpec((1, 4, 4, N, NT * C), lambda b, p: (b, 0, p, 0, 0))
TABLE = pl.BlockSpec((2, NT * C, MT * C), lambda b, p: (p, 0, 0))
TABLE_T = pl.BlockSpec((2, MT * C, NT * C), lambda b, p: (p, 0, 0))
SENT = pl.BlockSpec((16, 4, 3, 8, 128), lambda b, p: (0, b, 0, 0, 0))
SENT_SHAPE = (16, 8, 3, 8, 128)
PART, PLANE = 72, 144
ANY = pl.BlockSpec(memory_space=pl.ANY)


def whole(shape):
    return pl.BlockSpec(shape, lambda *ids: (0,) * len(shape))


def params(limit):
    return pltpu.CompilerParams(vmem_limit_bytes=limit * MIB)


def cost(flops, nbytes):
    return pl.CostEstimate(flops=flops, bytes_accessed=nbytes, transcendentals=0)


def in_hbm(*arrays):
    return [pltpu.with_memory_space_constraint(a, pltpu.HBM) for a in arrays]


def analyse_grad(cotangent, pre_activation, k):
    return pl.pallas_call(
        analyse_grad_kernel,
        grid=(2, 2),
        in_specs=[FIELD, FIELD, TABLE, whole((8 * KS, 8 * N))],
        out_specs=[SENT, FIELD],
        out_shape=[pltpu.HBM(SENT_SHAPE, F32), pltpu.HBM(cotangent.shape, BF16)],
        scratch_shapes=[
            pltpu.VMEM((2, 2 * N, NT * C), BF16),
            pltpu.VMEM((8, 2 * N, MT * C), BF16),
            pltpu.VMEM((4, 8 * KS, MT * C), F32),
        ],
        compiler_params=params(24),
        cost_estimate=cost(4 * 10**9, 14 * 10**6),
        name="analyse_grad",
    )(*in_hbm(cotangent, pre_activation, k["tables"], k["zl"]))


def analyse_input(inputs, k):
    return pl.pallas_call(
        analyse_input_kernel,
        grid=(2, 2),
        in_specs=[FIELD, TABLE, whole((8 * KS, 8 * N))],
        out_specs=SENT,
        out_shape=pltpu.HBM(SENT_SHAPE, F32),
        scratch_shapes=[pltpu.VMEM((4, 8 * KS, MT * C), F32)],
        compiler_params=params(24),
        cost_estimate=cost(4 * 10**9, 6 * 10**6),
        name="analyse_input",
    )(*in_hbm(inputs, k["tables"], k["zl"]))


def transform_x(got_ref, xl_ref, planes):
    for slot in range(3):
        field = jnp.concatenate(
            [got_ref[:, s, slot].reshape(128, 128).astype(BF16) for s in range(8)], axis=1
        )
        wide = dot(xl_ref[...], jnp.concatenate([field, field], axis=0))
        for s in range(8):
            planes[s, slot * 48 : slot * 48 + 48, :] = wide[:, s * 128 : s * 128 + 128]


def transform_y(planes, cy_ref, blocks):
    group = lane_group(72)

    def block(d, carry):
        totals = [jnp.zeros((72, 128), F32)] * 3
        for s in range(8):
            for half in range(2):
                starts = [slot * 48 + half * KS for slot in range(3)]
                rows = jnp.concatenate([planes[s, at : at + KS, :] for at in starts], axis=0)
                for j in range(3):
                    totals[j] = totals[j] + rows * cy_ref[d, j, half * 8 + s : half * 8 + s + 1, :]
        value = jnp.zeros((72, 128), F32)
        for j in range(3):
            total = totals[j] + pltpu.roll(totals[j], 64, 1)
            total = total + pltpu.roll(total, 32, 1)
            value = jnp.where(group == j, total, value)
        blocks[d] = value
        return carry

    lax.fori_loop(0, 8, block, 0)


def group_shape(rows):
    return jax.ShapeDtypeStruct((4, rows, 128), F32)


def deal(blocks, keep_ref, cross_ref):
    me = lax.axis_index("gy")
    for sx in range(4):
        keep_ref[sx] = blocks[me ^ (2 * sx)]
        cross_ref[sx] = blocks[me ^ (2 * sx + 1)]


def arrived(refs):
    keep, cross, *far = refs
    return [keep.at[0], cross.at[0]] + [ref.at[i] for ref in far for i in range(2)]


def collect(parts, blocks):
    me = lax.axis_index("gy")
    for s in range(8):
        blocks[me ^ s] = parts[s][...]


def planes_forward_kernel(got_ref, xl_ref, cy_ref, *rest):
    keep_ref, cross_ref, planes, blocks = rest
    transform_x(got_ref, xl_ref, planes)
    transform_y(planes, cy_ref, blocks)
    deal(blocks, keep_ref, cross_ref)


def planes_forward(got, xl, cy):
    return pl.pallas_call(
        planes_forward_kernel,
        out_shape=[group_shape(PART)] * 2,
        scratch_shapes=[pltpu.VMEM((8, PLANE, 128), F32), pltpu.VMEM((8, PART, 128), F32)],
        compiler_params=params(16),
        cost_estimate=cost(10**9, 3 * 10**6),
        name="planes_forward",
    )(got, xl, cy)


def planes_x_kernel(got_ref, xl_ref, keep_ref, cross_ref, planes):
    transform_x(got_ref, xl_ref, planes)
    deal(planes, keep_ref, cross_ref)


def planes_x(got, xl):
    return pl.pallas_call(
        planes_x_kernel,
        out_shape=[group_shape(PLANE)] * 2,
        scratch_shapes=[pltpu.VMEM((8, PLANE, 128), F32)],
        compiler_params=params(16),
        cost_estimate=cost(10**9, 2 * 10**6),
        name="planes_x",
    )(got, xl)


def planes_y_kernel(*refs):
    parts, (cy_ref, keep_ref, cross_ref, planes, blocks) = arrived(refs[:5]), refs[5:]
    collect(parts, planes)
    transform_y(planes, cy_ref, blocks)
    deal(blocks, keep_ref, cross_ref)


def planes_y(parts, cy):
    return pl.pallas_call(
        planes_y_kernel,
        out_shape=[group_shape(PART)] * 2,
        scratch_shapes=[pltpu.VMEM((8, PLANE, 128), F32), pltpu.VMEM((8, PART, 128), F32)],
        compiler_params=params(16),
        cost_estimate=cost(10**9, 2 * 10**6),
        name="planes_y",
    )(*parts, cy)


def back_y_kernel(*refs):
    parts, (cy_ref, spread_ref, keep_ref, cross_ref, blocks, copies, planes) = arrived(refs[:5]), refs[5:]
    collect(parts, blocks)
    field = blocks[...].reshape(576, 128).astype(BF16)
    for j in range(3):
        copies[j] = dot(field, spread_ref[j])

    def plane(s, carry):
        totals = [jnp.zeros((72, 128), F32)] * 2
        for d in range(8):
            for j in range(3):
                rows = copies[j, d * 72 : d * 72 + 72, :]
                for half in range(2):
                    totals[half] = totals[half] + rows * cy_ref[d, j, pl.ds(half * 8 + s, 1), :]
        for half in range(2):
            for slot in range(3):
                at = slot * 48 + half * KS
                planes[s, at : at + KS, :] = totals[half][slot * KS : slot * KS + KS]
        return carry

    lax.fori_loop(0, 8, plane, 0)
    deal(planes, keep_ref, cross_ref)


def back_y(parts, cy, spread):
    return pl.pallas_call(
        back_y_kernel,
        out_shape=[group_shape(PLANE)] * 2,
        scratch_shapes=[
            pltpu.VMEM((8, PART, 128), F32),
            pltpu.VMEM((3, 8 * PART, 128), F32),
            pltpu.VMEM((8, PLANE, 128), F32),
        ],
        compiler_params=params(16),
        cost_estimate=cost(10**9, 2 * 10**6),
        name="back_y",
    )(*parts, cy, spread)


def back_x_kernel(*refs):
    parts, (xl_ref, sent_ref, planes) = arrived(refs[:5]), refs[5:]
    collect(parts, planes)
    for slot in range(3):
        rows = slice(slot * 48, slot * 48 + 48)
        both = jnp.concatenate([planes[s, rows, :] for s in range(8)], axis=1).astype(BF16)
        wide = dot(xl_ref[...], jnp.concatenate([both, both], axis=0))
        for s in range(8):
            sent_ref[:, s, slot] = wide[:, s * 128 : s * 128 + 128].reshape(16, 8, 128)


def back_x(parts, xl_t):
    return pl.pallas_call(
        back_x_kernel,
        out_shape=pltpu.HBM(SENT_SHAPE, F32),
        out_specs=pl.BlockSpec(SENT_SHAPE, lambda: (0,) * 5),
        scratch_shapes=[pltpu.VMEM((8, PLANE, 128), F32)],
        compiler_params=params(16),
        cost_estimate=cost(10**9, 2 * 10**6),
        name="back_x",
    )(*parts, xl_t)


def pair_up_kernel(keep_ref, cross_ref, *outs):
    for sx in range(1, 4):
        outs[sx - 1][0] = keep_ref[sx]
        outs[sx - 1][1] = cross_ref[sx]


def pair_up(keep, cross):
    shape = jax.ShapeDtypeStruct((2, *keep.shape[1:]), F32)
    return pl.pallas_call(
        pair_up_kernel,
        out_shape=[shape] * 3,
        compiler_params=params(16),
        cost_estimate=cost(10**6, 10**6),
        name="pair_up",
    )(keep, cross)


def exchange_second(blocks):
    keep, cross = blocks
    cross = lax.ppermute(cross, "gy", [(i, i ^ 1) for i in range(8)])
    pairs = pair_up(keep, cross)
    far = [lax.ppermute(pairs[sx - 1], "gy", [(i, i ^ (2 * sx)) for i in range(8)]) for sx in range(1, 4)]
    return [keep, cross] + far


def mode_grad_kernel(*refs):
    parts, (spread_ref, weight_hbm, gather_hbm, keep_ref, cross_ref) = arrived(refs[:5]), refs[5:10]
    products, weight_ref, gather_ref, sems = refs[10:]
    copies = []
    for ky in range(3):
        copies.append(
            (
                pltpu.make_async_copy(weight_hbm.at[ky], weight_ref.at[ky], sems.at[0, ky]),
                pltpu.make_async_copy(gather_hbm.at[ky], gather_ref.at[ky], sems.at[1, ky]),
            )
        )
    for weight, gather in copies:
        weight.start()
        gather.start()
    me = lax.axis_index("gy")
    field = jnp.concatenate([part[...] for part in parts], axis=0).astype(BF16)
    total = None
    for ky in range(3):
        lanes = dot(field, spread_ref[ky])
        copies[ky][0].wait()
        for s in range(8):
            q = (me ^ s) & 3
            for slot in range(3):
                at = s * 72 + slot * KS
                weight = weight_ref[ky, slot * 4 + q].astype(F32)
                products[at : at + KS, :] = weight * jnp.concatenate([lanes[at : at + KS]] * 8, axis=1)
        copies[ky][1].wait()
        term = dot(products[...].astype(BF16), gather_ref[ky])
        total = term if total is None else total + term
    for sx in range(4):
        keep_ref[sx] = total[2 * sx * 72 : 2 * sx * 72 + 72]
        cross_ref[sx] = total[(2 * sx + 1) * 72 : (2 * sx + 1) * 72 + 72]


def mode_grad(parts, weights, k):
    vmem = pl.BlockSpec(memory_space=pltpu.VMEM)
    return pl.pallas_call(
        mode_grad_kernel,
        in_specs=[vmem] * 6 + [ANY] * 2,
        out_shape=[group_shape(PART)] * 2,
        scratch_shapes=[
            pltpu.VMEM((576, C * C), F32),
            pltpu.VMEM(weights.shape, BF16),
            pltpu.VMEM((3, C * C, 128), BF16),
            pltpu.SemaphoreType.DMA((2, 3)),
        ],
        compiler_params=params(16),
        cost_estimate=cost(10**9, 4 * 10**6),
        name="mode_grad",
    )(*parts, k["spread"], *in_hbm(weights, k["gather"]))


def spectral_grad_kernel(*refs):
    grads, fields, (spread_ref, wide_ref, out_ref) = arrived(refs[:5]), arrived(refs[5:10]), refs[10:]
    me = lax.axis_index("gy")
    grad = jnp.concatenate([part[...] for part in grads], axis=0).astype(BF16)
    field = jnp.concatenate([part[...] for part in fields], axis=0).astype(BF16)
    copies = dot(grad, spread_ref[0])
    wide = dot(field, wide_ref[0])
    for s in range(4):
        q = (me ^ s) & 3
        for slot in range(3):
            total = None
            for at in (s * 72 + slot * KS, (s + 4) * 72 + slot * KS):
                term = wide[at : at + KS] * jnp.concatenate([copies[at : at + KS]] * 8, axis=1)
                total = term if total is None else total + term
            out_ref[0, slot * 4 + q] = total


def spectral_grad(grads, fields, spread, wide):
    return pl.pallas_call(
        spectral_grad_kernel,
        grid=(3,),
        in_specs=[whole((4, PART, 128))] * 2
        + [whole((2, PART, 128))] * 3
        + [whole((4, PART, 128))] * 2
        + [whole((2, PART, 128))] * 3
        + [
            pl.BlockSpec((1, 128, 128), lambda i: (i, 0, 0)),
            pl.BlockSpec((1, 128, C * C), lambda i: (i, 0, 0)),
        ],
        out_specs=pl.BlockSpec((1, 12, KS, C * C), lambda i: (i, 0, 0, 0)),
        out_shape=pltpu.HBM((3, 12, KS, C * C), F32),
        compiler_params=params(24),
        cost_estimate=cost(10**9, 4 * 10**6),
        name="spectral_grad",
    )(*grads, *fields, *in_hbm(spread, wide))


def synthesise_kernel(got_ref, grad_ref, table_ref, zl_ref, mix_ref, out_ref, parts):
    step = pl.program_id(1)

    @pl.when(step == 0)
    def _():
        group = lane_group(8 * KS)
        for half in range(2):
            turned = []
            for q in range(4):
                tiles = []
                for kz in range(KS):
                    block, slot = divmod(2 * kz + half, 3)
                    tiles.append(got_ref[block, q, slot])
                value = jnp.concatenate(tiles, axis=0)
                turned.append(pltpu.roll(value, q * C, 1) if q else value)
            for p in range(4):
                value = turned[(-p) % 4]
                for g in range(1, 4):
                    value = jnp.where(group == g, turned[(g - p) % 4], value)
                parts[p, :, half * 128 : half * 128 + 128] = value.astype(BF16)

    for pair in range(2):
        timed = dot(parts[2 * step + pair], table_ref[pair]).astype(BF16)
        timed = jnp.concatenate([timed, jnp.zeros((64, NT * C), BF16)], axis=0)
        ys = slice(2 * pair, 2 * pair + 2)
        grad = grad_ref[0, :, ys].reshape(8 * N, NT * C)
        for side in range(2):
            lanes = slice(side * 256, side * 256 + 256)
            left = jnp.concatenate([zl_ref[...], grad[:, lanes]], axis=1)
            right = jnp.concatenate([timed[:, lanes], mix_ref[...]], axis=0)
            out_ref[0, :, ys, :, lanes] = dot(left, right).astype(BF16).reshape(4, 2, N, 256)


def synthesise(got, grad, mix, k):
    return pl.pallas_call(
        synthesise_kernel,
        grid=(2, 2),
        in_specs=[SENT, FIELD, TABLE_T, whole((8 * N, 256)), whole((256, 256))],
        out_specs=FIELD,
        out_shape=pltpu.HBM(grad.shape, BF16),
        scratch_shapes=[pltpu.VMEM((4, 8 * KS, MT * C), BF16)],
        compiler_params=params(24),
        cost_estimate=cost(4 * 10**9, 10 * 10**6),
        name="synthesise",
    )(got, *in_hbm(grad, k["tables_t"], k["zl_t"], mix))


def exchange_all(block):
    flat = block.reshape(128, 24, 128)
    return lax.all_to_all(flat, ("gx", "gy"), 0, 0, tiled=True).reshape(block.shape)


def exchange_first(block):
    flat = block.reshape(16, 192, 128)
    return lax.all_to_all(flat, "gx", 0, 0, tiled=True).reshape(block.shape)


def body(inputs, cotangent, pre_activation, pointwise, spectral):
    k = constants()
    xl, cy, spread = k["xl"], k["cy"], k["spread"]
    weights = jnp.transpose(spectral, (1, 2, 0, 3))
    mix = jnp.kron(jnp.eye(8, dtype=BF16), pointwise.T)
    sent, grad_pre = analyse_grad(cotangent, pre_activation, k)
    got = exchange_all(sent)
    got_input = exchange_first(analyse_input(inputs, k))
    grads = exchange_second(planes_forward(got, xl, cy))
    modes = exchange_second(mode_grad(grads, weights, k))
    back = exchange_first(back_x(exchange_second(back_y(modes, cy, spread)), k["xl_t"]))
    planes = exchange_second(planes_x(got_input, xl))
    fields = exchange_second(planes_y(planes, cy))
    weight_grad = spectral_grad(grads, fields, spread, k["wide"])
    return synthesise(back, grad_pre, mix, k), jnp.transpose(weight_grad, (2, 0, 1, 3))


def solution(mesh):
    in_specs = (
        P(None, "gx", "gy", None, None),
        P(None, "gx", "gy", None, None),
        P(None, "gx", "gy", None, None),
        P(),
        P(None, "gy", "gx", None),
    )
    out_specs = (P(None, "gx", "gy", None, None), P(None, "gy", "gx", None))
    return jax.shard_map(body, mesh=mesh, in_specs=in_specs, out_specs=out_specs, check_vma=False)
```

time: 154 us -> 144 us (0.935)
  local copies, waits for them, and re-layouts: 28.7 us -> 2.08 us
  waiting for transfers between devices: 37.3 us -> 49.2 us
  Pallas kernels: 34.7 us -> 43.5 us
  starting transfers between devices: 49.5 us -> 47.6 us
    unnamed x62 -> x28, local copies, waits for them, and re-layouts: 27.2 us -> 0.97 us
    all_to_all x3 -> x1, starting transfers between devices: 23.8 us -> 10.4 us  [exchange_all(): lax.all_to_all(flat, ('gx', 'gy'), 0, 0, tiled=True).reshape(block.shape)]
    all_to_all x0 -> x2, starting transfers between devices: none -> 12.8 us  [exchange_first(): return lax.all_to_all(flat, 'gx', 0, 0, tiled=True).reshape(block.shape)]
    ppermute x21 -> x20, waiting for transfers between devices: 21.9 us -> 32.9 us  [the longest x15 25.8 us: exchange_second(): lax.ppermute(pairs[sx - 1], 'gy', [(i, i ^ 2 * sx) for i in range(8)])]
    pallas_call x8 -> x15, Pallas kernels: 34.7 us -> 43.5 us  [the longest x1 11.8 us: analyse_grad(): pl.pallas_call(analyse_grad_kernel, grid=(2, 2), in_specs=[FIELD, FIELD,...]
    ppermute x21 -> x20, starting transfers between devices: 25.7 us -> 24.4 us  [the longest x15 23.9 us: exchange_second(): lax.ppermute(pairs[sx - 1], 'gy', [(i, i ^ 2 * sx) for i in range(8)])]
    all_to_all x3 -> x1, waiting for transfers between devices: 15.4 us -> 16.3 us  [exchange_all(): lax.all_to_all(flat, ('gx', 'gy'), 0, 0, tiled=True).reshape(block.shape)]
  transfers between devices with their start and end apart: 24 -> 23, of which waited for: 9 -> 20; matrix products, arithmetic and copies ran while one was open for 2% -> 1% of each run, Pallas kernels for 11% -> 17%
where the time goes in v2:
time: 144 us; the launch traced here: 143 us
  waiting for transfers between devices  49.2 us (34%)
  starting transfers between devices  47.6 us (33%)
  Pallas kernels  43.5 us (30%)
  local copies, waits for them, and re-layouts  2.08 us (1%)
    ppermute x15, waiting for transfers between devices, exchange_second(): lax.ppermute(pairs[sx - 1], 'gy', [(i, i ^ 2 * sx) for i in range(8)])  25.8 us
    ppermute x15, starting transfers between devices, exchange_second(): lax.ppermute(pairs[sx - 1], 'gy', [(i, i ^ 2 * sx) for i in range(8)])  23.9 us
    all_to_all x1, waiting for transfers between devices, exchange_all(): lax.all_to_all(flat, ('gx', 'gy'), 0, 0, tiled=True).reshape(block.shape)  16.3 us
    all_to_all x2, starting transfers between devices, exchange_first(): return lax.all_to_all(flat, 'gx', 0, 0, tiled=True).reshape(block.shape)  12.8 us
    pallas_call x1, Pallas kernels, analyse_grad(): pl.pallas_call(analyse_grad_kernel, grid=(2, 2), in_specs=[FIELD, FIELD,...  11.8 us
    all_to_all x1, starting transfers between devices, exchange_all(): lax.all_to_all(flat, ('gx', 'gy'), 0, 0, tiled=True).reshape(block.shape)  10.4 us
    pallas_call x1, Pallas kernels, synthesise(): pl.pallas_call(synthesise_kernel, grid=(2, 2), in_specs=[SENT, FIELD, TAB...  7.96 us
    pallas_call x1, Pallas kernels, analyse_input(): pl.pallas_call(analyse_input_kernel, grid=(2, 2), in_specs=[FIELD, TABLE,...  7.64 us
  transfers between devices with their start and end apart: 23, of which 20 were waited for; matrix products, arithmetic and copies ran while one was open for 1% of the time, Pallas kernels for 17%

profile of v2, /device:TPU:8, one launch (start us, length us, event | category | flops | bytes accessed | tf_op | source)
XLA Modules:
  0.0 143.3 jit_solution(5550406344671083124)
XLA Ops:
  0.6 11.8 %analyse_grad.1 = (f32[16,8,3,8,128]{4,3,2,1,0:T(8,128)}, bf16[2,4,8,64,512]{4,3,2,1,0:T(8,128)(2,1)}) custom-call(bf16[2,4,8,64,512]{4,3,2,1,0:T(8,128)(2,1)} %cot_ref.1, bf16[2,4,8,64,512]{4,3,2,1,0:T(8,128)(2,1)} %pre_ref.1, bf16[4,512,256]{2,1,0:T(8,128)(2,1)} %constant.20.clone.table_ref, bf16[192,512]{1,0:T(8,128)(2,1)} %constant.21.clone.zl_ref), custom_call_target="tpu_custom_call" | custom-call | flops 4000000000 | bytes 14000000 | tf_op jit(solution)/shard_map/analyse_grad/pallas_call | solution.py:178
  12.4 10.4 %all-to-all-start = ((f32[128,24,128]{2,1,0:T(8,128)}), f32[128,24,128]{2,1,0:T(8,128)S(1)}, u32[]{:S(2)}, u32[]{:S(2)}) async-start(f32[128,24,128]{2,1,0:T(8,128)} %bitcast.17), calls=%async_computation | async-start | bytes 3145728 | tf_op jit(solution)/shard_map/all_to_all | solution.py:540
  22.8 7.6 %analyse_input.1 = f32[16,8,3,8,128]{4,3,2,1,0:T(8,128)} custom-call(bf16[2,4,8,64,512]{4,3,2,1,0:T(8,128)(2,1)} %field_ref.1, bf16[4,512,256]{2,1,0:T(8,128)(2,1)} %constant.20.clone.table_ref, bf16[192,512]{1,0:T(8,128)(2,1)} %constant.21.clone.zl_ref), custom_call_target="tpu_custom_call" | custom-call | flops 4000000000 | bytes 6000000 | tf_op jit(solution)/shard_map/analyse_input/pallas_call | solution.py:196
  30.5 16.3 %all-to-all-done = f32[128,24,128]{2,1,0:T(8,128)S(1)} async-done(((f32[128,24,128]{2,1,0:T(8,128)}), f32[128,24,128]{2,1,0:T(8,128)S(1)}, u32[]{:S(2)}, u32[]{:S(2)}) %all-to-all-start) | async-done | bytes 1572896 | tf_op jit(solution)/shard_map/all_to_all | solution.py:540
  46.8 5.4 %all-to-all-start.2 = ((f32[16,192,128]{2,1,0:T(8,128)}), f32[16,192,128]{2,1,0:T(8,128)S(1)}, u32[]{:S(2)}, u32[]{:S(2)}) async-start(f32[16,192,128]{2,1,0:T(8,128)} %bitcast.15), calls=%async_computation.2 | async-start | bytes 3145728 | tf_op jit(solution)/shard_map/all_to_all | solution.py:545
  53.1 2.5 %planes_forward.1 = (f32[4,72,128]{2,1,0:T(8,128)S(1)}, f32[4,72,128]{2,1,0:T(8,128)S(1)}) custom-call(f32[16,8,3,8,128]{4,3,2,1,0:T(8,128)S(1)} %bitcast.13, bf16[48,256]{1,0:T(8,128)(2,1)S(1)} %copy-done.11, f32[8,3,16,128]{3,2,1,0:T(8,128)S(1)} %copy-done.7), custom_call_target="tpu_custom_call" | custom-call | flops 1000000000 | bytes 3000000 | tf_op jit(solution)/shard_map/planes_forward/pallas_call | solution.py:271
  59.4 2.5 %collective-permute-start.3 = (f32[2,72,128]{2,1,0:T(8,128)S(1)}, f32[2,72,128]{2,1,0:T(8,128)S(1)}, u32[]{:S(2)}, u32[]{:S(2)}) collective-permute-start(f32[2,72,128]{2,1,0:T(8,128)S(1)} %get-tuple-element.34), channel_id=1, source_target_pairs={{0,6},{1,7},{2,4},{3,5},{4,2},{5,3},{6,0},{7,1},{8,14},{9,15},{10,... | collective-permute-start | bytes 221192 | tf_op jit(solution)/shard_map/ppermute | solution.py:398
  65.1 3.8 %mode_grad.1 = (f32[4,72,128]{2,1,0:T(8,128)S(1)}, f32[4,72,128]{2,1,0:T(8,128)S(1)}) custom-call(f32[4,72,128]{2,1,0:T(8,128)S(1)} %get-tuple-element.30.keep_ref.refs_0_, f32[4,72,128]{2,1,0:T(8,128)S(1)} %collective-permute-done.cross_ref.refs_1_, f32[2,72,128]{2,1,0:T(8,128)S(1)} %collective-permute-done.1.refs_2_, ...), custom_call_target="tpu_custom_call" | custom-call | flops 1000000000 | bytes 4000000 | tf_op jit(solution)/shard_map/mode_grad/pallas_call | solution.py:438
  70.5 3.7 %collective-permute-start.6 = (f32[2,72,128]{2,1,0:T(8,128)S(1)}, f32[2,72,128]{2,1,0:T(8,128)S(1)}, u32[]{:S(2)}, u32[]{:S(2)}) collective-permute-start(f32[2,72,128]{2,1,0:T(8,128)S(1)} %get-tuple-element.38), channel_id=1, source_target_pairs={{0,4},{1,5},{2,6},{3,7},{4,0},{5,1},{6,2},{7,3},{8,12},{9,13},{10,... | collective-permute-start | bytes 221192 | tf_op jit(solution)/shard_map/ppermute | solution.py:398
  75.3 2.9 %collective-permute-done.6.refs_3_ = f32[2,72,128]{2,1,0:T(8,128)S(1)} collective-permute-done((f32[2,72,128]{2,1,0:T(8,128)S(1)}, f32[2,72,128]{2,1,0:T(8,128)S(1)}, u32[]{:S(2)}, u32[]{:S(2)}) %collective-permute-start.6) | collective-permute-done | bytes 73760 | tf_op jit(solution)/shard_map/ppermute | solution.py:398
  83.0 2.4 %collective-permute-start.10 = (f32[2,144,128]{2,1,0:T(8,128)S(1)}, f32[2,144,128]{2,1,0:T(8,128)S(1)}, u32[]{:S(2)}, u32[]{:S(2)}) collective-permute-start(f32[2,144,128]{2,1,0:T(8,128)S(1)} %get-tuple-element.43), channel_id=1, source_target_pairs={{0,4},{1,5},{2,6},{3,7},{4,0},{5,1},{6,2},{7,3},{8,12},{9,13},{10,... | collective-permute-start | bytes 442376 | tf_op jit(solution)/shard_map/ppermute | solution.py:398
  85.4 2.3 %collective-permute-start.11 = (f32[2,144,128]{2,1,0:T(8,128)S(1)}, f32[2,144,128]{2,1,0:T(8,128)S(1)}, u32[]{:S(2)}, u32[]{:S(2)}) collective-permute-start(f32[2,144,128]{2,1,0:T(8,128)S(1)} %get-tuple-element.44), channel_id=1, source_target_pairs={{0,6},{1,7},{2,4},{3,5},{4,2},{5,3},{6,0},{7,1},{8,14},{9,15},{10,... | collective-permute-start | bytes 442376 | tf_op jit(solution)/shard_map/ppermute | solution.py:398
  87.7 2.0 %collective-permute-done.9.refs_2_ = f32[2,144,128]{2,1,0:T(8,128)S(1)} collective-permute-done((f32[2,144,128]{2,1,0:T(8,128)S(1)}, f32[2,144,128]{2,1,0:T(8,128)S(1)}, u32[]{:S(2)}, u32[]{:S(2)}) %collective-permute-start.9) | collective-permute-done | bytes 147488 | tf_op jit(solution)/shard_map/ppermute | solution.py:398
  89.7 2.8 %collective-permute-done.10.refs_3_ = f32[2,144,128]{2,1,0:T(8,128)S(1)} collective-permute-done((f32[2,144,128]{2,1,0:T(8,128)S(1)}, f32[2,144,128]{2,1,0:T(8,128)S(1)}, u32[]{:S(2)}, u32[]{:S(2)}) %collective-permute-start.10) | collective-permute-done | bytes 147488 | tf_op jit(solution)/shard_map/ppermute | solution.py:398
  92.5 2.4 %collective-permute-done.11.refs_4_ = f32[2,144,128]{2,1,0:T(8,128)S(1)} collective-permute-done((f32[2,144,128]{2,1,0:T(8,128)S(1)}, f32[2,144,128]{2,1,0:T(8,128)S(1)}, u32[]{:S(2)}, u32[]{:S(2)}) %collective-permute-start.11) | collective-permute-done | bytes 147488 | tf_op jit(solution)/shard_map/ppermute | solution.py:398
  96.5 7.4 %all-to-all-start.1 = ((f32[16,192,128]{2,1,0:T(8,128)}), f32[16,192,128]{2,1,0:T(8,128)S(1)}, u32[]{:S(2)}, u32[]{:S(2)}) async-start(f32[16,192,128]{2,1,0:T(8,128)} %bitcast.16), calls=%async_computation.1 | async-start | bytes 3145728 | tf_op jit(solution)/shard_map/all_to_all | solution.py:545
  106.1 3.8 %collective-permute-start.14 = (f32[2,144,128]{2,1,0:T(8,128)S(1)}, f32[2,144,128]{2,1,0:T(8,128)S(1)}, u32[]{:S(2)}, u32[]{:S(2)}) collective-permute-start(f32[2,144,128]{2,1,0:T(8,128)S(1)} %get-tuple-element.49), channel_id=1, source_target_pairs={{0,4},{1,5},{2,6},{3,7},{4,0},{5,1},{6,2},{7,3},{8,12},{9,13},{10,... | collective-permute-start | bytes 442376 | tf_op jit(solution)/shard_map/ppermute | solution.py:398
  112.7 4.3 %collective-permute-done.14.refs_3_ = f32[2,144,128]{2,1,0:T(8,128)S(1)} collective-permute-done((f32[2,144,128]{2,1,0:T(8,128)S(1)}, f32[2,144,128]{2,1,0:T(8,128)S(1)}, u32[]{:S(2)}, u32[]{:S(2)}) %collective-permute-start.14) | collective-permute-done | bytes 147488 | tf_op jit(solution)/shard_map/ppermute | solution.py:398
  117.0 2.5 %collective-permute-done.15.refs_4_ = f32[2,144,128]{2,1,0:T(8,128)S(1)} collective-permute-done((f32[2,144,128]{2,1,0:T(8,128)S(1)}, f32[2,144,128]{2,1,0:T(8,128)S(1)}, u32[]{:S(2)}, u32[]{:S(2)}) %collective-permute-start.15) | collective-permute-done | bytes 147488 | tf_op jit(solution)/shard_map/ppermute | solution.py:398
  119.5 2.2 %planes_y.1 = (f32[4,72,128]{2,1,0:T(8,128)S(1)}, f32[4,72,128]{2,1,0:T(8,128)S(1)}) custom-call(f32[4,144,128]{2,1,0:T(8,128)S(1)} %get-tuple-element.46.keep_ref.refs_0_, f32[4,144,128]{2,1,0:T(8,128)S(1)} %collective-permute-done.12.cross_ref.refs_1_, f32[2,144,128]{2,1,0:T(8,128)S(1)} %collective-permute-done.13.refs_2_, ...), custom_call_target="tpu_custom_call" | custom-call | flops 1000000000 | bytes 2000000 | tf_op jit(solution)/shard_map/planes_y/pallas_call | solution.py:305
  123.2 2.3 %collective-permute-start.18 = (f32[2,72,128]{2,1,0:T(8,128)S(1)}, f32[2,72,128]{2,1,0:T(8,128)S(1)}, u32[]{:S(2)}, u32[]{:S(2)}) collective-permute-start(f32[2,72,128]{2,1,0:T(8,128)S(1)} %get-tuple-element.54), channel_id=1, source_target_pairs={{0,4},{1,5},{2,6},{3,7},{4,0},{5,1},{6,2},{7,3},{8,12},{9,13},{10,... | collective-permute-start | bytes 221192 | tf_op jit(solution)/shard_map/ppermute | solution.py:398
  125.5 2.4 %collective-permute-start.19 = (f32[2,72,128]{2,1,0:T(8,128)S(1)}, f32[2,72,128]{2,1,0:T(8,128)S(1)}, u32[]{:S(2)}, u32[]{:S(2)}) collective-permute-start(f32[2,72,128]{2,1,0:T(8,128)S(1)} %get-tuple-element.55), channel_id=1, source_target_pairs={{0,6},{1,7},{2,4},{3,5},{4,2},{5,3},{6,0},{7,1},{8,14},{9,15},{10,... | collective-permute-start | bytes 221192 | tf_op jit(solution)/shard_map/ppermute | solution.py:398
  131.1 4.2 %spectral_grad.1 = f32[3,12,24,1024]{3,2,1,0:T(8,128)} custom-call(f32[4,72,128]{2,1,0:T(8,128)S(1)} %get-tuple-element.30.keep_ref.refs_0_, f32[4,72,128]{2,1,0:T(8,128)S(1)} %collective-permute-done.cross_ref.refs_1_, f32[2,72,128]{2,1,0:T(8,128)S(1)} %copy-done.2, f32[2,72,128]{2,1,0:T(8,128)S(1)} %copy-done.4, f32[2,72,128]{2,1,0:T(8,128)S(1)} %copy-done.6, ...), custom_call_target="tpu_custom_call" | custom-call | flops 1000000000 | bytes 4000000 | tf_op jit(solution)/shard_map/spectral_grad/pallas_call | solution.py:472
  135.4 8.0 %synthesise.1 = bf16[2,4,8,64,512]{4,3,2,1,0:T(8,128)(2,1)} custom-call(f32[16,8,3,8,128]{4,3,2,1,0:T(8,128)S(1)} %bitcast.12, bf16[2,4,8,64,512]{4,3,2,1,0:T(8,128)(2,1)} %get-tuple-element.45.grad_ref, bf16[4,256,512]{2,1,0:T(8,128)(2,1)} %constant.28.clone.table_ref, bf16[512,256]{1,0:T(8,128)(2,1)} %constant.29.clone.zl_ref, bf16[256,256]{1,0:T(8,128)(2,1)} %mul.27.mix_ref), custom_call_target="tpu_custom_call" | custom-call | flops 4000000000 | bytes 10000000 | tf_op jit(solution)/shard_map/synthesise/pallas_call | solution.py:525
  (69 shorter events, 26.6 us)
Async XLA Ops:
  12.4 34.4 %all-to-all-start = ((f32[128,24,128]{2,1,0:T(8,128)}), f32[128,24,128]{2,1,0:T(8,128)S(1)}, u32[]{:S(2)}, u32[]{:S(2)}) async-start(f32[128,24,128]{2,1,0:T(8,128)} %bitcast.17), calls=%async_computation | async-start | bytes 3145728 | tf_op jit(solution)/shard_map/all_to_all | solution.py:540
  30.5 21.7 %copy-start.11 = (bf16[48,256]{1,0:T(8,128)(2,1)S(1)}, bf16[48,256]{1,0:T(8,128)(2,1)}, u32[]{:S(2)}) copy-start(bf16[48,256]{1,0:T(8,128)(2,1)} %constant.22.clone.xl_ref) | copy-start | bytes 73732
  46.8 49.7 %all-to-all-start.2 = ((f32[16,192,128]{2,1,0:T(8,128)}), f32[16,192,128]{2,1,0:T(8,128)S(1)}, u32[]{:S(2)}, u32[]{:S(2)}) async-start(f32[16,192,128]{2,1,0:T(8,128)} %bitcast.15), calls=%async_computation.2 | async-start | bytes 3145728 | tf_op jit(solution)/shard_map/all_to_all | solution.py:545
  55.6 1.5 %collective-permute-start = (f32[4,72,128]{2,1,0:T(8,128)S(1)}, f32[4,72,128]{2,1,0:T(8,128)S(1)}, u32[]{:S(2)}, u32[]{:S(2)}) collective-permute-start(f32[4,72,128]{2,1,0:T(8,128)S(1)} %get-tuple-element.31), channel_id=1, source_target_pairs={{0,1},{1,0},{2,3},{3,2},{4,5},{5,4},{6,7},{7,6},{8,9},{9,8},{10,11... | collective-permute-start | bytes 442376 | tf_op jit(solution)/shard_map/ppermute | solution.py:396
  57.1 5.2 %collective-permute-start.1 = (f32[2,72,128]{2,1,0:T(8,128)S(1)}, f32[2,72,128]{2,1,0:T(8,128)S(1)}, u32[]{:S(2)}, u32[]{:S(2)}) collective-permute-start(f32[2,72,128]{2,1,0:T(8,128)S(1)} %get-tuple-element.32), channel_id=1, source_target_pairs={{0,2},{1,3},{2,0},{3,1},{4,6},{5,7},{6,4},{7,5},{8,10},{9,11},{10,... | collective-permute-start | bytes 221192 | tf_op jit(solution)/shard_map/ppermute | solution.py:398
  57.8 6.0 %collective-permute-start.2 = (f32[2,72,128]{2,1,0:T(8,128)S(1)}, f32[2,72,128]{2,1,0:T(8,128)S(1)}, u32[]{:S(2)}, u32[]{:S(2)}) collective-permute-start(f32[2,72,128]{2,1,0:T(8,128)S(1)} %get-tuple-element.33), channel_id=1, source_target_pairs={{0,4},{1,5},{2,6},{3,7},{4,0},{5,1},{6,2},{7,3},{8,12},{9,13},{10,... | collective-permute-start | bytes 221192 | tf_op jit(solution)/shard_map/ppermute | solution.py:398
  59.4 5.8 %collective-permute-start.3 = (f32[2,72,128]{2,1,0:T(8,128)S(1)}, f32[2,72,128]{2,1,0:T(8,128)S(1)}, u32[]{:S(2)}, u32[]{:S(2)}) collective-permute-start(f32[2,72,128]{2,1,0:T(8,128)S(1)} %get-tuple-element.34), channel_id=1, source_target_pairs={{0,6},{1,7},{2,4},{3,5},{4,2},{5,3},{6,0},{7,1},{8,14},{9,15},{10,... | collective-permute-start | bytes 221192 | tf_op jit(solution)/shard_map/ppermute | solution.py:398
  68.9 1.5 %collective-permute-start.4 = (f32[4,72,128]{2,1,0:T(8,128)S(1)}, f32[4,72,128]{2,1,0:T(8,128)S(1)}, u32[]{:S(2)}, u32[]{:S(2)}) collective-permute-start(f32[4,72,128]{2,1,0:T(8,128)S(1)} %get-tuple-element.36), channel_id=1, source_target_pairs={{0,1},{1,0},{2,3},{3,2},{4,5},{5,4},{6,7},{7,6},{8,9},{9,8},{10,11... | collective-permute-start | bytes 442376 | tf_op jit(solution)/shard_map/ppermute | solution.py:396
  70.4 4.9 %collective-permute-start.5 = (f32[2,72,128]{2,1,0:T(8,128)S(1)}, f32[2,72,128]{2,1,0:T(8,128)S(1)}, u32[]{:S(2)}, u32[]{:S(2)}) collective-permute-start(f32[2,72,128]{2,1,0:T(8,128)S(1)} %get-tuple-element.37), channel_id=1, source_target_pairs={{0,2},{1,3},{2,0},{3,1},{4,6},{5,7},{6,4},{7,5},{8,10},{9,11},{10,... | collective-permute-start | bytes 221192 | tf_op jit(solution)/shard_map/ppermute | solution.py:398
  70.5 7.7 %collective-permute-start.6 = (f32[2,72,128]{2,1,0:T(8,128)S(1)}, f32[2,72,128]{2,1,0:T(8,128)S(1)}, u32[]{:S(2)}, u32[]{:S(2)}) collective-permute-start(f32[2,72,128]{2,1,0:T(8,128)S(1)} %get-tuple-element.38), channel_id=1, source_target_pairs={{0,4},{1,5},{2,6},{3,7},{4,0},{5,1},{6,2},{7,3},{8,12},{9,13},{10,... | collective-permute-start | bytes 221192 | tf_op jit(solution)/shard_map/ppermute | solution.py:398
  74.3 5.6 %collective-permute-start.7 = (f32[2,72,128]{2,1,0:T(8,128)S(1)}, f32[2,72,128]{2,1,0:T(8,128)S(1)}, u32[]{:S(2)}, u32[]{:S(2)}) collective-permute-start(f32[2,72,128]{2,1,0:T(8,128)S(1)} %get-tuple-element.39), channel_id=1, source_target_pairs={{0,6},{1,7},{2,4},{3,5},{4,2},{5,3},{6,0},{7,1},{8,14},{9,15},{10,... | collective-permute-start | bytes 221192 | tf_op jit(solution)/shard_map/ppermute | solution.py:398
  81.2 1.7 %collective-permute-start.8 = (f32[4,144,128]{2,1,0:T(8,128)S(1)}, f32[4,144,128]{2,1,0:T(8,128)S(1)}, u32[]{:S(2)}, u32[]{:S(2)}) collective-permute-start(f32[4,144,128]{2,1,0:T(8,128)S(1)} %get-tuple-element.41), channel_id=1, source_target_pairs={{0,1},{1,0},{2,3},{3,2},{4,5},{5,4},{6,7},{7,6},{8,9},{9,8},{10,11... | collective-permute-start | bytes 884744 | tf_op jit(solution)/shard_map/ppermute | solution.py:396
  82.9 6.8 %collective-permute-start.9 = (f32[2,144,128]{2,1,0:T(8,128)S(1)}, f32[2,144,128]{2,1,0:T(8,128)S(1)}, u32[]{:S(2)}, u32[]{:S(2)}) collective-permute-start(f32[2,144,128]{2,1,0:T(8,128)S(1)} %get-tuple-element.42), channel_id=1, source_target_pairs={{0,2},{1,3},{2,0},{3,1},{4,6},{5,7},{6,4},{7,5},{8,10},{9,11},{10,... | collective-permute-start | bytes 442376 | tf_op jit(solution)/shard_map/ppermute | solution.py:398
  83.0 9.5 %collective-permute-start.10 = (f32[2,144,128]{2,1,0:T(8,128)S(1)}, f32[2,144,128]{2,1,0:T(8,128)S(1)}, u32[]{:S(2)}, u32[]{:S(2)}) collective-permute-start(f32[2,144,128]{2,1,0:T(8,128)S(1)} %get-tuple-element.43), channel_id=1, source_target_pairs={{0,4},{1,5},{2,6},{3,7},{4,0},{5,1},{6,2},{7,3},{8,12},{9,13},{10,... | collective-permute-start | bytes 442376 | tf_op jit(solution)/shard_map/ppermute | solution.py:398
  85.4 9.5 %collective-permute-start.11 = (f32[2,144,128]{2,1,0:T(8,128)S(1)}, f32[2,144,128]{2,1,0:T(8,128)S(1)}, u32[]{:S(2)}, u32[]{:S(2)}) collective-permute-start(f32[2,144,128]{2,1,0:T(8,128)S(1)} %get-tuple-element.44), channel_id=1, source_target_pairs={{0,6},{1,7},{2,4},{3,5},{4,2},{5,3},{6,0},{7,1},{8,14},{9,15},{10,... | collective-permute-start | bytes 442376 | tf_op jit(solution)/shard_map/ppermute | solution.py:398
  96.5 38.9 %all-to-all-start.1 = ((f32[16,192,128]{2,1,0:T(8,128)}), f32[16,192,128]{2,1,0:T(8,128)S(1)}, u32[]{:S(2)}, u32[]{:S(2)}) async-start(f32[16,192,128]{2,1,0:T(8,128)} %bitcast.16), calls=%async_computation.1 | async-start | bytes 3145728 | tf_op jit(solution)/shard_map/all_to_all | solution.py:545
  104.3 1.7 %collective-permute-start.12 = (f32[4,144,128]{2,1,0:T(8,128)S(1)}, f32[4,144,128]{2,1,0:T(8,128)S(1)}, u32[]{:S(2)}, u32[]{:S(2)}) collective-permute-start(f32[4,144,128]{2,1,0:T(8,128)S(1)} %get-tuple-element.47), channel_id=1, source_target_pairs={{0,1},{1,0},{2,3},{3,2},{4,5},{5,4},{6,7},{7,6},{8,9},{9,8},{10,11... | collective-permute-start | bytes 884744 | tf_op jit(solution)/shard_map/ppermute | solution.py:396
  106.0 6.8 %collective-permute-start.13 = (f32[2,144,128]{2,1,0:T(8,128)S(1)}, f32[2,144,128]{2,1,0:T(8,128)S(1)}, u32[]{:S(2)}, u32[]{:S(2)}) collective-permute-start(f32[2,144,128]{2,1,0:T(8,128)S(1)} %get-tuple-element.48), channel_id=1, source_target_pairs={{0,2},{1,3},{2,0},{3,1},{4,6},{5,7},{6,4},{7,5},{8,10},{9,11},{10,... | collective-permute-start | bytes 442376 | tf_op jit(solution)/shard_map/ppermute | solution.py:398
  106.1 11.0 %collective-permute-start.14 = (f32[2,144,128]{2,1,0:T(8,128)S(1)}, f32[2,144,128]{2,1,0:T(8,128)S(1)}, u32[]{:S(2)}, u32[]{:S(2)}) collective-permute-start(f32[2,144,128]{2,1,0:T(8,128)S(1)} %get-tuple-element.49), channel_id=1, source_target_pairs={{0,4},{1,5},{2,6},{3,7},{4,0},{5,1},{6,2},{7,3},{8,12},{9,13},{10,... | collective-permute-start | bytes 442376 | tf_op jit(solution)/shard_map/ppermute | solution.py:398
  109.9 9.6 %collective-permute-start.15 = (f32[2,144,128]{2,1,0:T(8,128)S(1)}, f32[2,144,128]{2,1,0:T(8,128)S(1)}, u32[]{:S(2)}, u32[]{:S(2)}) collective-permute-start(f32[2,144,128]{2,1,0:T(8,128)S(1)} %get-tuple-element.50), channel_id=1, source_target_pairs={{0,6},{1,7},{2,4},{3,5},{4,2},{5,3},{6,0},{7,1},{8,14},{9,15},{10,... | collective-permute-start | bytes 442376 | tf_op jit(solution)/shard_map/ppermute | solution.py:398
  121.7 1.5 %collective-permute-start.16 = (f32[4,72,128]{2,1,0:T(8,128)S(1)}, f32[4,72,128]{2,1,0:T(8,128)S(1)}, u32[]{:S(2)}, u32[]{:S(2)}) collective-permute-start(f32[4,72,128]{2,1,0:T(8,128)S(1)} %get-tuple-element.52), channel_id=1, source_target_pairs={{0,1},{1,0},{2,3},{3,2},{4,5},{5,4},{6,7},{7,6},{8,9},{9,8},{10,11... | collective-permute-start | bytes 442376 | tf_op jit(solution)/shard_map/ppermute | solution.py:396
  123.1 5.9 %collective-permute-start.17 = (f32[2,72,128]{2,1,0:T(8,128)S(1)}, f32[2,72,128]{2,1,0:T(8,128)S(1)}, u32[]{:S(2)}, u32[]{:S(2)}) collective-permute-start(f32[2,72,128]{2,1,0:T(8,128)S(1)} %get-tuple-element.53), channel_id=1, source_target_pairs={{0,2},{1,3},{2,0},{3,1},{4,6},{5,7},{6,4},{7,5},{8,10},{9,11},{10,... | collective-permute-start | bytes 221192 | tf_op jit(solution)/shard_map/ppermute | solution.py:398
  123.2 6.3 %collective-permute-start.18 = (f32[2,72,128]{2,1,0:T(8,128)S(1)}, f32[2,72,128]{2,1,0:T(8,128)S(1)}, u32[]{:S(2)}, u32[]{:S(2)}) collective-permute-start(f32[2,72,128]{2,1,0:T(8,128)S(1)} %get-tuple-element.54), channel_id=1, source_target_pairs={{0,4},{1,5},{2,6},{3,7},{4,0},{5,1},{6,2},{7,3},{8,12},{9,13},{10,... | collective-permute-start | bytes 221192 | tf_op jit(solution)/shard_map/ppermute | solution.py:398
  125.5 5.6 %collective-permute-start.19 = (f32[2,72,128]{2,1,0:T(8,128)S(1)}, f32[2,72,128]{2,1,0:T(8,128)S(1)}, u32[]{:S(2)}, u32[]{:S(2)}) collective-permute-start(f32[2,72,128]{2,1,0:T(8,128)S(1)} %get-tuple-element.55), channel_id=1, source_target_pairs={{0,6},{1,7},{2,4},{3,5},{4,2},{5,3},{6,0},{7,1},{8,14},{9,15},{10,... | collective-permute-start | bytes 221192 | tf_op jit(solution)/shard_map/ppermute | solution.py:398
  (13 other events, 162.5 us)

commit v3 on v2

--- a/solution.py
+++ b/solution.py
@@ -62,23 +62,31 @@
     forms = [np.einsum("xk,hg->hkxg", part, eye_h).reshape(2 * KS, 2 * N) for part in (high, low)]
     out["xl"] = np.concatenate(forms, axis=1).astype(BF)
     out["xl_t"] = np.concatenate([form.T for form in forms], axis=1).astype(BF)
+    padded = np.zeros((N, 8, 4), np.float32)
+    padded[:, :, :3] = basis.reshape(N, 8, 3)
+    yb = np.einsum("slhdk,ce->shlcdke", padded.reshape(8, 4, 2, 8, 4), eye_c)
+    out["yb"] = yb.reshape(8, 256, 1024).astype(BF)
     second = basis.reshape(8, 4, 2, 8, 3)
     out["cy"] = np.repeat(np.einsum("slhdj->djhsl", second).reshape(8, 3, 16, 4), C, axis=3)
-    spread = np.zeros((3, 4, C, 4, C), np.float32)
-    gather = np.zeros((3, C, C, 4, C), np.float32)
-    wide = np.zeros((3, 4, C, C, C), np.float32)
-    for ky in range(3):
-        spread[ky, ky] = eye_c[:, None, :]
-        gather[ky, :, :, ky, :] = eye_c[:, None, :]
-        wide[ky, ky] = eye_c[:, :, None]
-    out["spread"] = spread.reshape(3, 128, 128).astype(BF)
-    out["gather"] = gather.reshape(3, C * C, 128).astype(BF)
-    out["wide"] = wide.reshape(3, 128, C * C).astype(BF)
+    spread = np.zeros((4, 4, C, 4, C), np.float32)
+    gather = np.zeros((4, C, C, 4, C), np.float32)
+    wide = np.zeros((4, 4, C, C, C), np.float32)
+    for j in range(4):
+        spread[j, j] = eye_c[:, None, :]
+        gather[j, :, :, j, :] = eye_c[:, None, :]
+        wide[j, j] = eye_c[:, :, None]
+    out["spread"] = spread.reshape(4, 128, 128).astype(BF)
+    out["gather"] = gather.reshape(4, C * C, 128).astype(BF)
+    out["wide"] = wide.reshape(4, 128, C * C).astype(BF)
     return out
 
 
 def dot(a, b):
     return jnp.dot(a, b, preferred_element_type=F32)
+
+
+def dot_t(a, b):
+    return lax.dot_general(a, b, (((1,), (1,)), ((), ())), preferred_element_type=F32)
 
 
 def gelu_slope(v):
@@ -154,7 +162,7 @@
 TABLE_T = pl.BlockSpec((2, MT * C, NT * C), lambda b, p: (p, 0, 0))
 SENT = pl.BlockSpec((16, 4, 3, 8, 128), lambda b, p: (0, b, 0, 0, 0))
 SENT_SHAPE = (16, 8, 3, 8, 128)
-PART, PLANE = 72, 144
+TILES = (6, 72, 128)
 ANY = pl.BlockSpec(memory_space=pl.ANY)
 
 
@@ -204,6 +212,95 @@
         cost_estimate=cost(4 * 10**9, 6 * 10**6),
         name="analyse_input",
     )(*in_hbm(inputs, k["tables"], k["zl"]))
+
+
+def mode_of(j, t):
+    return (j, t) if j < 3 else (t, 3)
+
+
+def forward_kernel(got_ref, xl_ref, yb_hbm, keep_ref, cross_ref, yb_ref, fields, blocks, sem):
+    me = lax.axis_index("gy")
+    copy = pltpu.make_async_copy(yb_hbm.at[me], yb_ref, sem)
+    copy.start()
+    for slot in range(3):
+        field = jnp.concatenate(
+            [got_ref[:, d, slot].reshape(128, 128).astype(BF16) for d in range(8)], axis=1
+        )
+        wide = dot(xl_ref[...], jnp.concatenate([field, field], axis=0))
+        for d in range(8):
+            for half in range(2):
+                rows = slice(d * 72 + slot * KS, d * 72 + slot * KS + KS)
+                fields[rows, half * 128 : half * 128 + 128] = wide[
+                    half * KS : half * KS + KS, d * 128 : d * 128 + 128
+                ]
+    copy.wait()
+    group = lane_group(72)
+    field = fields[...].astype(BF16)
+    for to in range(8):
+        part = dot(field, yb_ref[:, to * 128 : to * 128 + 128])
+        for b in range(2):
+            last = part[(4 * b + 3) * 72 : (4 * b + 4) * 72]
+            for t in range(3):
+                value = part[(4 * b + t) * 72 : (4 * b + t + 1) * 72]
+                blocks[to, 3 * b + t] = jnp.where(group == 3, pltpu.roll(last, 96 - 32 * t, 1), value)
+    for sx in range(4):
+        keep_ref[sx] = blocks[me ^ (2 * sx)]
+        cross_ref[sx] = blocks[me ^ (2 * sx + 1)]
+
+
+def forward(got, k):
+    vmem = pl.BlockSpec(memory_space=pltpu.VMEM)
+    return pl.pallas_call(
+        forward_kernel,
+        in_specs=[vmem, vmem, ANY],
+        out_shape=[jax.ShapeDtypeStruct((4, *TILES), F32)] * 2,
+        scratch_shapes=[
+            pltpu.VMEM((256, 1024), BF16),
+            pltpu.VMEM((576, 256), F32),
+            pltpu.VMEM((8, *TILES), F32),
+            pltpu.SemaphoreType.DMA,
+        ],
+        compiler_params=params(16),
+        cost_estimate=cost(10**9, 4 * 10**6),
+        name="forward",
+    )(got, k["xl"], *in_hbm(k["yb"]))
+
+
+def add_cores_kernel(keep_ref, cross_ref, *outs):
+    for sx in range(4):
+        outs[sx][...] = keep_ref[sx] + cross_ref[sx]
+
+
+def add_cores(keep, cross):
+    return pl.pallas_call(
+        add_cores_kernel,
+        out_shape=[jax.ShapeDtypeStruct(TILES, F32)] * 4,
+        compiler_params=params(16),
+        cost_estimate=cost(10**6, 10**6),
+        name="add_cores",
+    )(keep, cross)
+
+
+def across(block, sx):
+    return lax.ppermute(block, "gy", [(i, i ^ sx) for i in range(8)])
+
+
+def reduce_cores(blocks):
+    keep, cross = blocks
+    return add_cores(keep, across(cross, 1))
+
+
+def reduce_chips(sums):
+    own, *others = sums
+    return [own] + [across(other, 2 * sx + 2) for sx, other in enumerate(others)]
+
+
+def gather_second(block):
+    parts = [block, across(block, 1)]
+    for sx in range(1, 4):
+        far = across(block, 2 * sx)
+        parts += [far, across(far, 1)]
+    return parts
 
 
 def transform_x(got_ref, xl_ref, planes):
@@ -260,118 +357,31 @@
         blocks[me ^ s] = parts[s][...]
 
 
-def planes_forward_kernel(got_ref, xl_ref, cy_ref, *rest):
-    keep_ref, cross_ref, planes, blocks = rest
+def planes_kernel(got_ref, xl_ref, cy_hbm, keep_ref, cross_ref, cy_ref, planes, blocks, sem):
+    copy = pltpu.make_async_copy(cy_hbm, cy_ref, sem)
+    copy.start()
     transform_x(got_ref, xl_ref, planes)
+    copy.wait()
     transform_y(planes, cy_ref, blocks)
     deal(blocks, keep_ref, cross_ref)
 
 
-def planes_forward(got, xl, cy):
-    return pl.pallas_call(
-        planes_forward_kernel,
-        out_shape=[group_shape(PART)] * 2,
-        scratch_shapes=[pltpu.VMEM((8, PLANE, 128), F32), pltpu.VMEM((8, PART, 128), F32)],
+def planes(got, k):
+    vmem = pl.BlockSpec(memory_space=pltpu.VMEM)
+    return pl.pallas_call(
+        planes_kernel,
+        in_specs=[vmem, vmem, ANY],
+        out_shape=[group_shape(72)] * 2,
+        scratch_shapes=[
+            pltpu.VMEM((8, 3, 16, 128), F32),
+            pltpu.VMEM((8, 144, 128), F32),
+            pltpu.VMEM((8, 72, 128), F32),
+            pltpu.SemaphoreType.DMA,
+        ],
         compiler_params=params(16),
         cost_estimate=cost(10**9, 3 * 10**6),
-        name="planes_forward",
-    )(got, xl, cy)
-
-
-def planes_x_kernel(got_ref, xl_ref, keep_ref, cross_ref, planes):
-    transform_x(got_ref, xl_ref, planes)
-    deal(planes, keep_ref, cross_ref)
-
-
-def planes_x(got, xl):
-    return pl.pallas_call(
-        planes_x_kernel,
-        out_shape=[group_shape(PLANE)] * 2,
-        scratch_shapes=[pltpu.VMEM((8, PLANE, 128), F32)],
-        compiler_params=params(16),
-        cost_estimate=cost(10**9, 2 * 10**6),
-        name="planes_x",
-    )(got, xl)
-
-
-def planes_y_kernel(*refs):
-    parts, (cy_ref, keep_ref, cross_ref, planes, blocks) = arrived(refs[:5]), refs[5:]
-    collect(parts, planes)
-    transform_y(planes, cy_ref, blocks)
-    deal(blocks, keep_ref, cross_ref)
-
-
-def planes_y(parts, cy):
-    return pl.pallas_call(
-        planes_y_kernel,
-        out_shape=[group_shape(PART)] * 2,
-        scratch_shapes=[pltpu.VMEM((8, PLANE, 128), F32), pltpu.VMEM((8, PART, 128), F32)],
-        compiler_params=params(16),
-        cost_estimate=cost(10**9, 2 * 10**6),
-        name="planes_y",
-    )(*parts, cy)
-
-
-def back_y_kernel(*refs):
-    parts, (cy_ref, spread_ref, keep_ref, cross_ref, blocks, copies, planes) = arrived(refs[:5]), refs[5:]
-    collect(parts, blocks)
-    field = blocks[...].reshape(576, 128).astype(BF16)
-    for j in range(3):
-        copies[j] = dot(field, spread_ref[j])
-
-    def plane(s, carry):
-        totals = [jnp.zeros((72, 128), F32)] * 2
-        for d in range(8):
-            for j in range(3):
-                rows = copies[j, d * 72 : d * 72 + 72, :]
-                for half in range(2):
-                    totals[half] = totals[half] + rows * cy_ref[d, j, pl.ds(half * 8 + s, 1), :]
-        for half in range(2):
-            for slot in range(3):
-                at = slot * 48 + half * KS
-                planes[s, at : at + KS, :] = totals[half][slot * KS : slot * KS + KS]
-        return carry
-
-    lax.fori_loop(0, 8, plane, 0)
-    deal(planes, keep_ref, cross_ref)
-
-
-def back_y(parts, cy, spread):
-    return pl.pallas_call(
-        back_y_kernel,
-        out_shape=[group_shape(PLANE)] * 2,
-        scratch_shapes=[
-            pltpu.VMEM((8, PART, 128), F32),
-            pltpu.VMEM((3, 8 * PART, 128), F32),
-            pltpu.VMEM((8, PLANE, 128), F32),
-        ],
-        compiler_params=params(16),
-        cost_estimate=cost(10**9, 2 * 10**6),
-        name="back_y",
-    )(*parts, cy, spread)
-
-
-def back_x_kernel(*refs):
-    parts, (xl_ref, sent_ref, planes) = arrived(refs[:5]), refs[5:]
-    collect(parts, planes)
-    for slot in range(3):
-        rows = slice(slot * 48, slot * 48 + 48)
-        both = jnp.concatenate([planes[s, rows, :] for s in range(8)], axis=1).astype(BF16)
-        wide = dot(xl_ref[...], jnp.concatenate([both, both], axis=0))
-        for s in range(8):
-            sent_ref[:, s, slot] = wide[:, s * 128 : s * 128 + 128].reshape(16, 8, 128)
-
-
-def back_x(parts, xl_t):
-    return pl.pallas_call(
-        back_x_kernel,
-        out_shape=pltpu.HBM(SENT_SHAPE, F32),
-        out_specs=pl.BlockSpec(SENT_SHAPE, lambda: (0,) * 5),
-        scratch_shapes=[pltpu.VMEM((8, PLANE, 128), F32)],
-        compiler_params=params(16),
-        cost_estimate=cost(10**9, 2 * 10**6),
-        name="back_x",
-    )(*parts, xl_t)
+        name="planes",
+    )(got, k["xl"], *in_hbm(k["cy"]))
 
 
 def pair_up_kernel(keep_ref, cross_ref, *outs):
@@ -393,44 +403,41 @@
 
 def exchange_second(blocks):
     keep, cross = blocks
-    cross = lax.ppermute(cross, "gy", [(i, i ^ 1) for i in range(8)])
+    cross = across(cross, 1)
     pairs = pair_up(keep, cross)
-    far = [lax.ppermute(pairs[sx - 1], "gy", [(i, i ^ (2 * sx)) for i in range(8)]) for sx in range(1, 4)]
-    return [keep, cross] + far
+    return [keep, cross] + [across(pair, 2 * sx + 2) for sx, pair in enumerate(pairs)]
 
 
 def mode_grad_kernel(*refs):
-    parts, (spread_ref, weight_hbm, gather_hbm, keep_ref, cross_ref) = arrived(refs[:5]), refs[5:10]
+    parts, (spread_ref, weight_hbm, gather_hbm, out_ref, grads_ref) = arrived(refs[:5]), refs[5:10]
     products, weight_ref, gather_ref, sems = refs[10:]
     copies = []
     for ky in range(3):
-        copies.append(
-            (
-                pltpu.make_async_copy(weight_hbm.at[ky], weight_ref.at[ky], sems.at[0, ky]),
-                pltpu.make_async_copy(gather_hbm.at[ky], gather_ref.at[ky], sems.at[1, ky]),
-            )
-        )
-    for weight, gather in copies:
-        weight.start()
-        gather.start()
-    me = lax.axis_index("gy")
-    field = jnp.concatenate([part[...] for part in parts], axis=0).astype(BF16)
+        copies.append(pltpu.make_async_copy(weight_hbm.at[ky], weight_ref.at[ky], sems.at[ky]))
+    copies.append(pltpu.make_async_copy(gather_hbm, gather_ref, sems.at[3]))
+    for copy in copies:
+        copy.start()
+    collect(parts, grads_ref)
+    field = grads_ref[...].reshape(576, 128).astype(BF16)
+    lanes = [dot(field, spread_ref[ky]) for ky in range(3)]
     total = None
-    for ky in range(3):
-        lanes = dot(field, spread_ref[ky])
-        copies[ky][0].wait()
-        for s in range(8):
-            q = (me ^ s) & 3
-            for slot in range(3):
-                at = s * 72 + slot * KS
-                weight = weight_ref[ky, slot * 4 + q].astype(F32)
-                products[at : at + KS, :] = weight * jnp.concatenate([lanes[at : at + KS]] * 8, axis=1)
-        copies[ky][1].wait()
-        term = dot(products[...].astype(BF16), gather_ref[ky])
+    for j in range(4):
+        if j < 3:
+            copies[j].wait()
+        for b in range(2):
+            for t in range(3):
+                ky, q = mode_of(j, t)
+                for slot in range(3):
+                    at = (3 * b + t) * 72 + slot * KS
+                    source = (4 * b + q) * 72 + slot * KS
+                    weight = weight_ref[ky, slot * 4 + q].astype(F32)
+                    copy = lanes[ky][source : source + KS]
+                    products[at : at + KS, :] = weight * jnp.concatenate([copy] * 8, axis=1)
+        if j == 0:
+            copies[3].wait()
+        term = dot(products[...].astype(BF16), gather_ref[j])
         total = term if total is None else total + term
-    for sx in range(4):
-        keep_ref[sx] = total[2 * sx * 72 : 2 * sx * 72 + 72]
-        cross_ref[sx] = total[(2 * sx + 1) * 72 : (2 * sx + 1) * 72 + 72]
+    out_ref[...] = total.reshape(TILES)
 
 
 def mode_grad(parts, weights, k):
@@ -438,12 +445,12 @@
     return pl.pallas_call(
         mode_grad_kernel,
         in_specs=[vmem] * 6 + [ANY] * 2,
-        out_shape=[group_shape(PART)] * 2,
+        out_shape=[jax.ShapeDtypeStruct(TILES, F32), jax.ShapeDtypeStruct((8, 72, 128), F32)],
         scratch_shapes=[
-            pltpu.VMEM((576, C * C), F32),
+            pltpu.VMEM((432, C * C), F32),
             pltpu.VMEM(weights.shape, BF16),
-            pltpu.VMEM((3, C * C, 128), BF16),
-            pltpu.SemaphoreType.DMA((2, 3)),
+            pltpu.VMEM((4, C * C, 128), BF16),
+            pltpu.SemaphoreType.DMA((4,)),
         ],
         compiler_params=params(16),
         cost_estimate=cost(10**9, 4 * 10**6),
@@ -451,41 +458,92 @@
     )(*parts, k["spread"], *in_hbm(weights, k["gather"]))
 
 
-def spectral_grad_kernel(*refs):
-    grads, fields, (spread_ref, wide_ref, out_ref) = arrived(refs[:5]), arrived(refs[5:10]), refs[10:]
+def backward_kernel(*refs):
+    parts, (xl_ref, yb_hbm, sent_ref, yb_ref, blocks, sem) = refs[:8], refs[8:]
     me = lax.axis_index("gy")
-    grad = jnp.concatenate([part[...] for part in grads], axis=0).astype(BF16)
-    field = jnp.concatenate([part[...] for part in fields], axis=0).astype(BF16)
-    copies = dot(grad, spread_ref[0])
-    wide = dot(field, wide_ref[0])
-    for s in range(4):
-        q = (me ^ s) & 3
+    copy = pltpu.make_async_copy(yb_hbm.at[me], yb_ref, sem)
+    copy.start()
+    for s in range(8):
+        blocks[me ^ s] = parts[s][...]
+    group = lane_group(72)
+    columns = []
+    for s in range(8):
+        tiles = []
+        for b in range(2):
+            three = [blocks[s, 3 * b + t] for t in range(3)]
+            last = pltpu.roll(three[0], 32, 1)
+            for t in range(1, 3):
+                last = jnp.where(group == t, pltpu.roll(three[t], 32 + 32 * t, 1), last)
+            tiles += three + [last]
+        columns.append(jnp.concatenate(tiles, axis=0).astype(BF16))
+    copy.wait()
+    wide = dot_t(jnp.concatenate(columns, axis=1), yb_ref[...]).astype(BF16)
+    for slot in range(3):
+        both = []
+        for d in range(8):
+            rows = wide[d * 72 + slot * KS : d * 72 + slot * KS + KS]
+            both.append(jnp.concatenate([rows[:, :128], rows[:, 128:]], axis=0))
+        both = jnp.concatenate(both, axis=1)
+        out = dot(xl_ref[...], jnp.concatenate([both, both], axis=0))
+        for d in range(8):
+            sent_ref[:, d, slot] = out[:, d * 128 : d * 128 + 128].reshape(16, 8, 128)
+
+
+def backward(parts, k):
+    vmem = pl.BlockSpec(memory_space=pltpu.VMEM)
+    return pl.pallas_call(
+        backward_kernel,
+        in_specs=[vmem] * 9 + [ANY],
+        out_shape=pltpu.HBM(SENT_SHAPE, F32),
+        out_specs=pl.BlockSpec(SENT_SHAPE, lambda: (0,) * 5),
+        scratch_shapes=[
+            pltpu.VMEM((256, 1024), BF16),
+            pltpu.VMEM((8, *TILES), F32),
+            pltpu.SemaphoreType.DMA,
+        ],
+        compiler_params=params(16),
+        cost_estimate=cost(10**9, 4 * 10**6),
+        name="backward",
+    )(*parts, k["xl_t"], *in_hbm(k["yb"]))
+
+
+def spectral_grad_kernel(grads_ref, *refs):
+    fields, (spread_ref, wide_ref, out_ref) = refs[:4], refs[4:]
+    ky = pl.program_id(0)
+
+    def tile(t):
+        value = fields[0][t] + fields[1][t] + fields[2][t] + fields[3][t]
+        return value.astype(BF16)
+
+    copies = dot(grads_ref[...].reshape(576, 128).astype(BF16), spread_ref[ky])
+    for q in range(4):
+        j, t = (ky, q) if q < 3 else (3, ky)
+        field = jnp.concatenate([tile(t), tile(3 + t)], axis=0)
+        wide = dot(field, wide_ref[j])
         for slot in range(3):
             total = None
-            for at in (s * 72 + slot * KS, (s + 4) * 72 + slot * KS):
-                term = wide[at : at + KS] * jnp.concatenate([copies[at : at + KS]] * 8, axis=1)
+            for b in range(2):
+                at = b * 72 + slot * KS
+                source = (4 * b + q) * 72 + slot * KS
+                copy = copies[source : source + KS]
+                term = wide[at : at + KS] * jnp.concatenate([copy] * 8, axis=1)
                 total = term if total is None else total + term
             out_ref[0, slot * 4 + q] = total
 
 
-def spectral_grad(grads, fields, spread, wide):
+def spectral_grad(grads, fields, k):
     return pl.pallas_call(
         spectral_grad_kernel,
         grid=(3,),
-        in_specs=[whole((4, PART, 128))] * 2
-        + [whole((2, PART, 128))] * 3
-        + [whole((4, PART, 128))] * 2
-        + [whole((2, PART, 128))] * 3
-        + [
-            pl.BlockSpec((1, 128, 128), lambda i: (i, 0, 0)),
-            pl.BlockSpec((1, 128, C * C), lambda i: (i, 0, 0)),
-        ],
+        in_specs=[whole((8, 72, 128))]
+        + [whole(TILES)] * 4
+        + [whole((4, 128, 128)), whole((4, 128, C * C))],
         out_specs=pl.BlockSpec((1, 12, KS, C * C), lambda i: (i, 0, 0, 0)),
         out_shape=pltpu.HBM((3, 12, KS, C * C), F32),
         compiler_params=params(24),
         cost_estimate=cost(10**9, 4 * 10**6),
         name="spectral_grad",
-    )(*grads, *fields, *in_hbm(spread, wide))
+    )(grads, *fields, *in_hbm(k["spread"], k["wide"]))
 
 
 def synthesise_kernel(got_ref, grad_ref, table_ref, zl_ref, mix_ref, out_ref, parts):
@@ -547,18 +605,19 @@
 
 def body(inputs, cotangent, pre_activation, pointwise, spectral):
     k = constants()
-    xl, cy, spread = k["xl"], k["cy"], k["spread"]
     weights = jnp.transpose(spectral, (1, 2, 0, 3))
     mix = jnp.kron(jnp.eye(8, dtype=BF16), pointwise.T)
     sent, grad_pre = analyse_grad(cotangent, pre_activation, k)
     got = exchange_all(sent)
-    got_input = exchange_first(analyse_input(inputs, k))
-    grads = exchange_second(planes_forward(got, xl, cy))
-    modes = exchange_second(mode_grad(grads, weights, k))
-    back = exchange_first(back_x(exchange_second(back_y(modes, cy, spread)), k["xl_t"]))
-    planes = exchange_second(planes_x(got_input, xl))
-    fields = exchange_second(planes_y(planes, cy))
-    weight_grad = spectral_grad(grads, fields, spread, k["wide"])
+    sent_input = analyse_input(inputs, k)
+    got, *_ = lax.optimization_barrier((got, sent_input, mix))
+    got_input = exchange_first(sent_input)
+    modes, grads = mode_grad(exchange_second(planes(got, k)), weights, k)
+    parts = gather_second(modes)
+    got_input, *_ = lax.optimization_barrier((got_input, modes))
+    sums = reduce_cores(forward(got_input, k))
+    back = exchange_first(backward(parts, k))
+    weight_grad = spectral_grad(grads, reduce_chips(sums), k)
     return synthesise(back, grad_pre, mix, k), jnp.transpose(weight_grad, (2, 0, 1, 3))
 
 

time: 144 us -> 133 us (0.924)
  starting transfers between devices: 47.6 us -> 37.5 us
  waiting for transfers between devices: 49.2 us -> 45.1 us
    ppermute x20 -> x15, starting transfers between devices: 24.4 us -> 14.4 us  [across(): return lax.ppermute(block, 'gy', [(i, i ^ sx) for i in range(8)])]
    ppermute x20 -> x15, waiting for transfers between devices: 32.9 us -> 28.8 us  [across(): return lax.ppermute(block, 'gy', [(i, i ^ sx) for i in range(8)])]
    pallas_call x6 -> x5, Pallas kernels: 12.3 us -> 13.6 us  [the longest x1 4.34 us: spectral_grad(): pl.pallas_call(spectral_grad_kernel, grid=(3,), in_specs=[whole((8, 72, 1...]
  transfers between devices with their start and end apart: 23 -> 18, of which waited for: 20 -> 14; matrix products, arithmetic and copies ran while one was open for 1% -> 2% of each run, Pallas kernels for 17% -> 19%
where the time goes in v3:
time: 133 us; the launch traced here: 132 us
  waiting for transfers between devices  45.1 us (34%)
  Pallas kernels  44.9 us (34%)
  starting transfers between devices  37.5 us (28%)
  local copies, waits for them, and re-layouts  3.09 us (2%)
    ppermute x15, waiting for transfers between devices, across(): return lax.ppermute(block, 'gy', [(i, i ^ sx) for i in range(8)])  28.8 us
    all_to_all x1, waiting for transfers between devices, exchange_all(): lax.all_to_all(flat, ('gx', 'gy'), 0, 0, tiled=True).reshape(block.shape)  16.3 us
    ppermute x15, starting transfers between devices, across(): return lax.ppermute(block, 'gy', [(i, i ^ sx) for i in range(8)])  14.4 us
    all_to_all x2, starting transfers between devices, exchange_first(): return lax.all_to_all(flat, 'gx', 0, 0, tiled=True).reshape(block.shape)  12.7 us
    pallas_call x1, Pallas kernels, analyse_grad(): pl.pallas_call(analyse_grad_kernel, grid=(2, 2), in_specs=[FIELD, FIELD,...  11.8 us
    all_to_all x1, starting transfers between devices, exchange_all(): lax.all_to_all(flat, ('gx', 'gy'), 0, 0, tiled=True).reshape(block.shape)  10.4 us
    pallas_call x1, Pallas kernels, synthesise(): pl.pallas_call(synthesise_kernel, grid=(2, 2), in_specs=[SENT, FIELD, TAB...  7.96 us
    pallas_call x1, Pallas kernels, analyse_input(): pl.pallas_call(analyse_input_kernel, grid=(2, 2), in_specs=[FIELD, TABLE,...  7.6 us
  transfers between devices with their start and end apart: 18, of which 14 were waited for; matrix products, arithmetic and copies ran while one was open for 2% of the time, Pallas kernels for 19%

profile of v3, /device:TPU:8, one launch (start us, length us, event | category | flops | bytes accessed | tf_op | source)
XLA Modules:
  0.0 132.3 jit_solution(2398486408792849691)
XLA Ops:
  0.6 11.8 %analyse_grad.1 = (f32[16,8,3,8,128]{4,3,2,1,0:T(8,128)}, bf16[2,4,8,64,512]{4,3,2,1,0:T(8,128)(2,1)}) custom-call(bf16[2,4,8,64,512]{4,3,2,1,0:T(8,128)(2,1)} %cot_ref.1, bf16[2,4,8,64,512]{4,3,2,1,0:T(8,128)(2,1)} %pre_ref.1, bf16[4,512,256]{2,1,0:T(8,128)(2,1)} %constant.22.clone.table_ref, bf16[192,512]{1,0:T(8,128)(2,1)} %constant.23.clone.zl_ref), custom_call_target="tpu_custom_call" | custom-call | flops 4000000000 | bytes 14000000 | tf_op jit(solution)/shard_map/analyse_grad/pallas_call | solution.py:186
  12.4 10.4 %all-to-all-start = ((f32[128,24,128]{2,1,0:T(8,128)}), f32[128,24,128]{2,1,0:T(8,128)S(1)}, u32[]{:S(2)}, u32[]{:S(2)}) async-start(f32[128,24,128]{2,1,0:T(8,128)} %bitcast.17), calls=%async_computation | async-start | bytes 3145728 | tf_op jit(solution)/shard_map/all_to_all | solution.py:598
  22.9 7.6 %analyse_input.1 = f32[16,8,3,8,128]{4,3,2,1,0:T(8,128)} custom-call(bf16[2,4,8,64,512]{4,3,2,1,0:T(8,128)(2,1)} %field_ref.1, bf16[4,512,256]{2,1,0:T(8,128)(2,1)} %constant.22.clone.table_ref, bf16[192,512]{1,0:T(8,128)(2,1)} %constant.23.clone.zl_ref), custom_call_target="tpu_custom_call" | custom-call | flops 4000000000 | bytes 6000000 | tf_op jit(solution)/shard_map/analyse_input/pallas_call | solution.py:204
  30.5 16.3 %all-to-all-done = f32[128,24,128]{2,1,0:T(8,128)S(1)} async-done(((f32[128,24,128]{2,1,0:T(8,128)}), f32[128,24,128]{2,1,0:T(8,128)S(1)}, u32[]{:S(2)}, u32[]{:S(2)}) %all-to-all-start) | async-done | bytes 1572896 | tf_op jit(solution)/shard_map/all_to_all | solution.py:598
  46.8 5.4 %all-to-all-start.2 = ((f32[16,192,128]{2,1,0:T(8,128)}), f32[16,192,128]{2,1,0:T(8,128)S(1)}, u32[]{:S(2)}, u32[]{:S(2)}) async-start(f32[16,192,128]{2,1,0:T(8,128)} %bitcast.16), calls=%async_computation.2 | async-start | bytes 3145728 | tf_op jit(solution)/shard_map/all_to_all | solution.py:603
  53.2 2.1 %mul.27.mix_ref = bf16[256,256]{1,0:T(8,128)(2,1)} reshape(bf16[8,32,8,32]{3,2,1,0:T(8,128)(2,1)} %broadcast_multiply_fusion) | data formatting | bytes 262144 | tf_op jit(solution)/shard_map/jit(kron)/mul | solution.py:609
  55.3 3.3 %planes.1 = (f32[4,72,128]{2,1,0:T(8,128)S(1)}, f32[4,72,128]{2,1,0:T(8,128)S(1)}) custom-call(f32[16,8,3,8,128]{4,3,2,1,0:T(8,128)S(1)} %bitcast.13, bf16[48,256]{1,0:T(8,128)(2,1)S(1)} %copy-done.2, f32[8,3,16,128]{3,2,1,0:T(8,128)} %constant.24.clone.cy_hbm), custom_call_target="tpu_custom_call" | custom-call | flops 1000000000 | bytes 3000000 | tf_op jit(solution)/shard_map/planes/pallas_call | solution.py:371
  60.8 1.6 %collective-permute-start.2 = (f32[2,72,128]{2,1,0:T(8,128)S(1)}, f32[2,72,128]{2,1,0:T(8,128)S(1)}, u32[]{:S(2)}, u32[]{:S(2)}) collective-permute-start(f32[2,72,128]{2,1,0:T(8,128)S(1)} %get-tuple-element.24), channel_id=1, source_target_pairs={{0,4},{1,5},{2,6},{3,7},{4,0},{5,1},{6,2},{7,3},{8,12},{9,13},{10,... | collective-permute-start | bytes 221192 | tf_op jit(solution)/shard_map/ppermute | solution.py:285
  62.4 2.5 %collective-permute-start.3 = (f32[2,72,128]{2,1,0:T(8,128)S(1)}, f32[2,72,128]{2,1,0:T(8,128)S(1)}, u32[]{:S(2)}, u32[]{:S(2)}) collective-permute-start(f32[2,72,128]{2,1,0:T(8,128)S(1)} %get-tuple-element.25), channel_id=1, source_target_pairs={{0,6},{1,7},{2,4},{3,5},{4,2},{5,3},{6,0},{7,1},{8,14},{9,15},{10,... | collective-permute-start | bytes 221192 | tf_op jit(solution)/shard_map/ppermute | solution.py:285
  65.3 1.4 %collective-permute-done.2.refs_3_ = f32[2,72,128]{2,1,0:T(8,128)S(1)} collective-permute-done((f32[2,72,128]{2,1,0:T(8,128)S(1)}, f32[2,72,128]{2,1,0:T(8,128)S(1)}, u32[]{:S(2)}, u32[]{:S(2)}) %collective-permute-start.2) | collective-permute-done | bytes 73760 | tf_op jit(solution)/shard_map/ppermute | solution.py:285
  69.0 4.0 %mode_grad.1 = (f32[6,72,128]{2,1,0:T(8,128)S(1)}, f32[8,72,128]{2,1,0:T(8,128)S(1)}) custom-call(f32[4,72,128]{2,1,0:T(8,128)S(1)} %get-tuple-element.21.keep_ref.refs_0_, f32[4,72,128]{2,1,0:T(8,128)S(1)} %collective-permute-done.cross_ref.refs_1_, f32[2,72,128]{2,1,0:T(8,128)S(1)} %collective-permute-done.1.refs_2_, ...), custom_call_target="tpu_custom_call" | custom-call | flops 1000000000 | bytes 4000000 | tf_op jit(solution)/shard_map/mode_grad/pallas_call | solution.py:445
  73.0 2.4 %collective-permute-start.9 = (f32[6,72,128]{2,1,0:T(8,128)S(1)}, f32[6,72,128]{2,1,0:T(8,128)S(1)}, u32[]{:S(2)}, u32[]{:S(2)}) collective-permute-start(f32[6,72,128]{2,1,0:T(8,128)S(1)} %get-tuple-element.26.refs_0_), channel_id=1, source_target_pairs={{0,6},{1,7},{2,4},{3,5},{4,2},{5,3},{6,0},{7,1},{8,14},{9,15},{10,... | collective-permute-start | bytes 663560 | tf_op jit(solution)/shard_map/ppermute | solution.py:285
  75.4 1.8 %collective-permute-start.5 = (f32[6,72,128]{2,1,0:T(8,128)S(1)}, f32[6,72,128]{2,1,0:T(8,128)S(1)}, u32[]{:S(2)}, u32[]{:S(2)}) collective-permute-start(f32[6,72,128]{2,1,0:T(8,128)S(1)} %get-tuple-element.26.refs_0_), channel_id=1, source_target_pairs={{0,2},{1,3},{2,0},{3,1},{4,6},{5,7},{6,4},{7,5},{8,10},{9,11},{10,... | collective-permute-start | bytes 663560 | tf_op jit(solution)/shard_map/ppermute | solution.py:285
  77.2 8.7 %collective-permute-done.9.refs_6_ = f32[6,72,128]{2,1,0:T(8,128)S(1)} collective-permute-done((f32[6,72,128]{2,1,0:T(8,128)S(1)}, f32[6,72,128]{2,1,0:T(8,128)S(1)}, u32[]{:S(2)}, u32[]{:S(2)}) %collective-permute-start.9) | collective-permute-done | bytes 221216 | tf_op jit(solution)/shard_map/ppermute | solution.py:285
  88.0 3.5 %backward.1 = f32[16,8,3,8,128]{4,3,2,1,0:T(8,128)} custom-call(f32[6,72,128]{2,1,0:T(8,128)S(1)} %get-tuple-element.26.refs_0_, f32[6,72,128]{2,1,0:T(8,128)S(1)} %collective-permute-done.4.refs_1_, f32[6,72,128]{2,1,0:T(8,128)S(1)} %collective-permute-done.5.refs_2_, f32[6,72,128]{2,1,0:T(8,128)S(1)} %collective-permute-done.6.refs_3_, ...), custom_call_target="tpu_custom_call" | custom-call | flops 1000000000 | bytes 4000000 | tf_op jit(solution)/shard_map/backward/pallas_call | solution.py:494
  91.5 7.2 %all-to-all-start.1 = ((f32[16,192,128]{2,1,0:T(8,128)}), f32[16,192,128]{2,1,0:T(8,128)S(1)}, u32[]{:S(2)}, u32[]{:S(2)}) async-start(f32[16,192,128]{2,1,0:T(8,128)} %bitcast.14), calls=%async_computation.1 | async-start | bytes 3145728 | tf_op jit(solution)/shard_map/all_to_all | solution.py:603
  98.7 2.3 %forward.1 = (f32[4,6,72,128]{3,2,1,0:T(8,128)S(1)}, f32[4,6,72,128]{3,2,1,0:T(8,128)S(1)}) custom-call(f32[16,8,3,8,128]{4,3,2,1,0:T(8,128)S(1)} %bitcast.11, bf16[48,256]{1,0:T(8,128)(2,1)S(1)} %copy-done.2, bf16[8,256,1024]{2,1,0:T(8,128)(2,1)} %constant.28.clone.refs_9_.yb_hbm), custom_call_target="tpu_custom_call" | custom-call | flops 1000000000 | bytes 4000000 | tf_op jit(solution)/shard_map/forward/pallas_call | solution.py:253
  101.1 2.4 %collective-permute-done.11.cross_ref = f32[4,6,72,128]{3,2,1,0:T(8,128)S(1)} collective-permute-done((f32[4,6,72,128]{3,2,1,0:T(8,128)S(1)}, f32[4,6,72,128]{3,2,1,0:T(8,128)S(1)}, u32[]{:S(2)}, u32[]{:S(2)}) %collective-permute-start.11) | collective-permute-done | bytes 884768 | tf_op jit(solution)/shard_map/ppermute | solution.py:285
  103.9 3.3 %collective-permute-start.13 = (f32[6,72,128]{2,1,0:T(8,128)S(1)}, f32[6,72,128]{2,1,0:T(8,128)S(1)}, u32[]{:S(2)}, u32[]{:S(2)}) collective-permute-start(f32[6,72,128]{2,1,0:T(8,128)S(1)} %get-tuple-element.34), channel_id=1, source_target_pairs={{0,4},{1,5},{2,6},{3,7},{4,0},{5,1},{6,2},{7,3},{8,12},{9,13},{10,... | collective-permute-start | bytes 663560 | tf_op jit(solution)/shard_map/ppermute | solution.py:285
  108.4 3.6 %collective-permute-done.12.refs_1_ = f32[6,72,128]{2,1,0:T(8,128)S(1)} collective-permute-done((f32[6,72,128]{2,1,0:T(8,128)S(1)}, f32[6,72,128]{2,1,0:T(8,128)S(1)}, u32[]{:S(2)}, u32[]{:S(2)}) %collective-permute-start.12) | collective-permute-done | bytes 221216 | tf_op jit(solution)/shard_map/ppermute | solution.py:285
  112.0 5.4 %collective-permute-done.13.refs_2_ = f32[6,72,128]{2,1,0:T(8,128)S(1)} collective-permute-done((f32[6,72,128]{2,1,0:T(8,128)S(1)}, f32[6,72,128]{2,1,0:T(8,128)S(1)}, u32[]{:S(2)}, u32[]{:S(2)}) %collective-permute-start.13) | collective-permute-done | bytes 221216 | tf_op jit(solution)/shard_map/ppermute | solution.py:285
  117.4 2.6 %collective-permute-done.14.refs_3_ = f32[6,72,128]{2,1,0:T(8,128)S(1)} collective-permute-done((f32[6,72,128]{2,1,0:T(8,128)S(1)}, f32[6,72,128]{2,1,0:T(8,128)S(1)}, u32[]{:S(2)}, u32[]{:S(2)}) %collective-permute-start.14) | collective-permute-done | bytes 221216 | tf_op jit(solution)/shard_map/ppermute | solution.py:285
  120.0 4.3 %spectral_grad.1 = f32[3,12,24,1024]{3,2,1,0:T(8,128)} custom-call(f32[8,72,128]{2,1,0:T(8,128)S(1)} %get-tuple-element.28.grads_ref, f32[6,72,128]{2,1,0:T(8,128)S(1)} %get-tuple-element.32.refs_0_, f32[6,72,128]{2,1,0:T(8,128)S(1)} %collective-permute-done.12.refs_1_, f32[6,72,128]{2,1,0:T(8,128)S(1)} %collective-permute-done.13.refs_2_, ...), custom_call_target="tpu_custom_call" | custom-call | flops 1000000000 | bytes 4000000 | tf_op jit(solution)/shard_map/spectral_grad/pallas_call | solution.py:535
  124.4 8.0 %synthesise.1 = bf16[2,4,8,64,512]{4,3,2,1,0:T(8,128)(2,1)} custom-call(f32[16,8,3,8,128]{4,3,2,1,0:T(8,128)S(1)} %bitcast.12, bf16[2,4,8,64,512]{4,3,2,1,0:T(8,128)(2,1)} %get-tuple-element.27.grad_ref, bf16[4,256,512]{2,1,0:T(8,128)(2,1)} %constant.31.clone.table_ref, bf16[512,256]{1,0:T(8,128)(2,1)} %constant.32.clone.zl_ref, bf16[256,256]{1,0:T(8,128)(2,1)} %mul.27.mix_ref), custom_call_target="tpu_custom_call" | custom-call | flops 4000000000 | bytes 10000000 | tf_op jit(solution)/shard_map/synthesise/pallas_call | solution.py:583
  (34 shorter events, 9.7 us)
Async XLA Ops:
  12.4 34.4 %all-to-all-start = ((f32[128,24,128]{2,1,0:T(8,128)}), f32[128,24,128]{2,1,0:T(8,128)S(1)}, u32[]{:S(2)}, u32[]{:S(2)}) async-start(f32[128,24,128]{2,1,0:T(8,128)} %bitcast.17), calls=%async_computation | async-start | bytes 3145728 | tf_op jit(solution)/shard_map/all_to_all | solution.py:598
  22.9 29.3 %copy-start.3 = (bf16[32,32]{1,0:T(8,128)(2,1)S(1)}, bf16[32,32]{1,0:T(8,128)(2,1)}, u32[]{:S(2)}) copy-start(bf16[32,32]{1,0:T(8,128)(2,1)} %param.19) | copy-start | bytes 6148
  30.5 24.8 %copy-start.2 = (bf16[48,256]{1,0:T(8,128)(2,1)S(1)}, bf16[48,256]{1,0:T(8,128)(2,1)}, u32[]{:S(2)}) copy-start(bf16[48,256]{1,0:T(8,128)(2,1)} %constant.25.clone.xl_ref) | copy-start | bytes 73732
  46.8 44.7 %all-to-all-start.2 = ((f32[16,192,128]{2,1,0:T(8,128)}), f32[16,192,128]{2,1,0:T(8,128)S(1)}, u32[]{:S(2)}, u32[]{:S(2)}) async-start(f32[16,192,128]{2,1,0:T(8,128)} %bitcast.16), calls=%async_computation.2 | async-start | bytes 3145728 | tf_op jit(solution)/shard_map/all_to_all | solution.py:603
  55.3 32.7 %copy-start.1 = (bf16[128,96]{1,0:T(8,128)(2,1)S(1)}, bf16[128,96]{1,0:T(8,128)(2,1)}, u32[]{:S(2)}) copy-start(bf16[128,96]{1,0:T(8,128)(2,1)} %constant.29.clone.refs_8_) | copy-start | bytes 73732
  58.6 1.5 %collective-permute-start = (f32[4,72,128]{2,1,0:T(8,128)S(1)}, f32[4,72,128]{2,1,0:T(8,128)S(1)}, u32[]{:S(2)}, u32[]{:S(2)}) collective-permute-start(f32[4,72,128]{2,1,0:T(8,128)S(1)} %get-tuple-element.22), channel_id=1, source_target_pairs={{0,1},{1,0},{2,3},{3,2},{4,5},{5,4},{6,7},{7,6},{8,9},{9,8},{10,11... | collective-permute-start | bytes 442376 | tf_op jit(solution)/shard_map/ppermute | solution.py:285
  60.1 5.2 %collective-permute-start.1 = (f32[2,72,128]{2,1,0:T(8,128)S(1)}, f32[2,72,128]{2,1,0:T(8,128)S(1)}, u32[]{:S(2)}, u32[]{:S(2)}) collective-permute-start(f32[2,72,128]{2,1,0:T(8,128)S(1)} %get-tuple-element.23), channel_id=1, source_target_pairs={{0,2},{1,3},{2,0},{3,1},{4,6},{5,7},{6,4},{7,5},{8,10},{9,11},{10,... | collective-permute-start | bytes 221192 | tf_op jit(solution)/shard_map/ppermute | solution.py:285
  60.8 6.0 %collective-permute-start.2 = (f32[2,72,128]{2,1,0:T(8,128)S(1)}, f32[2,72,128]{2,1,0:T(8,128)S(1)}, u32[]{:S(2)}, u32[]{:S(2)}) collective-permute-start(f32[2,72,128]{2,1,0:T(8,128)S(1)} %get-tuple-element.24), channel_id=1, source_target_pairs={{0,4},{1,5},{2,6},{3,7},{4,0},{5,1},{6,2},{7,3},{8,12},{9,13},{10,... | collective-permute-start | bytes 221192 | tf_op jit(solution)/shard_map/ppermute | solution.py:285
  62.4 5.8 %collective-permute-start.3 = (f32[2,72,128]{2,1,0:T(8,128)S(1)}, f32[2,72,128]{2,1,0:T(8,128)S(1)}, u32[]{:S(2)}, u32[]{:S(2)}) collective-permute-start(f32[2,72,128]{2,1,0:T(8,128)S(1)} %get-tuple-element.25), channel_id=1, source_target_pairs={{0,6},{1,7},{2,4},{3,5},{4,2},{5,3},{6,0},{7,1},{8,14},{9,15},{10,... | collective-permute-start | bytes 221192 | tf_op jit(solution)/shard_map/ppermute | solution.py:285
  68.1 0.9 copy-start
  73.0 12.8 %collective-permute-start.9 = (f32[6,72,128]{2,1,0:T(8,128)S(1)}, f32[6,72,128]{2,1,0:T(8,128)S(1)}, u32[]{:S(2)}, u32[]{:S(2)}) collective-permute-start(f32[6,72,128]{2,1,0:T(8,128)S(1)} %get-tuple-element.26.refs_0_), channel_id=1, source_target_pairs={{0,6},{1,7},{2,4},{3,5},{4,2},{5,3},{6,0},{7,1},{8,14},{9,15},{10,... | collective-permute-start | bytes 663560 | tf_op jit(solution)/shard_map/ppermute | solution.py:285
  75.4 10.4 %collective-permute-start.7 = (f32[6,72,128]{2,1,0:T(8,128)S(1)}, f32[6,72,128]{2,1,0:T(8,128)S(1)}, u32[]{:S(2)}, u32[]{:S(2)}) collective-permute-start(f32[6,72,128]{2,1,0:T(8,128)S(1)} %get-tuple-element.26.refs_0_), channel_id=1, source_target_pairs={{0,4},{1,5},{2,6},{3,7},{4,0},{5,1},{6,2},{7,3},{8,12},{9,13},{10,... | collective-permute-start | bytes 663560 | tf_op jit(solution)/shard_map/ppermute | solution.py:285
  75.4 11.1 %collective-permute-start.5 = (f32[6,72,128]{2,1,0:T(8,128)S(1)}, f32[6,72,128]{2,1,0:T(8,128)S(1)}, u32[]{:S(2)}, u32[]{:S(2)}) collective-permute-start(f32[6,72,128]{2,1,0:T(8,128)S(1)} %get-tuple-element.26.refs_0_), channel_id=1, source_target_pairs={{0,2},{1,3},{2,0},{3,1},{4,6},{5,7},{6,4},{7,5},{8,10},{9,11},{10,... | collective-permute-start | bytes 663560 | tf_op jit(solution)/shard_map/ppermute | solution.py:285
  77.2 9.3 %collective-permute-start.4 = (f32[6,72,128]{2,1,0:T(8,128)S(1)}, f32[6,72,128]{2,1,0:T(8,128)S(1)}, u32[]{:S(2)}, u32[]{:S(2)}) collective-permute-start(f32[6,72,128]{2,1,0:T(8,128)S(1)} %get-tuple-element.26.refs_0_), channel_id=1, source_target_pairs={{0,1},{1,0},{2,3},{3,2},{4,5},{5,4},{6,7},{7,6},{8,9},{9,8},{10,11... | collective-permute-start | bytes 663560 | tf_op jit(solution)/shard_map/ppermute | solution.py:285
  85.8 1.5 %collective-permute-start.10 = (f32[6,72,128]{2,1,0:T(8,128)S(1)}, f32[6,72,128]{2,1,0:T(8,128)S(1)}, u32[]{:S(2)}, u32[]{:S(2)}) collective-permute-start(f32[6,72,128]{2,1,0:T(8,128)S(1)} %collective-permute-done.9.refs_6_), channel_id=1, source_target_pairs={{0,1},{1,0},{2,3},{3,2},{4,5},{5,4},{6,7},{7,6},{8,9},{9,8},{10,11... | collective-permute-start | bytes 663560 | tf_op jit(solution)/shard_map/ppermute | solution.py:285
  85.9 1.8 %collective-permute-start.8 = (f32[6,72,128]{2,1,0:T(8,128)S(1)}, f32[6,72,128]{2,1,0:T(8,128)S(1)}, u32[]{:S(2)}, u32[]{:S(2)}) collective-permute-start(f32[6,72,128]{2,1,0:T(8,128)S(1)} %collective-permute-done.7.refs_4_), channel_id=1, source_target_pairs={{0,1},{1,0},{2,3},{3,2},{4,5},{5,4},{6,7},{7,6},{8,9},{9,8},{10,11... | collective-permute-start | bytes 663560 | tf_op jit(solution)/shard_map/ppermute | solution.py:285
  86.5 1.5 %collective-permute-start.6 = (f32[6,72,128]{2,1,0:T(8,128)S(1)}, f32[6,72,128]{2,1,0:T(8,128)S(1)}, u32[]{:S(2)}, u32[]{:S(2)}) collective-permute-start(f32[6,72,128]{2,1,0:T(8,128)S(1)} %collective-permute-done.5.refs_2_), channel_id=1, source_target_pairs={{0,1},{1,0},{2,3},{3,2},{4,5},{5,4},{6,7},{7,6},{8,9},{9,8},{10,11... | collective-permute-start | bytes 663560 | tf_op jit(solution)/shard_map/ppermute | solution.py:285
  91.5 32.9 %all-to-all-start.1 = ((f32[16,192,128]{2,1,0:T(8,128)}), f32[16,192,128]{2,1,0:T(8,128)S(1)}, u32[]{:S(2)}, u32[]{:S(2)}) async-start(f32[16,192,128]{2,1,0:T(8,128)} %bitcast.14), calls=%async_computation.1 | async-start | bytes 3145728 | tf_op jit(solution)/shard_map/all_to_all | solution.py:603
  101.1 2.5 %collective-permute-start.11 = (f32[4,6,72,128]{3,2,1,0:T(8,128)S(1)}, f32[4,6,72,128]{3,2,1,0:T(8,128)S(1)}, u32[]{:S(2)}, u32[]{:S(2)}) collective-permute-start(f32[4,6,72,128]{3,2,1,0:T(8,128)S(1)} %get-tuple-element.31), channel_id=1, source_target_pairs={{0,1},{1,0},{2,3},{3,2},{4,5},{5,4},{6,7},{7,6},{8,9},{9,8},{10,11... | collective-permute-start | bytes 2654216 | tf_op jit(solution)/shard_map/ppermute | solution.py:285
  103.7 8.3 %collective-permute-start.12 = (f32[6,72,128]{2,1,0:T(8,128)S(1)}, f32[6,72,128]{2,1,0:T(8,128)S(1)}, u32[]{:S(2)}, u32[]{:S(2)}) collective-permute-start(f32[6,72,128]{2,1,0:T(8,128)S(1)} %get-tuple-element.33), channel_id=1, source_target_pairs={{0,2},{1,3},{2,0},{3,1},{4,6},{5,7},{6,4},{7,5},{8,10},{9,11},{10,... | collective-permute-start | bytes 663560 | tf_op jit(solution)/shard_map/ppermute | solution.py:285
  103.9 13.5 %collective-permute-start.13 = (f32[6,72,128]{2,1,0:T(8,128)S(1)}, f32[6,72,128]{2,1,0:T(8,128)S(1)}, u32[]{:S(2)}, u32[]{:S(2)}) collective-permute-start(f32[6,72,128]{2,1,0:T(8,128)S(1)} %get-tuple-element.34), channel_id=1, source_target_pairs={{0,4},{1,5},{2,6},{3,7},{4,0},{5,1},{6,2},{7,3},{8,12},{9,13},{10,... | collective-permute-start | bytes 663560 | tf_op jit(solution)/shard_map/ppermute | solution.py:285
  107.2 12.9 %collective-permute-start.14 = (f32[6,72,128]{2,1,0:T(8,128)S(1)}, f32[6,72,128]{2,1,0:T(8,128)S(1)}, u32[]{:S(2)}, u32[]{:S(2)}) collective-permute-start(f32[6,72,128]{2,1,0:T(8,128)S(1)} %get-tuple-element.35), channel_id=1, source_target_pairs={{0,6},{1,7},{2,4},{3,5},{4,2},{5,3},{6,0},{7,1},{8,14},{9,15},{10,... | collective-permute-start | bytes 663560 | tf_op jit(solution)/shard_map/ppermute | solution.py:285

commit v4 on v3

--- a/solution.py
+++ b/solution.py
@@ -55,7 +55,7 @@
     out["tables_t"] = np.swapaxes(tables, 1, 2).copy().astype(BF)
     zl = np.einsum("zk,rs->krsz", third, eye_r).reshape(KS * 8, 8 * N)
     out["zl"] = zl.astype(BF)
-    out["zl_t"] = np.concatenate([zl.T, np.zeros((8 * N, 64), np.float32)], axis=1).astype(BF)
+    out["zl_t"] = zl.T.copy().astype(BF)
     high = basis.astype(BF).astype(np.float32)
     low = (basis - high).astype(BF).astype(np.float32)
     eye_h = np.eye(2, dtype=np.float32)
@@ -113,44 +113,48 @@
                 sent_ref[block, q, slot] = value[kz * 8 : kz * 8 + 8]
 
 
-def analyse_grad_kernel(cot_ref, pre_ref, table_ref, zl_ref, sent_ref, grad_ref, flat, timed, parts):
+def analyse_grad_kernel(cot_ref, pre_ref, table_ref, zl_ref, sent_ref, even, odd, parts):
     step = pl.program_id(1)
 
-    def time(n, carry):
-        timed[n] = dot(flat[n & 1], table_ref[n // 4]).astype(BF16)
-        return carry
-
-    def slope(n, carry):
-        pair, x = n // 4, n % 4
-        before = jnp.maximum(n - 1, 0)
-        earlier = dot(flat[(n + 1) & 1], table_ref[before // 4])
-        for y in range(2):
-            for j in range(4):
-                rows = pl.ds(j * 16, 16)
-                v = pre_ref[0, x, 2 * pair + y, rows, :].astype(F32)
-                g = cot_ref[0, x, 2 * pair + y, rows, :].astype(F32)
-                grad = (g * gelu_slope(v)).astype(BF16)
-                grad_ref[0, x, 2 * pair + y, rows, :] = grad
-                flat[n & 1, y * N + j * 16 : y * N + j * 16 + 16, :] = grad
-        timed[before] = earlier.astype(BF16)
-        return carry
-
-    lax.fori_loop(0, 8, slope, 0)
-    time(7, 0)
-    for pair in range(2):
-        parts[2 * step + pair] = dot(zl_ref[...], timed[4 * pair : 4 * pair + 4].reshape(8 * N, MT * C))
+    def cells(pair, flat):
+        for x in range(4):
+            for y in range(2):
+                for j in range(4):
+                    rows = slice(j * 16, j * 16 + 16)
+                    v = pre_ref[0, x, 2 * pair + y, rows, :].astype(F32)
+                    g = cot_ref[0, x, 2 * pair + y, rows, :].astype(F32)
+                    at = (2 * x + y) * N + j * 16
+                    flat[at : at + 16, :] = (g * gelu_slope(v)).astype(BF16)
+
+    def analyse(pair, flat):
+        sectioned = dot(zl_ref[...], flat[...]).astype(BF16)
+        parts[pair] = dot(sectioned, table_ref[pair])
+
+    analyse((2 * step + 3) % 4, odd)
+    cells(0, even)
+    analyse(2 * step, even)
+    cells(1, odd)
 
     @pl.when(step == 1)
     def _():
+        analyse(3, odd)
         send_parts(parts, sent_ref)
 
 
-def analyse_input_kernel(field_ref, table_ref, zl_ref, sent_ref, parts):
+def analyse_input_kernel(field_ref, table_ref, zl_ref, weight_ref, sent_ref, mix_ref, parts):
     step = pl.program_id(1)
+
+    @pl.when((step == 0) & (pl.program_id(0) == 0))
+    def _():
+        rows = lax.broadcasted_iota(jnp.int32, (256, C), 0) % C
+        copies = (rows == lax.broadcasted_iota(jnp.int32, (256, C), 1)).astype(BF16)
+        mixed = dot_t(dot_t(copies, weight_ref[...]).astype(BF16), copies)
+        blocks = [lax.broadcasted_iota(jnp.int32, (256, 256), axis) // C for axis in range(2)]
+        mix_ref[...] = jnp.where(blocks[0] == blocks[1], mixed, 0.0).astype(BF16)
     for pair in range(2):
         field = field_ref[0, :, 2 * pair : 2 * pair + 2].reshape(8 * N, NT * C)
-        timed = dot(field, table_ref[pair]).astype(BF16)
-        parts[2 * step + pair] = dot(zl_ref[...], timed)
+        sectioned = dot(zl_ref[...], field).astype(BF16)
+        parts[2 * step + pair] = dot(sectioned, table_ref[pair])
 
     @pl.when(step == 1)
     def _():
@@ -186,12 +190,12 @@
     return pl.pallas_call(
         analyse_grad_kernel,
         grid=(2, 2),
-        in_specs=[FIELD, FIELD, TABLE, whole((8 * KS, 8 * N))],
-        out_specs=[SENT, FIELD],
-        out_shape=[pltpu.HBM(SENT_SHAPE, F32), pltpu.HBM(cotangent.shape, BF16)],
+        in_specs=[FIELD, FIELD, whole((4, NT * C, MT * C)), whole((8 * KS, 8 * N))],
+        out_specs=SENT,
+        out_shape=pltpu.HBM(SENT_SHAPE, F32),
         scratch_shapes=[
-            pltpu.VMEM((2, 2 * N, NT * C), BF16),
-            pltpu.VMEM((8, 2 * N, MT * C), BF16),
+            pltpu.VMEM((8 * N, NT * C), BF16),
+            pltpu.VMEM((8 * N, NT * C), BF16),
             pltpu.VMEM((4, 8 * KS, MT * C), F32),
         ],
         compiler_params=params(24),
@@ -200,18 +204,55 @@
     )(*in_hbm(cotangent, pre_activation, k["tables"], k["zl"]))
 
 
-def analyse_input(inputs, k):
+def mix_channels_kernel(cot_ref, pre_ref, mix_ref, out_ref, even, odd):
+    def cells(pair, flat):
+        for x in range(4):
+            for y in range(2):
+                for j in range(4):
+                    rows = slice(j * 16, j * 16 + 16)
+                    v = pre_ref[0, x, 2 * pair + y, rows, :].astype(F32)
+                    g = cot_ref[0, x, 2 * pair + y, rows, :].astype(F32)
+                    at = (2 * x + y) * N + j * 16
+                    flat[at : at + 16, :] = (g * gelu_slope(v)).astype(BF16)
+
+    def mix(pair, flat):
+        for side in range(2):
+            lanes = slice(side * 256, side * 256 + 256)
+            mixed = dot(flat[:, lanes], mix_ref[...]).astype(BF16)
+            out_ref[0, :, 2 * pair : 2 * pair + 2, :, lanes] = mixed.reshape(4, 2, N, 256)
+
+    cells(0, even)
+    mix(0, even)
+    cells(1, odd)
+    mix(1, odd)
+
+
+def mix_channels(cotangent, pre_activation, mix):
+    return pl.pallas_call(
+        mix_channels_kernel,
+        grid=(2, 2),
+        in_specs=[FIELD, FIELD, whole((256, 256))],
+        out_specs=FIELD,
+        out_shape=pltpu.HBM(cotangent.shape, BF16),
+        scratch_shapes=[pltpu.VMEM((8 * N, NT * C), BF16)] * 2,
+        compiler_params=params(24),
+        cost_estimate=cost(4 * 10**9, 12 * 10**6),
+        name="mix_channels",
+    )(*in_hbm(cotangent, pre_activation, mix))
+
+
+def analyse_input(inputs, pointwise, k):
     return pl.pallas_call(
         analyse_input_kernel,
         grid=(2, 2),
-        in_specs=[FIELD, TABLE, whole((8 * KS, 8 * N))],
-        out_specs=SENT,
-        out_shape=pltpu.HBM(SENT_SHAPE, F32),
+        in_specs=[FIELD, TABLE, whole((8 * KS, 8 * N)), whole((C, C))],
+        out_specs=[SENT, whole((256, 256))],
+        out_shape=[pltpu.HBM(SENT_SHAPE, F32), pltpu.HBM((256, 256), BF16)],
         scratch_shapes=[pltpu.VMEM((4, 8 * KS, MT * C), F32)],
         compiler_params=params(24),
         cost_estimate=cost(4 * 10**9, 6 * 10**6),
         name="analyse_input",
-    )(*in_hbm(inputs, k["tables"], k["zl"]))
+    )(*in_hbm(inputs, k["tables"], k["zl"], pointwise))
 
 
 def mode_of(j, t):
@@ -410,34 +451,39 @@
 
 def mode_grad_kernel(*refs):
     parts, (spread_ref, weight_hbm, gather_hbm, out_ref, grads_ref) = arrived(refs[:5]), refs[5:10]
-    products, weight_ref, gather_ref, sems = refs[10:]
+    weight_ref, gather_ref, sems = refs[10:]
     copies = []
     for ky in range(3):
-        copies.append(pltpu.make_async_copy(weight_hbm.at[ky], weight_ref.at[ky], sems.at[ky]))
-    copies.append(pltpu.make_async_copy(gather_hbm, gather_ref, sems.at[3]))
+        copies.append(pltpu.make_async_copy(weight_hbm.at[ky], weight_ref.at[ky], sems.at[0, ky]))
+        copies.append(pltpu.make_async_copy(gather_hbm.at[ky], gather_ref.at[ky], sems.at[1, ky]))
     for copy in copies:
         copy.start()
     collect(parts, grads_ref)
-    field = grads_ref[...].reshape(576, 128).astype(BF16)
-    lanes = [dot(field, spread_ref[ky]) for ky in range(3)]
+    field = []
+    for b in range(2):
+        for slot in range(3):
+            for q in range(4):
+                field.append(grads_ref[4 * b + q, slot * KS : slot * KS + KS, :])
+    field = jnp.concatenate(field, axis=0).astype(BF16)
     total = None
-    for j in range(4):
-        if j < 3:
-            copies[j].wait()
+    for ky in range(3):
+        lanes = dot(field, spread_ref[ky]).astype(BF16)
+        copies[2 * ky].wait()
+        products = []
         for b in range(2):
-            for t in range(3):
-                ky, q = mode_of(j, t)
-                for slot in range(3):
-                    at = (3 * b + t) * 72 + slot * KS
-                    source = (4 * b + q) * 72 + slot * KS
-                    weight = weight_ref[ky, slot * 4 + q].astype(F32)
-                    copy = lanes[ky][source : source + KS]
-                    products[at : at + KS, :] = weight * jnp.concatenate([copy] * 8, axis=1)
-        if j == 0:
-            copies[3].wait()
-        term = dot(products[...].astype(BF16), gather_ref[j])
+            copy = lanes[b * 288 : b * 288 + 288]
+            products.append(weight_ref[ky] * jnp.concatenate([copy] * 8, axis=1))
+        copies[2 * ky + 1].wait()
+        term = dot(jnp.concatenate(products, axis=0), gather_ref[ky])
         total = term if total is None else total + term
-    out_ref[...] = total.reshape(TILES)
+    group = lane_group(72)
+    for b in range(2):
+        modes = []
+        for q in range(4):
+            starts = [b * 288 + (slot * 4 + q) * KS for slot in range(3)]
+            modes.append(jnp.concatenate([total[at : at + KS] for at in starts], axis=0))
+        for t in range(3):
+            out_ref[3 * b + t] = jnp.where(group == 3, pltpu.roll(modes[3], 96 - 32 * t, 1), modes[t])
 
 
 def mode_grad(parts, weights, k):
@@ -447,15 +493,14 @@
         in_specs=[vmem] * 6 + [ANY] * 2,
         out_shape=[jax.ShapeDtypeStruct(TILES, F32), jax.ShapeDtypeStruct((8, 72, 128), F32)],
         scratch_shapes=[
-            pltpu.VMEM((432, C * C), F32),
-            pltpu.VMEM(weights.shape, BF16),
+            pltpu.VMEM((3, 12 * KS, C * C), BF16),
             pltpu.VMEM((4, C * C, 128), BF16),
-            pltpu.SemaphoreType.DMA((4,)),
+            pltpu.SemaphoreType.DMA((2, 3)),
         ],
         compiler_params=params(16),
         cost_estimate=cost(10**9, 4 * 10**6),
         name="mode_grad",
-    )(*parts, k["spread"], *in_hbm(weights, k["gather"]))
+    )(*parts, k["spread"], *in_hbm(weights.reshape(3, 12 * KS, C * C), k["gather"]))
 
 
 def backward_kernel(*refs):
@@ -546,7 +591,7 @@
     )(grads, *fields, *in_hbm(k["spread"], k["wide"]))
 
 
-def synthesise_kernel(got_ref, grad_ref, table_ref, zl_ref, mix_ref, out_ref, parts):
+def synthesise_kernel(got_ref, mixed_ref, table_ref, zl_ref, out_ref, parts):
     step = pl.program_id(1)
 
     @pl.when(step == 0)
@@ -569,28 +614,23 @@
 
     for pair in range(2):
         timed = dot(parts[2 * step + pair], table_ref[pair]).astype(BF16)
-        timed = jnp.concatenate([timed, jnp.zeros((64, NT * C), BF16)], axis=0)
         ys = slice(2 * pair, 2 * pair + 2)
-        grad = grad_ref[0, :, ys].reshape(8 * N, NT * C)
-        for side in range(2):
-            lanes = slice(side * 256, side * 256 + 256)
-            left = jnp.concatenate([zl_ref[...], grad[:, lanes]], axis=1)
-            right = jnp.concatenate([timed[:, lanes], mix_ref[...]], axis=0)
-            out_ref[0, :, ys, :, lanes] = dot(left, right).astype(BF16).reshape(4, 2, N, 256)
-
-
-def synthesise(got, grad, mix, k):
+        value = dot(zl_ref[...], timed).reshape(4, 2, N, NT * C)
+        out_ref[0, :, ys] = (value + mixed_ref[0, :, ys].astype(F32)).astype(BF16)
+
+
+def synthesise(got, mixed, k):
     return pl.pallas_call(
         synthesise_kernel,
         grid=(2, 2),
-        in_specs=[SENT, FIELD, TABLE_T, whole((8 * N, 256)), whole((256, 256))],
+        in_specs=[SENT, FIELD, TABLE_T, whole((8 * N, 8 * KS))],
         out_specs=FIELD,
-        out_shape=pltpu.HBM(grad.shape, BF16),
+        out_shape=pltpu.HBM(mixed.shape, BF16),
         scratch_shapes=[pltpu.VMEM((4, 8 * KS, MT * C), BF16)],
         compiler_params=params(24),
         cost_estimate=cost(4 * 10**9, 10 * 10**6),
         name="synthesise",
-    )(got, *in_hbm(grad, k["tables_t"], k["zl_t"], mix))
+    )(got, *in_hbm(mixed, k["tables_t"], k["zl_t"]))
 
 
 def exchange_all(block):
@@ -606,19 +646,21 @@
 def body(inputs, cotangent, pre_activation, pointwise, spectral):
     k = constants()
     weights = jnp.transpose(spectral, (1, 2, 0, 3))
-    mix = jnp.kron(jnp.eye(8, dtype=BF16), pointwise.T)
-    sent, grad_pre = analyse_grad(cotangent, pre_activation, k)
+    sent = analyse_grad(cotangent, pre_activation, k)
     got = exchange_all(sent)
-    sent_input = analyse_input(inputs, k)
-    got, *_ = lax.optimization_barrier((got, sent_input, mix))
+    sent_input, mix = analyse_input(inputs, pointwise, k)
+    mixed = mix_channels(cotangent, pre_activation, mix)
+    got, *_ = lax.optimization_barrier((got, sent_input, mixed))
+    blocks = planes(got, k)
+    sent_input, *_ = lax.optimization_barrier((sent_input, blocks[0]))
     got_input = exchange_first(sent_input)
-    modes, grads = mode_grad(exchange_second(planes(got, k)), weights, k)
-    parts = gather_second(modes)
+    modes, grads = mode_grad(exchange_second(blocks), weights, k)
     got_input, *_ = lax.optimization_barrier((got_input, modes))
     sums = reduce_cores(forward(got_input, k))
-    back = exchange_first(backward(parts, k))
+    back = exchange_first(backward(gather_second(modes), k))
     weight_grad = spectral_grad(grads, reduce_chips(sums), k)
-    return synthesise(back, grad_pre, mix, k), jnp.transpose(weight_grad, (2, 0, 1, 3))
+    back, *_ = lax.optimization_barrier((back, weight_grad))
+    return synthesise(back, mixed, k), jnp.transpose(weight_grad, (2, 0, 1, 3))
 
 
 def solution(mesh):

time: 133 us -> 126 us (0.947)
  waiting for transfers between devices: 45.1 us -> 37.7 us
  Pallas kernels: 44.9 us -> 49.2 us
  local copies, waits for them, and re-layouts: 3.09 us -> 0.01 us
    pallas_call x0 -> x1, Pallas kernels: none -> 8.1 us  [mix_channels(): pl.pallas_call(mix_channels_kernel, grid=(2, 2), in_specs=[FIELD, FIELD,...]
    all_to_all x1, waiting for transfers between devices: 16.3 us -> 8.85 us  [exchange_all(): lax.all_to_all(flat, ('gx', 'gy'), 0, 0, tiled=True).reshape(block.shape)]
    mul x1 -> x0, local copies, waits for them, and re-layouts: 2.09 us -> none  [body(): mix = jnp.kron(jnp.eye(8, dtype=BF16), pointwise.T)]
    pallas_call x1, Pallas kernels: 11.8 us -> 9.87 us  [analyse_grad(): pl.pallas_call(analyse_grad_kernel, grid=(2, 2), in_specs=[FIELD, FIELD,...]
  transfers between devices with their start and end apart: 18 -> 18, of which waited for: 14 -> 14; matrix products, arithmetic and copies ran while one was open for 2% -> 0% of each run, Pallas kernels for 19% -> 23%
where the time goes in v4:
time: 126 us; the launch traced here: 125 us
  Pallas kernels  49.2 us (39%)
  waiting for transfers between devices  37.7 us (30%)
  starting transfers between devices  37.4 us (30%)
    ppermute x15, waiting for transfers between devices, across(): return lax.ppermute(block, 'gy', [(i, i ^ sx) for i in range(8)])  28.9 us
    ppermute x15, starting transfers between devices, across(): return lax.ppermute(block, 'gy', [(i, i ^ sx) for i in range(8)])  14.3 us
    all_to_all x2, starting transfers between devices, exchange_first(): return lax.all_to_all(flat, 'gx', 0, 0, tiled=True).reshape(block.shape)  12.7 us
    all_to_all x1, starting transfers between devices, exchange_all(): lax.all_to_all(flat, ('gx', 'gy'), 0, 0, tiled=True).reshape(block.shape)  10.4 us
    pallas_call x1, Pallas kernels, analyse_grad(): pl.pallas_call(analyse_grad_kernel, grid=(2, 2), in_specs=[FIELD, FIELD,...  9.87 us
    all_to_all x1, waiting for transfers between devices, exchange_all(): lax.all_to_all(flat, ('gx', 'gy'), 0, 0, tiled=True).reshape(block.shape)  8.85 us
    pallas_call x1, Pallas kernels, mix_channels(): pl.pallas_call(mix_channels_kernel, grid=(2, 2), in_specs=[FIELD, FIELD,...  8.1 us
    pallas_call x1, Pallas kernels, synthesise(): pl.pallas_call(synthesise_kernel, grid=(2, 2), in_specs=[SENT, FIELD, TAB...  7.09 us
  transfers between devices with their start and end apart: 18, of which 14 were waited for; matrix products, arithmetic and copies ran while one was open for 0% of the time, Pallas kernels for 23%

profile of v4, /device:TPU:8, one launch (start us, length us, event | category | flops | bytes accessed | tf_op | source)
XLA Modules:
  0.0 125.1 jit_solution(306799459582274934)
XLA Ops:
  0.6 9.9 %analyse_grad.1 = f32[16,8,3,8,128]{4,3,2,1,0:T(8,128)} custom-call(bf16[2,4,8,64,512]{4,3,2,1,0:T(8,128)(2,1)} %cot_ref.3, bf16[2,4,8,64,512]{4,3,2,1,0:T(8,128)(2,1)} %pre_ref.3, bf16[4,512,256]{2,1,0:T(8,128)(2,1)} %constant.22.clone.table_ref, bf16[192,512]{1,0:T(8,128)(2,1)} %constant.23.clone.zl_ref), custom_call_target="tpu_custom_call" | custom-call | flops 4000000000 | bytes 14000000 | tf_op jit(solution)/shard_map/analyse_grad/pallas_call | solution.py:190
  10.5 10.4 %all-to-all-start = ((f32[128,24,128]{2,1,0:T(8,128)}), f32[128,24,128]{2,1,0:T(8,128)S(1)}, u32[]{:S(2)}, u32[]{:S(2)}) async-start(f32[128,24,128]{2,1,0:T(8,128)} %bitcast.16), calls=%async_computation | async-start | bytes 3145728 | tf_op jit(solution)/shard_map/all_to_all | solution.py:638
  21.0 7.0 %analyse_input.1 = (f32[16,8,3,8,128]{4,3,2,1,0:T(8,128)}, bf16[256,256]{1,0:T(8,128)(2,1)}) custom-call(bf16[2,4,8,64,512]{4,3,2,1,0:T(8,128)(2,1)} %field_ref.1, bf16[4,512,256]{2,1,0:T(8,128)(2,1)} %constant.22.clone.table_ref, bf16[192,512]{1,0:T(8,128)(2,1)} %constant.23.clone.zl_ref, bf16[32,32]{1,0:T(8,128)(2,1)} %weight_ref.1), custom_call_target="tpu_custom_call" | custom-call | flops 4000000000 | bytes 6000000 | tf_op jit(solution)/shard_map/analyse_input/pallas_call | solution.py:245
  27.9 8.1 %mix_channels.1.mixed_ref = bf16[2,4,8,64,512]{4,3,2,1,0:T(8,128)(2,1)} custom-call(bf16[2,4,8,64,512]{4,3,2,1,0:T(8,128)(2,1)} %cot_ref.3, bf16[2,4,8,64,512]{4,3,2,1,0:T(8,128)(2,1)} %pre_ref.3, bf16[256,256]{1,0:T(8,128)(2,1)} %get-tuple-element.22.mix_ref), custom_call_target="tpu_custom_call" | custom-call | flops 4000000000 | bytes 12000000 | tf_op jit(solution)/shard_map/mix_channels/pallas_call | solution.py:231
  36.0 8.8 %all-to-all-done = f32[128,24,128]{2,1,0:T(8,128)S(1)} async-done(((f32[128,24,128]{2,1,0:T(8,128)}), f32[128,24,128]{2,1,0:T(8,128)S(1)}, u32[]{:S(2)}, u32[]{:S(2)}) %all-to-all-start) | async-done | bytes 1572896 | tf_op jit(solution)/shard_map/all_to_all | solution.py:638
  44.9 3.3 %planes.1 = (f32[4,72,128]{2,1,0:T(8,128)S(1)}, f32[4,72,128]{2,1,0:T(8,128)S(1)}) custom-call(f32[16,8,3,8,128]{4,3,2,1,0:T(8,128)S(1)} %bitcast.12, bf16[48,256]{1,0:T(8,128)(2,1)S(1)} %copy-done.2, f32[8,3,16,128]{3,2,1,0:T(8,128)} %constant.24.clone.cy_hbm), custom_call_target="tpu_custom_call" | custom-call | flops 1000000000 | bytes 3000000 | tf_op jit(solution)/shard_map/planes/pallas_call | solution.py:412
  48.2 5.4 %all-to-all-start.2 = ((f32[16,192,128]{2,1,0:T(8,128)}), f32[16,192,128]{2,1,0:T(8,128)S(1)}, u32[]{:S(2)}, u32[]{:S(2)}) async-start(f32[16,192,128]{2,1,0:T(8,128)} %bitcast.15), calls=%async_computation.2 | async-start | bytes 3145728 | tf_op jit(solution)/shard_map/all_to_all | solution.py:643
  55.7 1.6 %collective-permute-start.2 = (f32[2,72,128]{2,1,0:T(8,128)S(1)}, f32[2,72,128]{2,1,0:T(8,128)S(1)}, u32[]{:S(2)}, u32[]{:S(2)}) collective-permute-start(f32[2,72,128]{2,1,0:T(8,128)S(1)} %get-tuple-element.27), channel_id=1, source_target_pairs={{0,4},{1,5},{2,6},{3,7},{4,0},{5,1},{6,2},{7,3},{8,12},{9,13},{10,... | collective-permute-start | bytes 221192 | tf_op jit(solution)/shard_map/ppermute | solution.py:326
  57.3 2.5 %collective-permute-start.3 = (f32[2,72,128]{2,1,0:T(8,128)S(1)}, f32[2,72,128]{2,1,0:T(8,128)S(1)}, u32[]{:S(2)}, u32[]{:S(2)}) collective-permute-start(f32[2,72,128]{2,1,0:T(8,128)S(1)} %get-tuple-element.28), channel_id=1, source_target_pairs={{0,6},{1,7},{2,4},{3,5},{4,2},{5,3},{6,0},{7,1},{8,14},{9,15},{10,... | collective-permute-start | bytes 221192 | tf_op jit(solution)/shard_map/ppermute | solution.py:326
  60.2 1.4 %collective-permute-done.2.refs_3_ = f32[2,72,128]{2,1,0:T(8,128)S(1)} collective-permute-done((f32[2,72,128]{2,1,0:T(8,128)S(1)}, f32[2,72,128]{2,1,0:T(8,128)S(1)}, u32[]{:S(2)}, u32[]{:S(2)}) %collective-permute-start.2) | collective-permute-done | bytes 73760 | tf_op jit(solution)/shard_map/ppermute | solution.py:326
  63.1 3.6 %mode_grad.1 = (f32[6,72,128]{2,1,0:T(8,128)S(1)}, f32[8,72,128]{2,1,0:T(8,128)S(1)}) custom-call(f32[4,72,128]{2,1,0:T(8,128)S(1)} %get-tuple-element.24.keep_ref.refs_0_, f32[4,72,128]{2,1,0:T(8,128)S(1)} %collective-permute-done.cross_ref.refs_1_, f32[2,72,128]{2,1,0:T(8,128)S(1)} %collective-permute-done.1.refs_2_, ...), custom_call_target="tpu_custom_call" | custom-call | flops 1000000000 | bytes 4000000 | tf_op jit(solution)/shard_map/mode_grad/pallas_call | solution.py:491
  66.6 2.4 %collective-permute-start.9 = (f32[6,72,128]{2,1,0:T(8,128)S(1)}, f32[6,72,128]{2,1,0:T(8,128)S(1)}, u32[]{:S(2)}, u32[]{:S(2)}) collective-permute-start(f32[6,72,128]{2,1,0:T(8,128)S(1)} %get-tuple-element.29.refs_0_), channel_id=1, source_target_pairs={{0,6},{1,7},{2,4},{3,5},{4,2},{5,3},{6,0},{7,1},{8,14},{9,15},{10,... | collective-permute-start | bytes 663560 | tf_op jit(solution)/shard_map/ppermute | solution.py:326
  69.0 1.8 %collective-permute-start.5 = (f32[6,72,128]{2,1,0:T(8,128)S(1)}, f32[6,72,128]{2,1,0:T(8,128)S(1)}, u32[]{:S(2)}, u32[]{:S(2)}) collective-permute-start(f32[6,72,128]{2,1,0:T(8,128)S(1)} %get-tuple-element.29.refs_0_), channel_id=1, source_target_pairs={{0,2},{1,3},{2,0},{3,1},{4,6},{5,7},{6,4},{7,5},{8,10},{9,11},{10,... | collective-permute-start | bytes 663560 | tf_op jit(solution)/shard_map/ppermute | solution.py:326
  70.8 8.7 %collective-permute-done.9.refs_6_ = f32[6,72,128]{2,1,0:T(8,128)S(1)} collective-permute-done((f32[6,72,128]{2,1,0:T(8,128)S(1)}, f32[6,72,128]{2,1,0:T(8,128)S(1)}, u32[]{:S(2)}, u32[]{:S(2)}) %collective-permute-start.9) | collective-permute-done | bytes 221216 | tf_op jit(solution)/shard_map/ppermute | solution.py:326
  81.6 3.5 %backward.1 = f32[16,8,3,8,128]{4,3,2,1,0:T(8,128)} custom-call(f32[6,72,128]{2,1,0:T(8,128)S(1)} %get-tuple-element.29.refs_0_, f32[6,72,128]{2,1,0:T(8,128)S(1)} %collective-permute-done.4.refs_1_, f32[6,72,128]{2,1,0:T(8,128)S(1)} %collective-permute-done.5.refs_2_, f32[6,72,128]{2,1,0:T(8,128)S(1)} %collective-permute-done.6.refs_3_, ...), custom_call_target="tpu_custom_call" | custom-call | flops 1000000000 | bytes 4000000 | tf_op jit(solution)/shard_map/backward/pallas_call | solution.py:539
  85.1 7.2 %all-to-all-start.1 = ((f32[16,192,128]{2,1,0:T(8,128)}), f32[16,192,128]{2,1,0:T(8,128)S(1)}, u32[]{:S(2)}, u32[]{:S(2)}) async-start(f32[16,192,128]{2,1,0:T(8,128)} %bitcast.13), calls=%async_computation.1 | async-start | bytes 3145728 | tf_op jit(solution)/shard_map/all_to_all | solution.py:643
  92.3 2.3 %forward.1 = (f32[4,6,72,128]{3,2,1,0:T(8,128)S(1)}, f32[4,6,72,128]{3,2,1,0:T(8,128)S(1)}) custom-call(f32[16,8,3,8,128]{4,3,2,1,0:T(8,128)S(1)} %bitcast.10, bf16[48,256]{1,0:T(8,128)(2,1)S(1)} %copy-done.2, bf16[8,256,1024]{2,1,0:T(8,128)(2,1)} %constant.28.clone.refs_9_.yb_hbm), custom_call_target="tpu_custom_call" | custom-call | flops 1000000000 | bytes 4000000 | tf_op jit(solution)/shard_map/forward/pallas_call | solution.py:294
  94.7 2.4 %collective-permute-done.11.cross_ref = f32[4,6,72,128]{3,2,1,0:T(8,128)S(1)} collective-permute-done((f32[4,6,72,128]{3,2,1,0:T(8,128)S(1)}, f32[4,6,72,128]{3,2,1,0:T(8,128)S(1)}, u32[]{:S(2)}, u32[]{:S(2)}) %collective-permute-start.11) | collective-permute-done | bytes 884768 | tf_op jit(solution)/shard_map/ppermute | solution.py:326
  97.5 3.3 %collective-permute-start.13 = (f32[6,72,128]{2,1,0:T(8,128)S(1)}, f32[6,72,128]{2,1,0:T(8,128)S(1)}, u32[]{:S(2)}, u32[]{:S(2)}) collective-permute-start(f32[6,72,128]{2,1,0:T(8,128)S(1)} %get-tuple-element.37), channel_id=1, source_target_pairs={{0,4},{1,5},{2,6},{3,7},{4,0},{5,1},{6,2},{7,3},{8,12},{9,13},{10,... | collective-permute-start | bytes 663560 | tf_op jit(solution)/shard_map/ppermute | solution.py:326
  102.0 3.6 %collective-permute-done.12.refs_1_ = f32[6,72,128]{2,1,0:T(8,128)S(1)} collective-permute-done((f32[6,72,128]{2,1,0:T(8,128)S(1)}, f32[6,72,128]{2,1,0:T(8,128)S(1)}, u32[]{:S(2)}, u32[]{:S(2)}) %collective-permute-start.12) | collective-permute-done | bytes 221216 | tf_op jit(solution)/shard_map/ppermute | solution.py:326
  105.6 5.4 %collective-permute-done.13.refs_2_ = f32[6,72,128]{2,1,0:T(8,128)S(1)} collective-permute-done((f32[6,72,128]{2,1,0:T(8,128)S(1)}, f32[6,72,128]{2,1,0:T(8,128)S(1)}, u32[]{:S(2)}, u32[]{:S(2)}) %collective-permute-start.13) | collective-permute-done | bytes 221216 | tf_op jit(solution)/shard_map/ppermute | solution.py:326
  111.1 2.6 %collective-permute-done.14.refs_3_ = f32[6,72,128]{2,1,0:T(8,128)S(1)} collective-permute-done((f32[6,72,128]{2,1,0:T(8,128)S(1)}, f32[6,72,128]{2,1,0:T(8,128)S(1)}, u32[]{:S(2)}, u32[]{:S(2)}) %collective-permute-start.14) | collective-permute-done | bytes 221216 | tf_op jit(solution)/shard_map/ppermute | solution.py:326
  113.6 4.3 %spectral_grad.1 = f32[3,12,24,1024]{3,2,1,0:T(8,128)} custom-call(f32[8,72,128]{2,1,0:T(8,128)S(1)} %get-tuple-element.30.grads_ref, f32[6,72,128]{2,1,0:T(8,128)S(1)} %get-tuple-element.35.refs_0_, f32[6,72,128]{2,1,0:T(8,128)S(1)} %collective-permute-done.12.refs_1_, f32[6,72,128]{2,1,0:T(8,128)S(1)} %collective-permute-done.13.refs_2_, ...), custom_call_target="tpu_custom_call" | custom-call | flops 1000000000 | bytes 4000000 | tf_op jit(solution)/shard_map/spectral_grad/pallas_call | solution.py:580
  118.0 7.1 %synthesise.1 = bf16[2,4,8,64,512]{4,3,2,1,0:T(8,128)(2,1)} custom-call(f32[16,8,3,8,128]{4,3,2,1,0:T(8,128)S(1)} %bitcast.11, bf16[2,4,8,64,512]{4,3,2,1,0:T(8,128)(2,1)} %mix_channels.1.mixed_ref, bf16[4,256,512]{2,1,0:T(8,128)(2,1)} %constant.31.clone.table_ref, bf16[512,192]{1,0:T(8,128)(2,1)} %constant.32.clone.zl_ref), custom_call_target="tpu_custom_call" | custom-call | flops 4000000000 | bytes 10000000 | tf_op jit(solution)/shard_map/synthesise/pallas_call | solution.py:623
  (29 shorter events, 7.7 us)
Async XLA Ops:
  10.5 34.4 %all-to-all-start = ((f32[128,24,128]{2,1,0:T(8,128)}), f32[128,24,128]{2,1,0:T(8,128)S(1)}, u32[]{:S(2)}, u32[]{:S(2)}) async-start(f32[128,24,128]{2,1,0:T(8,128)} %bitcast.16), calls=%async_computation | async-start | bytes 3145728 | tf_op jit(solution)/shard_map/all_to_all | solution.py:638
  27.9 16.9 %copy-start.2 = (bf16[48,256]{1,0:T(8,128)(2,1)S(1)}, bf16[48,256]{1,0:T(8,128)(2,1)}, u32[]{:S(2)}) copy-start(bf16[48,256]{1,0:T(8,128)(2,1)} %constant.25.clone.xl_ref) | copy-start | bytes 73732
  44.9 18.2 %copy-start = (bf16[4,128,128]{2,1,0:T(8,128)(2,1)S(1)}, bf16[4,128,128]{2,1,0:T(8,128)(2,1)}, u32[]{:S(2)}) copy-start(bf16[4,128,128]{2,1,0:T(8,128)(2,1)} %constant.27.clone.refs_5_.refs_4_) | copy-start | bytes 393220
  48.2 33.4 %copy-start.1 = (bf16[128,96]{1,0:T(8,128)(2,1)S(1)}, bf16[128,96]{1,0:T(8,128)(2,1)}, u32[]{:S(2)}) copy-start(bf16[128,96]{1,0:T(8,128)(2,1)} %constant.29.clone.refs_8_) | copy-start | bytes 73732
  48.2 36.9 %all-to-all-start.2 = ((f32[16,192,128]{2,1,0:T(8,128)}), f32[16,192,128]{2,1,0:T(8,128)S(1)}, u32[]{:S(2)}, u32[]{:S(2)}) async-start(f32[16,192,128]{2,1,0:T(8,128)} %bitcast.15), calls=%async_computation.2 | async-start | bytes 3145728 | tf_op jit(solution)/shard_map/all_to_all | solution.py:643
  53.6 1.4 %collective-permute-start = (f32[4,72,128]{2,1,0:T(8,128)S(1)}, f32[4,72,128]{2,1,0:T(8,128)S(1)}, u32[]{:S(2)}, u32[]{:S(2)}) collective-permute-start(f32[4,72,128]{2,1,0:T(8,128)S(1)} %get-tuple-element.25), channel_id=1, source_target_pairs={{0,1},{1,0},{2,3},{3,2},{4,5},{5,4},{6,7},{7,6},{8,9},{9,8},{10,11... | collective-permute-start | bytes 442376 | tf_op jit(solution)/shard_map/ppermute | solution.py:326
  55.0 5.2 %collective-permute-start.1 = (f32[2,72,128]{2,1,0:T(8,128)S(1)}, f32[2,72,128]{2,1,0:T(8,128)S(1)}, u32[]{:S(2)}, u32[]{:S(2)}) collective-permute-start(f32[2,72,128]{2,1,0:T(8,128)S(1)} %get-tuple-element.26), channel_id=1, source_target_pairs={{0,2},{1,3},{2,0},{3,1},{4,6},{5,7},{6,4},{7,5},{8,10},{9,11},{10,... | collective-permute-start | bytes 221192 | tf_op jit(solution)/shard_map/ppermute | solution.py:326
  55.7 6.0 %collective-permute-start.2 = (f32[2,72,128]{2,1,0:T(8,128)S(1)}, f32[2,72,128]{2,1,0:T(8,128)S(1)}, u32[]{:S(2)}, u32[]{:S(2)}) collective-permute-start(f32[2,72,128]{2,1,0:T(8,128)S(1)} %get-tuple-element.27), channel_id=1, source_target_pairs={{0,4},{1,5},{2,6},{3,7},{4,0},{5,1},{6,2},{7,3},{8,12},{9,13},{10,... | collective-permute-start | bytes 221192 | tf_op jit(solution)/shard_map/ppermute | solution.py:326
  57.3 5.8 %collective-permute-start.3 = (f32[2,72,128]{2,1,0:T(8,128)S(1)}, f32[2,72,128]{2,1,0:T(8,128)S(1)}, u32[]{:S(2)}, u32[]{:S(2)}) collective-permute-start(f32[2,72,128]{2,1,0:T(8,128)S(1)} %get-tuple-element.28), channel_id=1, source_target_pairs={{0,6},{1,7},{2,4},{3,5},{4,2},{5,3},{6,0},{7,1},{8,14},{9,15},{10,... | collective-permute-start | bytes 221192 | tf_op jit(solution)/shard_map/ppermute | solution.py:326
  66.6 12.8 %collective-permute-start.9 = (f32[6,72,128]{2,1,0:T(8,128)S(1)}, f32[6,72,128]{2,1,0:T(8,128)S(1)}, u32[]{:S(2)}, u32[]{:S(2)}) collective-permute-start(f32[6,72,128]{2,1,0:T(8,128)S(1)} %get-tuple-element.29.refs_0_), channel_id=1, source_target_pairs={{0,6},{1,7},{2,4},{3,5},{4,2},{5,3},{6,0},{7,1},{8,14},{9,15},{10,... | collective-permute-start | bytes 663560 | tf_op jit(solution)/shard_map/ppermute | solution.py:326
  69.0 10.4 %collective-permute-start.7 = (f32[6,72,128]{2,1,0:T(8,128)S(1)}, f32[6,72,128]{2,1,0:T(8,128)S(1)}, u32[]{:S(2)}, u32[]{:S(2)}) collective-permute-start(f32[6,72,128]{2,1,0:T(8,128)S(1)} %get-tuple-element.29.refs_0_), channel_id=1, source_target_pairs={{0,4},{1,5},{2,6},{3,7},{4,0},{5,1},{6,2},{7,3},{8,12},{9,13},{10,... | collective-permute-start | bytes 663560 | tf_op jit(solution)/shard_map/ppermute | solution.py:326
  69.0 11.1 %collective-permute-start.5 = (f32[6,72,128]{2,1,0:T(8,128)S(1)}, f32[6,72,128]{2,1,0:T(8,128)S(1)}, u32[]{:S(2)}, u32[]{:S(2)}) collective-permute-start(f32[6,72,128]{2,1,0:T(8,128)S(1)} %get-tuple-element.29.refs_0_), channel_id=1, source_target_pairs={{0,2},{1,3},{2,0},{3,1},{4,6},{5,7},{6,4},{7,5},{8,10},{9,11},{10,... | collective-permute-start | bytes 663560 | tf_op jit(solution)/shard_map/ppermute | solution.py:326
  70.8 9.3 %collective-permute-start.4 = (f32[6,72,128]{2,1,0:T(8,128)S(1)}, f32[6,72,128]{2,1,0:T(8,128)S(1)}, u32[]{:S(2)}, u32[]{:S(2)}) collective-permute-start(f32[6,72,128]{2,1,0:T(8,128)S(1)} %get-tuple-element.29.refs_0_), channel_id=1, source_target_pairs={{0,1},{1,0},{2,3},{3,2},{4,5},{5,4},{6,7},{7,6},{8,9},{9,8},{10,11... | collective-permute-start | bytes 663560 | tf_op jit(solution)/shard_map/ppermute | solution.py:326
  79.5 1.5 %collective-permute-start.10 = (f32[6,72,128]{2,1,0:T(8,128)S(1)}, f32[6,72,128]{2,1,0:T(8,128)S(1)}, u32[]{:S(2)}, u32[]{:S(2)}) collective-permute-start(f32[6,72,128]{2,1,0:T(8,128)S(1)} %collective-permute-done.9.refs_6_), channel_id=1, source_target_pairs={{0,1},{1,0},{2,3},{3,2},{4,5},{5,4},{6,7},{7,6},{8,9},{9,8},{10,11... | collective-permute-start | bytes 663560 | tf_op jit(solution)/shard_map/ppermute | solution.py:326
  79.5 1.8 %collective-permute-start.8 = (f32[6,72,128]{2,1,0:T(8,128)S(1)}, f32[6,72,128]{2,1,0:T(8,128)S(1)}, u32[]{:S(2)}, u32[]{:S(2)}) collective-permute-start(f32[6,72,128]{2,1,0:T(8,128)S(1)} %collective-permute-done.7.refs_4_), channel_id=1, source_target_pairs={{0,1},{1,0},{2,3},{3,2},{4,5},{5,4},{6,7},{7,6},{8,9},{9,8},{10,11... | collective-permute-start | bytes 663560 | tf_op jit(solution)/shard_map/ppermute | solution.py:326
  80.1 1.5 %collective-permute-start.6 = (f32[6,72,128]{2,1,0:T(8,128)S(1)}, f32[6,72,128]{2,1,0:T(8,128)S(1)}, u32[]{:S(2)}, u32[]{:S(2)}) collective-permute-start(f32[6,72,128]{2,1,0:T(8,128)S(1)} %collective-permute-done.5.refs_2_), channel_id=1, source_target_pairs={{0,1},{1,0},{2,3},{3,2},{4,5},{5,4},{6,7},{7,6},{8,9},{9,8},{10,11... | collective-permute-start | bytes 663560 | tf_op jit(solution)/shard_map/ppermute | solution.py:326
  85.1 32.9 %all-to-all-start.1 = ((f32[16,192,128]{2,1,0:T(8,128)}), f32[16,192,128]{2,1,0:T(8,128)S(1)}, u32[]{:S(2)}, u32[]{:S(2)}) async-start(f32[16,192,128]{2,1,0:T(8,128)} %bitcast.13), calls=%async_computation.1 | async-start | bytes 3145728 | tf_op jit(solution)/shard_map/all_to_all | solution.py:643
  94.7 2.5 %collective-permute-start.11 = (f32[4,6,72,128]{3,2,1,0:T(8,128)S(1)}, f32[4,6,72,128]{3,2,1,0:T(8,128)S(1)}, u32[]{:S(2)}, u32[]{:S(2)}) collective-permute-start(f32[4,6,72,128]{3,2,1,0:T(8,128)S(1)} %get-tuple-element.34), channel_id=1, source_target_pairs={{0,1},{1,0},{2,3},{3,2},{4,5},{5,4},{6,7},{7,6},{8,9},{9,8},{10,11... | collective-permute-start | bytes 2654216 | tf_op jit(solution)/shard_map/ppermute | solution.py:326
  97.3 8.3 %collective-permute-start.12 = (f32[6,72,128]{2,1,0:T(8,128)S(1)}, f32[6,72,128]{2,1,0:T(8,128)S(1)}, u32[]{:S(2)}, u32[]{:S(2)}) collective-permute-start(f32[6,72,128]{2,1,0:T(8,128)S(1)} %get-tuple-element.36), channel_id=1, source_target_pairs={{0,2},{1,3},{2,0},{3,1},{4,6},{5,7},{6,4},{7,5},{8,10},{9,11},{10,... | collective-permute-start | bytes 663560 | tf_op jit(solution)/shard_map/ppermute | solution.py:326
  97.5 13.5 %collective-permute-start.13 = (f32[6,72,128]{2,1,0:T(8,128)S(1)}, f32[6,72,128]{2,1,0:T(8,128)S(1)}, u32[]{:S(2)}, u32[]{:S(2)}) collective-permute-start(f32[6,72,128]{2,1,0:T(8,128)S(1)} %get-tuple-element.37), channel_id=1, source_target_pairs={{0,4},{1,5},{2,6},{3,7},{4,0},{5,1},{6,2},{7,3},{8,12},{9,13},{10,... | collective-permute-start | bytes 663560 | tf_op jit(solution)/shard_map/ppermute | solution.py:326
  100.8 12.9 %collective-permute-start.14 = (f32[6,72,128]{2,1,0:T(8,128)S(1)}, f32[6,72,128]{2,1,0:T(8,128)S(1)}, u32[]{:S(2)}, u32[]{:S(2)}) collective-permute-start(f32[6,72,128]{2,1,0:T(8,128)S(1)} %get-tuple-element.38), channel_id=1, source_target_pairs={{0,6},{1,7},{2,4},{3,5},{4,2},{5,3},{6,0},{7,1},{8,14},{9,15},{10,... | collective-permute-start | bytes 663560 | tf_op jit(solution)/shard_map/ppermute | solution.py:326

commit v5 on v4

--- a/solution.py
+++ b/solution.py
@@ -45,14 +45,9 @@
     eye_c = np.eye(C, dtype=np.float32)
     eye_r = np.eye(8, dtype=np.float32)
     out = {}
-    tables = np.zeros((4, NT, C, 2, 4, C), np.float32)
-    for pair in range(4):
-        for kt in range(MT):
-            half, q = divmod(kt, 4)
-            tables[pair, :, :, half, (q + pair) % 4, :] = time[:, kt][:, None, None] * eye_c[None]
-    tables = tables.reshape(4, NT * C, MT * C)
-    out["tables"] = tables.astype(BF)
-    out["tables_t"] = np.swapaxes(tables, 1, 2).copy().astype(BF)
+    table = np.einsum("tm,cd->tcmd", time, eye_c).reshape(NT * C, MT * C)
+    out["table"] = table.astype(BF)
+    out["table_t"] = table.T.copy().astype(BF)
     zl = np.einsum("zk,rs->krsz", third, eye_r).reshape(KS * 8, 8 * N)
     out["zl"] = zl.astype(BF)
     out["zl_t"] = zl.T.copy().astype(BF)
@@ -65,7 +60,9 @@
     padded = np.zeros((N, 8, 4), np.float32)
     padded[:, :, :3] = basis.reshape(N, 8, 3)
     yb = np.einsum("slhdk,ce->shlcdke", padded.reshape(8, 4, 2, 8, 4), eye_c)
-    out["yb"] = yb.reshape(8, 256, 1024).astype(BF)
+    yb = yb.reshape(8, 256, 1024).astype(BF)
+    out["yb"] = yb
+    out["yb_t"] = np.swapaxes(yb, 1, 2).copy()
     second = basis.reshape(8, 4, 2, 8, 3)
     out["cy"] = np.repeat(np.einsum("slhdj->djhsl", second).reshape(8, 3, 16, 4), C, axis=3)
     spread = np.zeros((4, 4, C, 4, C), np.float32)
@@ -102,10 +99,12 @@
     group = lane_group(8 * KS)
     for half in range(2):
         lanes = slice(half * 128, half * 128 + 128)
+        turned = [parts[p, :, lanes] for p in range(4)]
+        turned = [pltpu.roll(value, p * C, 1) if p else value for p, value in enumerate(turned)]
         for q in range(4):
-            value = parts[(-q) % 4, :, lanes]
+            value = turned[(-q) % 4]
             for p in range(1, 4):
-                value = jnp.where(group == p, parts[(p - q) % 4, :, lanes], value)
+                value = jnp.where(group == p, turned[(p - q) % 4], value)
             if q:
                 value = pltpu.roll(value, 128 - q * C, 1)
             for kz in range(KS):
@@ -128,7 +127,7 @@
 
     def analyse(pair, flat):
         sectioned = dot(zl_ref[...], flat[...]).astype(BF16)
-        parts[pair] = dot(sectioned, table_ref[pair])
+        parts[pair] = dot(sectioned, table_ref[...])
 
     analyse((2 * step + 3) % 4, odd)
     cells(0, even)
@@ -154,7 +153,7 @@
     for pair in range(2):
         field = field_ref[0, :, 2 * pair : 2 * pair + 2].reshape(8 * N, NT * C)
         sectioned = dot(zl_ref[...], field).astype(BF16)
-        parts[2 * step + pair] = dot(sectioned, table_ref[pair])
+        parts[2 * step + pair] = dot(sectioned, table_ref[...])
 
     @pl.when(step == 1)
     def _():
@@ -162,8 +161,6 @@
 
 
 FIELD = pl.BlockSpec((1, 4, 4, N, NT * C), lambda b, p: (b, 0, p, 0, 0))
-TABLE = pl.BlockSpec((2, NT * C, MT * C), lambda b, p: (p, 0, 0))
-TABLE_T = pl.BlockSpec((2, MT * C, NT * C), lambda b, p: (p, 0, 0))
 SENT = pl.BlockSpec((16, 4, 3, 8, 128), lambda b, p: (0, b, 0, 0, 0))
 SENT_SHAPE = (16, 8, 3, 8, 128)
 TILES = (6, 72, 128)
@@ -190,7 +187,7 @@
     return pl.pallas_call(
         analyse_grad_kernel,
         grid=(2, 2),
-        in_specs=[FIELD, FIELD, whole((4, NT * C, MT * C)), whole((8 * KS, 8 * N))],
+        in_specs=[FIELD, FIELD, whole((NT * C, MT * C)), whole((8 * KS, 8 * N))],
         out_specs=SENT,
         out_shape=pltpu.HBM(SENT_SHAPE, F32),
         scratch_shapes=[
@@ -201,7 +198,7 @@
         compiler_params=params(24),
         cost_estimate=cost(4 * 10**9, 14 * 10**6),
         name="analyse_grad",
-    )(*in_hbm(cotangent, pre_activation, k["tables"], k["zl"]))
+    )(*in_hbm(cotangent, pre_activation, k["table"], k["zl"]))
 
 
 def mix_channels_kernel(cot_ref, pre_ref, mix_ref, out_ref, even, odd):
@@ -245,14 +242,14 @@
     return pl.pallas_call(
         analyse_input_kernel,
         grid=(2, 2),
-        in_specs=[FIELD, TABLE, whole((8 * KS, 8 * N)), whole((C, C))],
+        in_specs=[FIELD, whole((NT * C, MT * C)), whole((8 * KS, 8 * N)), whole((C, C))],
         out_specs=[SENT, whole((256, 256))],
         out_shape=[pltpu.HBM(SENT_SHAPE, F32), pltpu.HBM((256, 256), BF16)],
         scratch_shapes=[pltpu.VMEM((4, 8 * KS, MT * C), F32)],
         compiler_params=params(24),
         cost_estimate=cost(4 * 10**9, 6 * 10**6),
         name="analyse_input",
-    )(*in_hbm(inputs, k["tables"], k["zl"], pointwise))
+    )(*in_hbm(inputs, k["table"], k["zl"], pointwise))
 
 
 def mode_of(j, t):
@@ -450,12 +447,13 @@
 
 
 def mode_grad_kernel(*refs):
-    parts, (spread_ref, weight_hbm, gather_hbm, out_ref, grads_ref) = arrived(refs[:5]), refs[5:10]
-    weight_ref, gather_ref, sems = refs[10:]
+    parts, (spread_ref, weight_hbm, gather_hbm, yb_hbm) = arrived(refs[:5]), refs[5:9]
+    out_ref, grads_ref, yb_ref, weight_ref, gather_ref, sems = refs[9:]
     copies = []
     for ky in range(3):
         copies.append(pltpu.make_async_copy(weight_hbm.at[ky], weight_ref.at[ky], sems.at[0, ky]))
         copies.append(pltpu.make_async_copy(gather_hbm.at[ky], gather_ref.at[ky], sems.at[1, ky]))
+    copies.append(pltpu.make_async_copy(yb_hbm.at[lax.axis_index("gy")], yb_ref, sems.at[0, 3]))
     for copy in copies:
         copy.start()
     collect(parts, grads_ref)
@@ -484,30 +482,33 @@
             modes.append(jnp.concatenate([total[at : at + KS] for at in starts], axis=0))
         for t in range(3):
             out_ref[3 * b + t] = jnp.where(group == 3, pltpu.roll(modes[3], 96 - 32 * t, 1), modes[t])
+    copies[6].wait()
 
 
 def mode_grad(parts, weights, k):
     vmem = pl.BlockSpec(memory_space=pltpu.VMEM)
     return pl.pallas_call(
         mode_grad_kernel,
-        in_specs=[vmem] * 6 + [ANY] * 2,
-        out_shape=[jax.ShapeDtypeStruct(TILES, F32), jax.ShapeDtypeStruct((8, 72, 128), F32)],
+        in_specs=[vmem] * 6 + [ANY] * 3,
+        out_shape=[
+            jax.ShapeDtypeStruct(TILES, F32),
+            jax.ShapeDtypeStruct((8, 72, 128), F32),
+            pltpu.VMEM((1024, 256), BF16),
+        ],
         scratch_shapes=[
             pltpu.VMEM((3, 12 * KS, C * C), BF16),
             pltpu.VMEM((4, C * C, 128), BF16),
-            pltpu.SemaphoreType.DMA((2, 3)),
+            pltpu.SemaphoreType.DMA((2, 4)),
         ],
         compiler_params=params(16),
         cost_estimate=cost(10**9, 4 * 10**6),
         name="mode_grad",
-    )(*parts, k["spread"], *in_hbm(weights.reshape(3, 12 * KS, C * C), k["gather"]))
+    )(*parts, k["spread"], *in_hbm(weights.reshape(3, 12 * KS, C * C), k["gather"], k["yb_t"]))
 
 
 def backward_kernel(*refs):
-    parts, (xl_ref, yb_hbm, sent_ref, yb_ref, blocks, sem) = refs[:8], refs[8:]
+    parts, (xl_ref, yb_ref, sent_hbm, blocks, sent, sems) = refs[:8], refs[8:]
     me = lax.axis_index("gy")
-    copy = pltpu.make_async_copy(yb_hbm.at[me], yb_ref, sem)
-    copy.start()
     for s in range(8):
         blocks[me ^ s] = parts[s][...]
     group = lane_group(72)
@@ -521,8 +522,8 @@
                 last = jnp.where(group == t, pltpu.roll(three[t], 32 + 32 * t, 1), last)
             tiles += three + [last]
         columns.append(jnp.concatenate(tiles, axis=0).astype(BF16))
-    copy.wait()
-    wide = dot_t(jnp.concatenate(columns, axis=1), yb_ref[...]).astype(BF16)
+    wide = dot(jnp.concatenate(columns, axis=1), yb_ref[...]).astype(BF16)
+    copies = []
     for slot in range(3):
         both = []
         for d in range(8):
@@ -531,25 +532,27 @@
         both = jnp.concatenate(both, axis=1)
         out = dot(xl_ref[...], jnp.concatenate([both, both], axis=0))
         for d in range(8):
-            sent_ref[:, d, slot] = out[:, d * 128 : d * 128 + 128].reshape(16, 8, 128)
-
-
-def backward(parts, k):
-    vmem = pl.BlockSpec(memory_space=pltpu.VMEM)
+            sent[slot, :, d] = out[:, d * 128 : d * 128 + 128].reshape(16, 8, 128)
+        copies.append(pltpu.make_async_copy(sent.at[slot], sent_hbm.at[:, :, slot], sems.at[slot]))
+        copies[-1].start()
+    for copy in copies:
+        copy.wait()
+
+
+def backward(parts, yb, k):
     return pl.pallas_call(
         backward_kernel,
-        in_specs=[vmem] * 9 + [ANY],
         out_shape=pltpu.HBM(SENT_SHAPE, F32),
-        out_specs=pl.BlockSpec(SENT_SHAPE, lambda: (0,) * 5),
+        out_specs=ANY,
         scratch_shapes=[
-            pltpu.VMEM((256, 1024), BF16),
             pltpu.VMEM((8, *TILES), F32),
-            pltpu.SemaphoreType.DMA,
+            pltpu.VMEM((3, 16, 8, 8, 128), F32),
+            pltpu.SemaphoreType.DMA((3,)),
         ],
         compiler_params=params(16),
         cost_estimate=cost(10**9, 4 * 10**6),
         name="backward",
-    )(*parts, k["xl_t"], *in_hbm(k["yb"]))
+    )(*parts, k["xl_t"], yb)
 
 
 def spectral_grad_kernel(grads_ref, *refs):
@@ -591,11 +594,17 @@
     )(grads, *fields, *in_hbm(k["spread"], k["wide"]))
 
 
-def synthesise_kernel(got_ref, mixed_ref, table_ref, zl_ref, out_ref, parts):
-    step = pl.program_id(1)
-
-    @pl.when(step == 0)
-    def _():
+def synthesise_kernel(got_ref, table_ref, zl_ref, mixed_hbm, out_hbm, mixed, out, parts, in_sems, out_sems):
+    def incoming(n):
+        return pltpu.make_async_copy(mixed_hbm.at[n // 4, :, pl.ds(2 * (n % 4), 2)], mixed.at[n], in_sems.at[n])
+
+    def outgoing(n):
+        return pltpu.make_async_copy(out.at[n], out_hbm.at[n // 4, :, pl.ds(2 * (n % 4), 2)], out_sems.at[n])
+
+    for n in range(8):
+        incoming(n).start()
+
+    def gather(b):
         group = lane_group(8 * KS)
         for half in range(2):
             turned = []
@@ -603,34 +612,51 @@
                 tiles = []
                 for kz in range(KS):
                     block, slot = divmod(2 * kz + half, 3)
-                    tiles.append(got_ref[block, q, slot])
+                    tiles.append(got_ref[block, 4 * b + q, slot])
                 value = jnp.concatenate(tiles, axis=0)
                 turned.append(pltpu.roll(value, q * C, 1) if q else value)
             for p in range(4):
                 value = turned[(-p) % 4]
                 for g in range(1, 4):
                     value = jnp.where(group == g, turned[(g - p) % 4], value)
+                value = pltpu.roll(value, 128 - p * C, 1) if p else value
                 parts[p, :, half * 128 : half * 128 + 128] = value.astype(BF16)
 
-    for pair in range(2):
-        timed = dot(parts[2 * step + pair], table_ref[pair]).astype(BF16)
-        ys = slice(2 * pair, 2 * pair + 2)
+    def chunk(n, carry):
+        @pl.when(n % 4 == 0)
+        def _():
+            gather(n // 4)
+
+        incoming(n).wait()
+        timed = dot(parts[n % 4], table_ref[...]).astype(BF16)
         value = dot(zl_ref[...], timed).reshape(4, 2, N, NT * C)
-        out_ref[0, :, ys] = (value + mixed_ref[0, :, ys].astype(F32)).astype(BF16)
+        out[n] = (value + mixed[n].astype(F32)).astype(BF16)
+        outgoing(n).start()
+        return carry
+
+    lax.fori_loop(0, 8, chunk, 0)
+    for n in range(8):
+        outgoing(n).wait()
 
 
 def synthesise(got, mixed, k):
+    vmem = pl.BlockSpec(memory_space=pltpu.VMEM)
     return pl.pallas_call(
         synthesise_kernel,
-        grid=(2, 2),
-        in_specs=[SENT, FIELD, TABLE_T, whole((8 * N, 8 * KS))],
-        out_specs=FIELD,
+        in_specs=[vmem, vmem, vmem, ANY],
+        out_specs=ANY,
         out_shape=pltpu.HBM(mixed.shape, BF16),
-        scratch_shapes=[pltpu.VMEM((4, 8 * KS, MT * C), BF16)],
+        scratch_shapes=[
+            pltpu.VMEM((8, 4, 2, N, NT * C), BF16),
+            pltpu.VMEM((8, 4, 2, N, NT * C), BF16),
+            pltpu.VMEM((4, 8 * KS, MT * C), BF16),
+            pltpu.SemaphoreType.DMA((8,)),
+            pltpu.SemaphoreType.DMA((8,)),
+        ],
         compiler_params=params(24),
         cost_estimate=cost(4 * 10**9, 10 * 10**6),
         name="synthesise",
-    )(got, *in_hbm(mixed, k["tables_t"], k["zl_t"]))
+    )(got, k["table_t"], k["zl_t"], *in_hbm(mixed))
 
 
 def exchange_all(block):
@@ -654,10 +680,10 @@
     blocks = planes(got, k)
     sent_input, *_ = lax.optimization_barrier((sent_input, blocks[0]))
     got_input = exchange_first(sent_input)
-    modes, grads = mode_grad(exchange_second(blocks), weights, k)
+    modes, grads, yb = mode_grad(exchange_second(blocks), weights, k)
     got_input, *_ = lax.optimization_barrier((got_input, modes))
     sums = reduce_cores(forward(got_input, k))
-    back = exchange_first(backward(gather_second(modes), k))
+    back = exchange_first(backward(gather_second(modes), yb, k))
     weight_grad = spectral_grad(grads, reduce_chips(sums), k)
     back, *_ = lax.optimization_barrier((back, weight_grad))
     return synthesise(back, mixed, k), jnp.transpose(weight_grad, (2, 0, 1, 3))

time: 126 us -> 124 us (0.984)
  Pallas kernels: 49.2 us -> 47 us
    pallas_call x4, Pallas kernels: 21.1 us -> 18.9 us  [the longest x1 7.1 us: analyse_input(): pl.pallas_call(analyse_input_kernel, grid=(2, 2), in_specs=[FIELD, whole(...]
  transfers between devices with their start and end apart: 18 -> 18, of which waited for: 14 -> 14; matrix products, arithmetic and copies ran while one was open for 0% -> 0% of each run, Pallas kernels for 23% -> 22%
where the time goes in v5:
time: 124 us; the launch traced here: 123 us
  Pallas kernels  47 us (38%)
  waiting for transfers between devices  37.6 us (30%)
  starting transfers between devices  37.4 us (30%)
    ppermute x15, waiting for transfers between devices, across(): return lax.ppermute(block, 'gy', [(i, i ^ sx) for i in range(8)])  28.9 us
    ppermute x15, starting transfers between devices, across(): return lax.ppermute(block, 'gy', [(i, i ^ sx) for i in range(8)])  14.3 us
    all_to_all x2, starting transfers between devices, exchange_first(): return lax.all_to_all(flat, 'gx', 0, 0, tiled=True).reshape(block.shape)  12.7 us
    all_to_all x1, starting transfers between devices, exchange_all(): lax.all_to_all(flat, ('gx', 'gy'), 0, 0, tiled=True).reshape(block.shape)  10.4 us
    pallas_call x1, Pallas kernels, analyse_grad(): pl.pallas_call(analyse_grad_kernel, grid=(2, 2), in_specs=[FIELD, FIELD,...  9.84 us
    all_to_all x1, waiting for transfers between devices, exchange_all(): lax.all_to_all(flat, ('gx', 'gy'), 0, 0, tiled=True).reshape(block.shape)  8.72 us
    pallas_call x1, Pallas kernels, mix_channels(): pl.pallas_call(mix_channels_kernel, grid=(2, 2), in_specs=[FIELD, FIELD,...  8.1 us
    pallas_call x1, Pallas kernels, analyse_input(): pl.pallas_call(analyse_input_kernel, grid=(2, 2), in_specs=[FIELD, whole(...  7.1 us
  transfers between devices with their start and end apart: 18, of which 14 were waited for; matrix products, arithmetic and copies ran while one was open for 0% of the time, Pallas kernels for 22%

profile of v5, /device:TPU:8, one launch (start us, length us, event | category | flops | bytes accessed | tf_op | source)
XLA Modules:
  0.0 122.9 jit_solution(1786309110361081559)
XLA Ops:
  0.6 9.8 %analyse_grad.1 = f32[16,8,3,8,128]{4,3,2,1,0:T(8,128)} custom-call(bf16[2,4,8,64,512]{4,3,2,1,0:T(8,128)(2,1)} %cot_ref.3, bf16[2,4,8,64,512]{4,3,2,1,0:T(8,128)(2,1)} %pre_ref.3, bf16[512,256]{1,0:T(8,128)(2,1)} %constant.24.clone.table_ref, bf16[192,512]{1,0:T(8,128)(2,1)} %constant.25.clone.zl_ref), custom_call_target="tpu_custom_call" | custom-call | flops 4000000000 | bytes 14000000 | tf_op jit(solution)/shard_map/analyse_grad/pallas_call | solution.py:187
  10.5 10.4 %all-to-all-start = ((f32[128,24,128]{2,1,0:T(8,128)}), f32[128,24,128]{2,1,0:T(8,128)S(1)}, u32[]{:S(2)}, u32[]{:S(2)}) async-start(f32[128,24,128]{2,1,0:T(8,128)} %bitcast.17), calls=%async_computation | async-start | bytes 3145728 | tf_op jit(solution)/shard_map/all_to_all | solution.py:664
  20.9 7.1 %analyse_input.1 = (f32[16,8,3,8,128]{4,3,2,1,0:T(8,128)}, bf16[256,256]{1,0:T(8,128)(2,1)}) custom-call(bf16[2,4,8,64,512]{4,3,2,1,0:T(8,128)(2,1)} %field_ref.1, bf16[512,256]{1,0:T(8,128)(2,1)} %constant.24.clone.table_ref, bf16[192,512]{1,0:T(8,128)(2,1)} %constant.25.clone.zl_ref, bf16[32,32]{1,0:T(8,128)(2,1)} %weight_ref.1), custom_call_target="tpu_custom_call" | custom-call | flops 4000000000 | bytes 6000000 | tf_op jit(solution)/shard_map/analyse_input/pallas_call | solution.py:242
  28.0 8.1 %mix_channels.1.mixed_hbm = bf16[2,4,8,64,512]{4,3,2,1,0:T(8,128)(2,1)} custom-call(bf16[2,4,8,64,512]{4,3,2,1,0:T(8,128)(2,1)} %cot_ref.3, bf16[2,4,8,64,512]{4,3,2,1,0:T(8,128)(2,1)} %pre_ref.3, bf16[256,256]{1,0:T(8,128)(2,1)} %get-tuple-element.23.mix_ref), custom_call_target="tpu_custom_call" | custom-call | flops 4000000000 | bytes 12000000 | tf_op jit(solution)/shard_map/mix_channels/pallas_call | solution.py:228
  36.1 8.7 %all-to-all-done = f32[128,24,128]{2,1,0:T(8,128)S(1)} async-done(((f32[128,24,128]{2,1,0:T(8,128)}), f32[128,24,128]{2,1,0:T(8,128)S(1)}, u32[]{:S(2)}, u32[]{:S(2)}) %all-to-all-start) | async-done | bytes 1572896 | tf_op jit(solution)/shard_map/all_to_all | solution.py:664
  44.8 3.3 %planes.1 = (f32[4,72,128]{2,1,0:T(8,128)S(1)}, f32[4,72,128]{2,1,0:T(8,128)S(1)}) custom-call(f32[16,8,3,8,128]{4,3,2,1,0:T(8,128)S(1)} %bitcast.12, bf16[48,256]{1,0:T(8,128)(2,1)S(1)} %copy-done.4, f32[8,3,16,128]{3,2,1,0:T(8,128)} %constant.26.clone.cy_hbm), custom_call_target="tpu_custom_call" | custom-call | flops 1000000000 | bytes 3000000 | tf_op jit(solution)/shard_map/planes/pallas_call | solution.py:409
  48.2 5.4 %all-to-all-start.2 = ((f32[16,192,128]{2,1,0:T(8,128)}), f32[16,192,128]{2,1,0:T(8,128)S(1)}, u32[]{:S(2)}, u32[]{:S(2)}) async-start(f32[16,192,128]{2,1,0:T(8,128)} %bitcast.16), calls=%async_computation.2 | async-start | bytes 3145728 | tf_op jit(solution)/shard_map/all_to_all | solution.py:669
  55.6 1.6 %collective-permute-start.2 = (f32[2,72,128]{2,1,0:T(8,128)S(1)}, f32[2,72,128]{2,1,0:T(8,128)S(1)}, u32[]{:S(2)}, u32[]{:S(2)}) collective-permute-start(f32[2,72,128]{2,1,0:T(8,128)S(1)} %get-tuple-element.28), channel_id=1, source_target_pairs={{0,4},{1,5},{2,6},{3,7},{4,0},{5,1},{6,2},{7,3},{8,12},{9,13},{10,... | collective-permute-start | bytes 221192 | tf_op jit(solution)/shard_map/ppermute | solution.py:323
  57.3 2.5 %collective-permute-start.3 = (f32[2,72,128]{2,1,0:T(8,128)S(1)}, f32[2,72,128]{2,1,0:T(8,128)S(1)}, u32[]{:S(2)}, u32[]{:S(2)}) collective-permute-start(f32[2,72,128]{2,1,0:T(8,128)S(1)} %get-tuple-element.29), channel_id=1, source_target_pairs={{0,6},{1,7},{2,4},{3,5},{4,2},{5,3},{6,0},{7,1},{8,14},{9,15},{10,... | collective-permute-start | bytes 221192 | tf_op jit(solution)/shard_map/ppermute | solution.py:323
  60.2 1.4 %collective-permute-done.2.refs_3_ = f32[2,72,128]{2,1,0:T(8,128)S(1)} collective-permute-done((f32[2,72,128]{2,1,0:T(8,128)S(1)}, f32[2,72,128]{2,1,0:T(8,128)S(1)}, u32[]{:S(2)}, u32[]{:S(2)}) %collective-permute-start.2) | collective-permute-done | bytes 73760 | tf_op jit(solution)/shard_map/ppermute | solution.py:323
  63.0 3.6 %mode_grad.1 = (f32[6,72,128]{2,1,0:T(8,128)S(1)}, f32[8,72,128]{2,1,0:T(8,128)S(1)}, bf16[1024,256]{1,0:T(8,128)(2,1)S(1)}) custom-call(f32[4,72,128]{2,1,0:T(8,128)S(1)} %get-tuple-element.25.keep_ref.refs_0_, f32[4,72,128]{2,1,0:T(8,128)S(1)} %collective-permute-done.cross_ref.refs_1_, f32[2,72,128]{2,1,0:T(8,128)S(1)} %collective-permute-done.1.refs_2_, ...), custom_call_target="tpu_custom_call" | custom-call | flops 1000000000 | bytes 4000000 | tf_op jit(solution)/shard_map/mode_grad/pallas_call | solution.py:490
  66.6 2.4 %collective-permute-start.9 = (f32[6,72,128]{2,1,0:T(8,128)S(1)}, f32[6,72,128]{2,1,0:T(8,128)S(1)}, u32[]{:S(2)}, u32[]{:S(2)}) collective-permute-start(f32[6,72,128]{2,1,0:T(8,128)S(1)} %get-tuple-element.30.refs_0_), channel_id=1, source_target_pairs={{0,6},{1,7},{2,4},{3,5},{4,2},{5,3},{6,0},{7,1},{8,14},{9,15},{10,... | collective-permute-start | bytes 663560 | tf_op jit(solution)/shard_map/ppermute | solution.py:323
  69.0 1.8 %collective-permute-start.5 = (f32[6,72,128]{2,1,0:T(8,128)S(1)}, f32[6,72,128]{2,1,0:T(8,128)S(1)}, u32[]{:S(2)}, u32[]{:S(2)}) collective-permute-start(f32[6,72,128]{2,1,0:T(8,128)S(1)} %get-tuple-element.30.refs_0_), channel_id=1, source_target_pairs={{0,2},{1,3},{2,0},{3,1},{4,6},{5,7},{6,4},{7,5},{8,10},{9,11},{10,... | collective-permute-start | bytes 663560 | tf_op jit(solution)/shard_map/ppermute | solution.py:323
  70.8 8.7 %collective-permute-done.9.refs_6_ = f32[6,72,128]{2,1,0:T(8,128)S(1)} collective-permute-done((f32[6,72,128]{2,1,0:T(8,128)S(1)}, f32[6,72,128]{2,1,0:T(8,128)S(1)}, u32[]{:S(2)}, u32[]{:S(2)}) %collective-permute-start.9) | collective-permute-done | bytes 221216 | tf_op jit(solution)/shard_map/ppermute | solution.py:323
  81.6 2.1 %backward.1 = f32[16,8,3,8,128]{4,3,2,1,0:T(8,128)} custom-call(f32[6,72,128]{2,1,0:T(8,128)S(1)} %get-tuple-element.30.refs_0_, f32[6,72,128]{2,1,0:T(8,128)S(1)} %collective-permute-done.4.refs_1_, f32[6,72,128]{2,1,0:T(8,128)S(1)} %collective-permute-done.5.refs_2_, f32[6,72,128]{2,1,0:T(8,128)S(1)} %collective-permute-done.6.refs_3_, ...), custom_call_target="tpu_custom_call" | custom-call | flops 1000000000 | bytes 4000000 | tf_op jit(solution)/shard_map/backward/pallas_call | solution.py:543
  83.7 7.2 %all-to-all-start.1 = ((f32[16,192,128]{2,1,0:T(8,128)}), f32[16,192,128]{2,1,0:T(8,128)S(1)}, u32[]{:S(2)}, u32[]{:S(2)}) async-start(f32[16,192,128]{2,1,0:T(8,128)} %bitcast.13), calls=%async_computation.1 | async-start | bytes 3145728 | tf_op jit(solution)/shard_map/all_to_all | solution.py:669
  90.9 2.3 %forward.1 = (f32[4,6,72,128]{3,2,1,0:T(8,128)S(1)}, f32[4,6,72,128]{3,2,1,0:T(8,128)S(1)}) custom-call(f32[16,8,3,8,128]{4,3,2,1,0:T(8,128)S(1)} %bitcast.10, bf16[48,256]{1,0:T(8,128)(2,1)S(1)} %copy-done.4, bf16[8,256,1024]{2,1,0:T(8,128)(2,1)} %constant.31.clone.yb_hbm), custom_call_target="tpu_custom_call" | custom-call | flops 1000000000 | bytes 4000000 | tf_op jit(solution)/shard_map/forward/pallas_call | solution.py:291
  93.3 2.4 %collective-permute-done.11.cross_ref = f32[4,6,72,128]{3,2,1,0:T(8,128)S(1)} collective-permute-done((f32[4,6,72,128]{3,2,1,0:T(8,128)S(1)}, f32[4,6,72,128]{3,2,1,0:T(8,128)S(1)}, u32[]{:S(2)}, u32[]{:S(2)}) %collective-permute-start.11) | collective-permute-done | bytes 884768 | tf_op jit(solution)/shard_map/ppermute | solution.py:323
  96.1 3.3 %collective-permute-start.13 = (f32[6,72,128]{2,1,0:T(8,128)S(1)}, f32[6,72,128]{2,1,0:T(8,128)S(1)}, u32[]{:S(2)}, u32[]{:S(2)}) collective-permute-start(f32[6,72,128]{2,1,0:T(8,128)S(1)} %get-tuple-element.39), channel_id=1, source_target_pairs={{0,4},{1,5},{2,6},{3,7},{4,0},{5,1},{6,2},{7,3},{8,12},{9,13},{10,... | collective-permute-start | bytes 663560 | tf_op jit(solution)/shard_map/ppermute | solution.py:323
  100.6 3.6 %collective-permute-done.12.refs_1_ = f32[6,72,128]{2,1,0:T(8,128)S(1)} collective-permute-done((f32[6,72,128]{2,1,0:T(8,128)S(1)}, f32[6,72,128]{2,1,0:T(8,128)S(1)}, u32[]{:S(2)}, u32[]{:S(2)}) %collective-permute-start.12) | collective-permute-done | bytes 221216 | tf_op jit(solution)/shard_map/ppermute | solution.py:323
  104.2 5.4 %collective-permute-done.13.refs_2_ = f32[6,72,128]{2,1,0:T(8,128)S(1)} collective-permute-done((f32[6,72,128]{2,1,0:T(8,128)S(1)}, f32[6,72,128]{2,1,0:T(8,128)S(1)}, u32[]{:S(2)}, u32[]{:S(2)}) %collective-permute-start.13) | collective-permute-done | bytes 221216 | tf_op jit(solution)/shard_map/ppermute | solution.py:323
  109.6 2.6 %collective-permute-done.14.refs_3_ = f32[6,72,128]{2,1,0:T(8,128)S(1)} collective-permute-done((f32[6,72,128]{2,1,0:T(8,128)S(1)}, f32[6,72,128]{2,1,0:T(8,128)S(1)}, u32[]{:S(2)}, u32[]{:S(2)}) %collective-permute-start.14) | collective-permute-done | bytes 221216 | tf_op jit(solution)/shard_map/ppermute | solution.py:323
  112.2 4.3 %spectral_grad.1 = f32[3,12,24,1024]{3,2,1,0:T(8,128)} custom-call(f32[8,72,128]{2,1,0:T(8,128)S(1)} %copy-done.2, f32[6,72,128]{2,1,0:T(8,128)S(1)} %get-tuple-element.37.refs_0_, f32[6,72,128]{2,1,0:T(8,128)S(1)} %collective-permute-done.12.refs_1_, f32[6,72,128]{2,1,0:T(8,128)S(1)} %collective-permute-done.13.refs_2_, ...), custom_call_target="tpu_custom_call" | custom-call | flops 1000000000 | bytes 4000000 | tf_op jit(solution)/shard_map/spectral_grad/pallas_call | solution.py:583
  116.6 6.2 %synthesise.1 = bf16[2,4,8,64,512]{4,3,2,1,0:T(8,128)(2,1)} custom-call(f32[16,8,3,8,128]{4,3,2,1,0:T(8,128)S(1)} %bitcast.11, bf16[256,512]{1,0:T(8,128)(2,1)S(1)} %copy-done.6, bf16[512,192]{1,0:T(8,128)(2,1)S(1)} %copy-done.5, bf16[2,4,8,64,512]{4,3,2,1,0:T(8,128)(2,1)} %mix_channels.1.mixed_hbm), custom_call_target="tpu_custom_call" | custom-call | flops 4000000000 | bytes 10000000 | tf_op jit(solution)/shard_map/synthesise/pallas_call | solution.py:644
  (37 shorter events, 7.7 us)
Async XLA Ops:
  10.5 34.4 %all-to-all-start = ((f32[128,24,128]{2,1,0:T(8,128)}), f32[128,24,128]{2,1,0:T(8,128)S(1)}, u32[]{:S(2)}, u32[]{:S(2)}) async-start(f32[128,24,128]{2,1,0:T(8,128)} %bitcast.17), calls=%async_computation | async-start | bytes 3145728 | tf_op jit(solution)/shard_map/all_to_all | solution.py:664
  44.8 18.2 %copy-start = (bf16[4,128,128]{2,1,0:T(8,128)(2,1)S(1)}, bf16[4,128,128]{2,1,0:T(8,128)(2,1)}, u32[]{:S(2)}) copy-start(bf16[4,128,128]{2,1,0:T(8,128)(2,1)} %constant.30.clone.refs_5_.refs_4_) | copy-start | bytes 393220
  48.2 35.5 %all-to-all-start.2 = ((f32[16,192,128]{2,1,0:T(8,128)}), f32[16,192,128]{2,1,0:T(8,128)S(1)}, u32[]{:S(2)}, u32[]{:S(2)}) async-start(f32[16,192,128]{2,1,0:T(8,128)} %bitcast.16), calls=%async_computation.2 | async-start | bytes 3145728 | tf_op jit(solution)/shard_map/all_to_all | solution.py:669
  53.6 1.4 %collective-permute-start = (f32[4,72,128]{2,1,0:T(8,128)S(1)}, f32[4,72,128]{2,1,0:T(8,128)S(1)}, u32[]{:S(2)}, u32[]{:S(2)}) collective-permute-start(f32[4,72,128]{2,1,0:T(8,128)S(1)} %get-tuple-element.26), channel_id=1, source_target_pairs={{0,1},{1,0},{2,3},{3,2},{4,5},{5,4},{6,7},{7,6},{8,9},{9,8},{10,11... | collective-permute-start | bytes 442376 | tf_op jit(solution)/shard_map/ppermute | solution.py:323
  55.0 5.2 %collective-permute-start.1 = (f32[2,72,128]{2,1,0:T(8,128)S(1)}, f32[2,72,128]{2,1,0:T(8,128)S(1)}, u32[]{:S(2)}, u32[]{:S(2)}) collective-permute-start(f32[2,72,128]{2,1,0:T(8,128)S(1)} %get-tuple-element.27), channel_id=1, source_target_pairs={{0,2},{1,3},{2,0},{3,1},{4,6},{5,7},{6,4},{7,5},{8,10},{9,11},{10,... | collective-permute-start | bytes 221192 | tf_op jit(solution)/shard_map/ppermute | solution.py:323
  55.6 6.0 %collective-permute-start.2 = (f32[2,72,128]{2,1,0:T(8,128)S(1)}, f32[2,72,128]{2,1,0:T(8,128)S(1)}, u32[]{:S(2)}, u32[]{:S(2)}) collective-permute-start(f32[2,72,128]{2,1,0:T(8,128)S(1)} %get-tuple-element.28), channel_id=1, source_target_pairs={{0,4},{1,5},{2,6},{3,7},{4,0},{5,1},{6,2},{7,3},{8,12},{9,13},{10,... | collective-permute-start | bytes 221192 | tf_op jit(solution)/shard_map/ppermute | solution.py:323
  57.3 5.8 %collective-permute-start.3 = (f32[2,72,128]{2,1,0:T(8,128)S(1)}, f32[2,72,128]{2,1,0:T(8,128)S(1)}, u32[]{:S(2)}, u32[]{:S(2)}) collective-permute-start(f32[2,72,128]{2,1,0:T(8,128)S(1)} %get-tuple-element.29), channel_id=1, source_target_pairs={{0,6},{1,7},{2,4},{3,5},{4,2},{5,3},{6,0},{7,1},{8,14},{9,15},{10,... | collective-permute-start | bytes 221192 | tf_op jit(solution)/shard_map/ppermute | solution.py:323
  63.0 18.6 %copy-start.3 = (bf16[128,96]{1,0:T(8,128)(2,1)S(1)}, bf16[128,96]{1,0:T(8,128)(2,1)}, u32[]{:S(2)}) copy-start(bf16[128,96]{1,0:T(8,128)(2,1)} %constant.32.clone.refs_8_) | copy-start | bytes 73732
  66.6 17.0 %copy-start.1 = (f32[8,72,128]{2,1,0:T(8,128)}, f32[8,72,128]{2,1,0:T(8,128)S(1)}, u32[]{:S(2)}) copy-start(f32[8,72,128]{2,1,0:T(8,128)S(1)} %get-tuple-element.32.grads_ref) | copy-start | bytes 884740
  66.6 12.8 %collective-permute-start.9 = (f32[6,72,128]{2,1,0:T(8,128)S(1)}, f32[6,72,128]{2,1,0:T(8,128)S(1)}, u32[]{:S(2)}, u32[]{:S(2)}) collective-permute-start(f32[6,72,128]{2,1,0:T(8,128)S(1)} %get-tuple-element.30.refs_0_), channel_id=1, source_target_pairs={{0,6},{1,7},{2,4},{3,5},{4,2},{5,3},{6,0},{7,1},{8,14},{9,15},{10,... | collective-permute-start | bytes 663560 | tf_op jit(solution)/shard_map/ppermute | solution.py:323
  69.0 10.4 %collective-permute-start.7 = (f32[6,72,128]{2,1,0:T(8,128)S(1)}, f32[6,72,128]{2,1,0:T(8,128)S(1)}, u32[]{:S(2)}, u32[]{:S(2)}) collective-permute-start(f32[6,72,128]{2,1,0:T(8,128)S(1)} %get-tuple-element.30.refs_0_), channel_id=1, source_target_pairs={{0,4},{1,5},{2,6},{3,7},{4,0},{5,1},{6,2},{7,3},{8,12},{9,13},{10,... | collective-permute-start | bytes 663560 | tf_op jit(solution)/shard_map/ppermute | solution.py:323
  69.0 11.1 %collective-permute-start.5 = (f32[6,72,128]{2,1,0:T(8,128)S(1)}, f32[6,72,128]{2,1,0:T(8,128)S(1)}, u32[]{:S(2)}, u32[]{:S(2)}) collective-permute-start(f32[6,72,128]{2,1,0:T(8,128)S(1)} %get-tuple-element.30.refs_0_), channel_id=1, source_target_pairs={{0,2},{1,3},{2,0},{3,1},{4,6},{5,7},{6,4},{7,5},{8,10},{9,11},{10,... | collective-permute-start | bytes 663560 | tf_op jit(solution)/shard_map/ppermute | solution.py:323
  70.8 9.3 %collective-permute-start.4 = (f32[6,72,128]{2,1,0:T(8,128)S(1)}, f32[6,72,128]{2,1,0:T(8,128)S(1)}, u32[]{:S(2)}, u32[]{:S(2)}) collective-permute-start(f32[6,72,128]{2,1,0:T(8,128)S(1)} %get-tuple-element.30.refs_0_), channel_id=1, source_target_pairs={{0,1},{1,0},{2,3},{3,2},{4,5},{5,4},{6,7},{7,6},{8,9},{9,8},{10,11... | collective-permute-start | bytes 663560 | tf_op jit(solution)/shard_map/ppermute | solution.py:323
  79.5 1.5 %collective-permute-start.10 = (f32[6,72,128]{2,1,0:T(8,128)S(1)}, f32[6,72,128]{2,1,0:T(8,128)S(1)}, u32[]{:S(2)}, u32[]{:S(2)}) collective-permute-start(f32[6,72,128]{2,1,0:T(8,128)S(1)} %collective-permute-done.9.refs_6_), channel_id=1, source_target_pairs={{0,1},{1,0},{2,3},{3,2},{4,5},{5,4},{6,7},{7,6},{8,9},{9,8},{10,11... | collective-permute-start | bytes 663560 | tf_op jit(solution)/shard_map/ppermute | solution.py:323
  79.5 1.8 %collective-permute-start.8 = (f32[6,72,128]{2,1,0:T(8,128)S(1)}, f32[6,72,128]{2,1,0:T(8,128)S(1)}, u32[]{:S(2)}, u32[]{:S(2)}) collective-permute-start(f32[6,72,128]{2,1,0:T(8,128)S(1)} %collective-permute-done.7.refs_4_), channel_id=1, source_target_pairs={{0,1},{1,0},{2,3},{3,2},{4,5},{5,4},{6,7},{7,6},{8,9},{9,8},{10,11... | collective-permute-start | bytes 663560 | tf_op jit(solution)/shard_map/ppermute | solution.py:323
  80.1 1.5 %collective-permute-start.6 = (f32[6,72,128]{2,1,0:T(8,128)S(1)}, f32[6,72,128]{2,1,0:T(8,128)S(1)}, u32[]{:S(2)}, u32[]{:S(2)}) collective-permute-start(f32[6,72,128]{2,1,0:T(8,128)S(1)} %collective-permute-done.5.refs_2_), channel_id=1, source_target_pairs={{0,1},{1,0},{2,3},{3,2},{4,5},{5,4},{6,7},{7,6},{8,9},{9,8},{10,11... | collective-permute-start | bytes 663560 | tf_op jit(solution)/shard_map/ppermute | solution.py:323
  83.7 32.9 %all-to-all-start.1 = ((f32[16,192,128]{2,1,0:T(8,128)}), f32[16,192,128]{2,1,0:T(8,128)S(1)}, u32[]{:S(2)}, u32[]{:S(2)}) async-start(f32[16,192,128]{2,1,0:T(8,128)} %bitcast.13), calls=%async_computation.1 | async-start | bytes 3145728 | tf_op jit(solution)/shard_map/all_to_all | solution.py:669
  90.9 21.3 %copy-start.2 = (f32[8,72,128]{2,1,0:T(8,128)S(1)}, f32[8,72,128]{2,1,0:T(8,128)}, u32[]{:S(2)}) copy-start(f32[8,72,128]{2,1,0:T(8,128)} %copy-done.1) | copy-start | bytes 884740
  93.2 2.5 %collective-permute-start.11 = (f32[4,6,72,128]{3,2,1,0:T(8,128)S(1)}, f32[4,6,72,128]{3,2,1,0:T(8,128)S(1)}, u32[]{:S(2)}, u32[]{:S(2)}) collective-permute-start(f32[4,6,72,128]{3,2,1,0:T(8,128)S(1)} %get-tuple-element.36), channel_id=1, source_target_pairs={{0,1},{1,0},{2,3},{3,2},{4,5},{5,4},{6,7},{7,6},{8,9},{9,8},{10,11... | collective-permute-start | bytes 2654216 | tf_op jit(solution)/shard_map/ppermute | solution.py:323
  95.7 20.8 %copy-start.5 = (bf16[512,192]{1,0:T(8,128)(2,1)S(1)}, bf16[512,192]{1,0:T(8,128)(2,1)}, u32[]{:S(2)}) copy-start(bf16[512,192]{1,0:T(8,128)(2,1)} %constant.35.clone.zl_ref) | copy-start | bytes 589828
  95.7 20.8 %copy-start.6 = (bf16[256,512]{1,0:T(8,128)(2,1)S(1)}, bf16[256,512]{1,0:T(8,128)(2,1)}, u32[]{:S(2)}) copy-start(bf16[256,512]{1,0:T(8,128)(2,1)} %constant.34.clone.table_ref) | copy-start | bytes 786436
  95.8 8.3 %collective-permute-start.12 = (f32[6,72,128]{2,1,0:T(8,128)S(1)}, f32[6,72,128]{2,1,0:T(8,128)S(1)}, u32[]{:S(2)}, u32[]{:S(2)}) collective-permute-start(f32[6,72,128]{2,1,0:T(8,128)S(1)} %get-tuple-element.38), channel_id=1, source_target_pairs={{0,2},{1,3},{2,0},{3,1},{4,6},{5,7},{6,4},{7,5},{8,10},{9,11},{10,... | collective-permute-start | bytes 663560 | tf_op jit(solution)/shard_map/ppermute | solution.py:323
  96.1 13.5 %collective-permute-start.13 = (f32[6,72,128]{2,1,0:T(8,128)S(1)}, f32[6,72,128]{2,1,0:T(8,128)S(1)}, u32[]{:S(2)}, u32[]{:S(2)}) collective-permute-start(f32[6,72,128]{2,1,0:T(8,128)S(1)} %get-tuple-element.39), channel_id=1, source_target_pairs={{0,4},{1,5},{2,6},{3,7},{4,0},{5,1},{6,2},{7,3},{8,12},{9,13},{10,... | collective-permute-start | bytes 663560 | tf_op jit(solution)/shard_map/ppermute | solution.py:323
  99.3 12.9 %collective-permute-start.14 = (f32[6,72,128]{2,1,0:T(8,128)S(1)}, f32[6,72,128]{2,1,0:T(8,128)S(1)}, u32[]{:S(2)}, u32[]{:S(2)}) collective-permute-start(f32[6,72,128]{2,1,0:T(8,128)S(1)} %get-tuple-element.40), channel_id=1, source_target_pairs={{0,6},{1,7},{2,4},{3,5},{4,2},{5,3},{6,0},{7,1},{8,14},{9,15},{10,... | collective-permute-start | bytes 663560 | tf_op jit(solution)/shard_map/ppermute | solution.py:323
  (1 other events, 16.8 us)

commit v6 on v5

--- a/solution.py
+++ b/solution.py
@@ -522,14 +522,14 @@
                 last = jnp.where(group == t, pltpu.roll(three[t], 32 + 32 * t, 1), last)
             tiles += three + [last]
         columns.append(jnp.concatenate(tiles, axis=0).astype(BF16))
-    wide = dot(jnp.concatenate(columns, axis=1), yb_ref[...]).astype(BF16)
+    wide = dot(jnp.concatenate(columns, axis=1), yb_ref[...])
     copies = []
     for slot in range(3):
         both = []
         for d in range(8):
             rows = wide[d * 72 + slot * KS : d * 72 + slot * KS + KS]
             both.append(jnp.concatenate([rows[:, :128], rows[:, 128:]], axis=0))
-        both = jnp.concatenate(both, axis=1)
+        both = jnp.concatenate(both, axis=1).astype(BF16)
         out = dot(xl_ref[...], jnp.concatenate([both, both], axis=0))
         for d in range(8):
             sent[slot, :, d] = out[:, d * 128 : d * 128 + 128].reshape(16, 8, 128)

time: 124 us -> 124 us (level)
  no operation moved by 1% of the time
where the time goes in v6:
time: 124 us; the launch traced here: 123 us
  Pallas kernels  47 us (38%)
  waiting for transfers between devices  37.6 us (30%)
  starting transfers between devices  37.4 us (30%)
    ppermute x15, waiting for transfers between devices, across(): return lax.ppermute(block, 'gy', [(i, i ^ sx) for i in range(8)])  28.9 us
    ppermute x15, starting transfers between devices, across(): return lax.ppermute(block, 'gy', [(i, i ^ sx) for i in range(8)])  14.3 us
    all_to_all x2, starting transfers between devices, exchange_first(): return lax.all_to_all(flat, 'gx', 0, 0, tiled=True).reshape(block.shape)  12.7 us
    all_to_all x1, starting transfers between devices, exchange_all(): lax.all_to_all(flat, ('gx', 'gy'), 0, 0, tiled=True).reshape(block.shape)  10.4 us
    pallas_call x1, Pallas kernels, analyse_grad(): pl.pallas_call(analyse_grad_kernel, grid=(2, 2), in_specs=[FIELD, FIELD,...  9.84 us
    all_to_all x1, waiting for transfers between devices, exchange_all(): lax.all_to_all(flat, ('gx', 'gy'), 0, 0, tiled=True).reshape(block.shape)  8.72 us
    pallas_call x1, Pallas kernels, mix_channels(): pl.pallas_call(mix_channels_kernel, grid=(2, 2), in_specs=[FIELD, FIELD,...  8.1 us
    pallas_call x1, Pallas kernels, analyse_input(): pl.pallas_call(analyse_input_kernel, grid=(2, 2), in_specs=[FIELD, whole(...  7.1 us
  transfers between devices with their start and end apart: 18, of which 14 were waited for; matrix products, arithmetic and copies ran while one was open for 0% of the time, Pallas kernels for 22%

profile of v6, /device:TPU:8, one launch (start us, length us, event | category | flops | bytes accessed | tf_op | source)
XLA Modules:
  0.0 122.9 jit_solution(4805071659353115582)
XLA Ops:
  0.6 9.8 %analyse_grad.1 = f32[16,8,3,8,128]{4,3,2,1,0:T(8,128)} custom-call(bf16[2,4,8,64,512]{4,3,2,1,0:T(8,128)(2,1)} %cot_ref.3, bf16[2,4,8,64,512]{4,3,2,1,0:T(8,128)(2,1)} %pre_ref.3, bf16[512,256]{1,0:T(8,128)(2,1)} %constant.24.clone.table_ref, bf16[192,512]{1,0:T(8,128)(2,1)} %constant.25.clone.zl_ref), custom_call_target="tpu_custom_call" | custom-call | flops 4000000000 | bytes 14000000 | tf_op jit(solution)/shard_map/analyse_grad/pallas_call | solution.py:187
  10.5 10.4 %all-to-all-start = ((f32[128,24,128]{2,1,0:T(8,128)}), f32[128,24,128]{2,1,0:T(8,128)S(1)}, u32[]{:S(2)}, u32[]{:S(2)}) async-start(f32[128,24,128]{2,1,0:T(8,128)} %bitcast.17), calls=%async_computation | async-start | bytes 3145728 | tf_op jit(solution)/shard_map/all_to_all | solution.py:664
  20.9 7.1 %analyse_input.1 = (f32[16,8,3,8,128]{4,3,2,1,0:T(8,128)}, bf16[256,256]{1,0:T(8,128)(2,1)}) custom-call(bf16[2,4,8,64,512]{4,3,2,1,0:T(8,128)(2,1)} %field_ref.1, bf16[512,256]{1,0:T(8,128)(2,1)} %constant.24.clone.table_ref, bf16[192,512]{1,0:T(8,128)(2,1)} %constant.25.clone.zl_ref, bf16[32,32]{1,0:T(8,128)(2,1)} %weight_ref.1), custom_call_target="tpu_custom_call" | custom-call | flops 4000000000 | bytes 6000000 | tf_op jit(solution)/shard_map/analyse_input/pallas_call | solution.py:242
  28.0 8.1 %mix_channels.1.mixed_hbm = bf16[2,4,8,64,512]{4,3,2,1,0:T(8,128)(2,1)} custom-call(bf16[2,4,8,64,512]{4,3,2,1,0:T(8,128)(2,1)} %cot_ref.3, bf16[2,4,8,64,512]{4,3,2,1,0:T(8,128)(2,1)} %pre_ref.3, bf16[256,256]{1,0:T(8,128)(2,1)} %get-tuple-element.23.mix_ref), custom_call_target="tpu_custom_call" | custom-call | flops 4000000000 | bytes 12000000 | tf_op jit(solution)/shard_map/mix_channels/pallas_call | solution.py:228
  36.1 8.7 %all-to-all-done = f32[128,24,128]{2,1,0:T(8,128)S(1)} async-done(((f32[128,24,128]{2,1,0:T(8,128)}), f32[128,24,128]{2,1,0:T(8,128)S(1)}, u32[]{:S(2)}, u32[]{:S(2)}) %all-to-all-start) | async-done | bytes 1572896 | tf_op jit(solution)/shard_map/all_to_all | solution.py:664
  44.8 3.3 %planes.1 = (f32[4,72,128]{2,1,0:T(8,128)S(1)}, f32[4,72,128]{2,1,0:T(8,128)S(1)}) custom-call(f32[16,8,3,8,128]{4,3,2,1,0:T(8,128)S(1)} %bitcast.12, bf16[48,256]{1,0:T(8,128)(2,1)S(1)} %copy-done.4, f32[8,3,16,128]{3,2,1,0:T(8,128)} %constant.26.clone.cy_hbm), custom_call_target="tpu_custom_call" | custom-call | flops 1000000000 | bytes 3000000 | tf_op jit(solution)/shard_map/planes/pallas_call | solution.py:409
  48.2 5.4 %all-to-all-start.2 = ((f32[16,192,128]{2,1,0:T(8,128)}), f32[16,192,128]{2,1,0:T(8,128)S(1)}, u32[]{:S(2)}, u32[]{:S(2)}) async-start(f32[16,192,128]{2,1,0:T(8,128)} %bitcast.16), calls=%async_computation.2 | async-start | bytes 3145728 | tf_op jit(solution)/shard_map/all_to_all | solution.py:669
  55.6 1.6 %collective-permute-start.2 = (f32[2,72,128]{2,1,0:T(8,128)S(1)}, f32[2,72,128]{2,1,0:T(8,128)S(1)}, u32[]{:S(2)}, u32[]{:S(2)}) collective-permute-start(f32[2,72,128]{2,1,0:T(8,128)S(1)} %get-tuple-element.28), channel_id=1, source_target_pairs={{0,4},{1,5},{2,6},{3,7},{4,0},{5,1},{6,2},{7,3},{8,12},{9,13},{10,... | collective-permute-start | bytes 221192 | tf_op jit(solution)/shard_map/ppermute | solution.py:323
  57.3 2.5 %collective-permute-start.3 = (f32[2,72,128]{2,1,0:T(8,128)S(1)}, f32[2,72,128]{2,1,0:T(8,128)S(1)}, u32[]{:S(2)}, u32[]{:S(2)}) collective-permute-start(f32[2,72,128]{2,1,0:T(8,128)S(1)} %get-tuple-element.29), channel_id=1, source_target_pairs={{0,6},{1,7},{2,4},{3,5},{4,2},{5,3},{6,0},{7,1},{8,14},{9,15},{10,... | collective-permute-start | bytes 221192 | tf_op jit(solution)/shard_map/ppermute | solution.py:323
  60.2 1.4 %collective-permute-done.2.refs_3_ = f32[2,72,128]{2,1,0:T(8,128)S(1)} collective-permute-done((f32[2,72,128]{2,1,0:T(8,128)S(1)}, f32[2,72,128]{2,1,0:T(8,128)S(1)}, u32[]{:S(2)}, u32[]{:S(2)}) %collective-permute-start.2) | collective-permute-done | bytes 73760 | tf_op jit(solution)/shard_map/ppermute | solution.py:323
  63.0 3.6 %mode_grad.1 = (f32[6,72,128]{2,1,0:T(8,128)S(1)}, f32[8,72,128]{2,1,0:T(8,128)S(1)}, bf16[1024,256]{1,0:T(8,128)(2,1)S(1)}) custom-call(f32[4,72,128]{2,1,0:T(8,128)S(1)} %get-tuple-element.25.keep_ref.refs_0_, f32[4,72,128]{2,1,0:T(8,128)S(1)} %collective-permute-done.cross_ref.refs_1_, f32[2,72,128]{2,1,0:T(8,128)S(1)} %collective-permute-done.1.refs_2_, ...), custom_call_target="tpu_custom_call" | custom-call | flops 1000000000 | bytes 4000000 | tf_op jit(solution)/shard_map/mode_grad/pallas_call | solution.py:490
  66.6 2.4 %collective-permute-start.9 = (f32[6,72,128]{2,1,0:T(8,128)S(1)}, f32[6,72,128]{2,1,0:T(8,128)S(1)}, u32[]{:S(2)}, u32[]{:S(2)}) collective-permute-start(f32[6,72,128]{2,1,0:T(8,128)S(1)} %get-tuple-element.30.refs_0_), channel_id=1, source_target_pairs={{0,6},{1,7},{2,4},{3,5},{4,2},{5,3},{6,0},{7,1},{8,14},{9,15},{10,... | collective-permute-start | bytes 663560 | tf_op jit(solution)/shard_map/ppermute | solution.py:323
  69.0 1.8 %collective-permute-start.5 = (f32[6,72,128]{2,1,0:T(8,128)S(1)}, f32[6,72,128]{2,1,0:T(8,128)S(1)}, u32[]{:S(2)}, u32[]{:S(2)}) collective-permute-start(f32[6,72,128]{2,1,0:T(8,128)S(1)} %get-tuple-element.30.refs_0_), channel_id=1, source_target_pairs={{0,2},{1,3},{2,0},{3,1},{4,6},{5,7},{6,4},{7,5},{8,10},{9,11},{10,... | collective-permute-start | bytes 663560 | tf_op jit(solution)/shard_map/ppermute | solution.py:323
  70.8 8.7 %collective-permute-done.9.refs_6_ = f32[6,72,128]{2,1,0:T(8,128)S(1)} collective-permute-done((f32[6,72,128]{2,1,0:T(8,128)S(1)}, f32[6,72,128]{2,1,0:T(8,128)S(1)}, u32[]{:S(2)}, u32[]{:S(2)}) %collective-permute-start.9) | collective-permute-done | bytes 221216 | tf_op jit(solution)/shard_map/ppermute | solution.py:323
  81.6 2.1 %backward.1 = f32[16,8,3,8,128]{4,3,2,1,0:T(8,128)} custom-call(f32[6,72,128]{2,1,0:T(8,128)S(1)} %get-tuple-element.30.refs_0_, f32[6,72,128]{2,1,0:T(8,128)S(1)} %collective-permute-done.4.refs_1_, f32[6,72,128]{2,1,0:T(8,128)S(1)} %collective-permute-done.5.refs_2_, f32[6,72,128]{2,1,0:T(8,128)S(1)} %collective-permute-done.6.refs_3_, ...), custom_call_target="tpu_custom_call" | custom-call | flops 1000000000 | bytes 4000000 | tf_op jit(solution)/shard_map/backward/pallas_call | solution.py:543
  83.7 7.2 %all-to-all-start.1 = ((f32[16,192,128]{2,1,0:T(8,128)}), f32[16,192,128]{2,1,0:T(8,128)S(1)}, u32[]{:S(2)}, u32[]{:S(2)}) async-start(f32[16,192,128]{2,1,0:T(8,128)} %bitcast.13), calls=%async_computation.1 | async-start | bytes 3145728 | tf_op jit(solution)/shard_map/all_to_all | solution.py:669
  90.9 2.3 %forward.1 = (f32[4,6,72,128]{3,2,1,0:T(8,128)S(1)}, f32[4,6,72,128]{3,2,1,0:T(8,128)S(1)}) custom-call(f32[16,8,3,8,128]{4,3,2,1,0:T(8,128)S(1)} %bitcast.10, bf16[48,256]{1,0:T(8,128)(2,1)S(1)} %copy-done.4, bf16[8,256,1024]{2,1,0:T(8,128)(2,1)} %constant.31.clone.yb_hbm), custom_call_target="tpu_custom_call" | custom-call | flops 1000000000 | bytes 4000000 | tf_op jit(solution)/shard_map/forward/pallas_call | solution.py:291
  93.3 2.4 %collective-permute-done.11.cross_ref = f32[4,6,72,128]{3,2,1,0:T(8,128)S(1)} collective-permute-done((f32[4,6,72,128]{3,2,1,0:T(8,128)S(1)}, f32[4,6,72,128]{3,2,1,0:T(8,128)S(1)}, u32[]{:S(2)}, u32[]{:S(2)}) %collective-permute-start.11) | collective-permute-done | bytes 884768 | tf_op jit(solution)/shard_map/ppermute | solution.py:323
  96.1 3.3 %collective-permute-start.13 = (f32[6,72,128]{2,1,0:T(8,128)S(1)}, f32[6,72,128]{2,1,0:T(8,128)S(1)}, u32[]{:S(2)}, u32[]{:S(2)}) collective-permute-start(f32[6,72,128]{2,1,0:T(8,128)S(1)} %get-tuple-element.39), channel_id=1, source_target_pairs={{0,4},{1,5},{2,6},{3,7},{4,0},{5,1},{6,2},{7,3},{8,12},{9,13},{10,... | collective-permute-start | bytes 663560 | tf_op jit(solution)/shard_map/ppermute | solution.py:323
  100.6 3.6 %collective-permute-done.12.refs_1_ = f32[6,72,128]{2,1,0:T(8,128)S(1)} collective-permute-done((f32[6,72,128]{2,1,0:T(8,128)S(1)}, f32[6,72,128]{2,1,0:T(8,128)S(1)}, u32[]{:S(2)}, u32[]{:S(2)}) %collective-permute-start.12) | collective-permute-done | bytes 221216 | tf_op jit(solution)/shard_map/ppermute | solution.py:323
  104.2 5.4 %collective-permute-done.13.refs_2_ = f32[6,72,128]{2,1,0:T(8,128)S(1)} collective-permute-done((f32[6,72,128]{2,1,0:T(8,128)S(1)}, f32[6,72,128]{2,1,0:T(8,128)S(1)}, u32[]{:S(2)}, u32[]{:S(2)}) %collective-permute-start.13) | collective-permute-done | bytes 221216 | tf_op jit(solution)/shard_map/ppermute | solution.py:323
  109.6 2.6 %collective-permute-done.14.refs_3_ = f32[6,72,128]{2,1,0:T(8,128)S(1)} collective-permute-done((f32[6,72,128]{2,1,0:T(8,128)S(1)}, f32[6,72,128]{2,1,0:T(8,128)S(1)}, u32[]{:S(2)}, u32[]{:S(2)}) %collective-permute-start.14) | collective-permute-done | bytes 221216 | tf_op jit(solution)/shard_map/ppermute | solution.py:323
  112.2 4.3 %spectral_grad.1 = f32[3,12,24,1024]{3,2,1,0:T(8,128)} custom-call(f32[8,72,128]{2,1,0:T(8,128)S(1)} %copy-done.2, f32[6,72,128]{2,1,0:T(8,128)S(1)} %get-tuple-element.37.refs_0_, f32[6,72,128]{2,1,0:T(8,128)S(1)} %collective-permute-done.12.refs_1_, f32[6,72,128]{2,1,0:T(8,128)S(1)} %collective-permute-done.13.refs_2_, ...), custom_call_target="tpu_custom_call" | custom-call | flops 1000000000 | bytes 4000000 | tf_op jit(solution)/shard_map/spectral_grad/pallas_call | solution.py:583
  116.5 6.2 %synthesise.1 = bf16[2,4,8,64,512]{4,3,2,1,0:T(8,128)(2,1)} custom-call(f32[16,8,3,8,128]{4,3,2,1,0:T(8,128)S(1)} %bitcast.11, bf16[256,512]{1,0:T(8,128)(2,1)S(1)} %copy-done.6, bf16[512,192]{1,0:T(8,128)(2,1)S(1)} %copy-done.5, bf16[2,4,8,64,512]{4,3,2,1,0:T(8,128)(2,1)} %mix_channels.1.mixed_hbm), custom_call_target="tpu_custom_call" | custom-call | flops 4000000000 | bytes 10000000 | tf_op jit(solution)/shard_map/synthesise/pallas_call | solution.py:644
  (37 shorter events, 7.7 us)
Async XLA Ops:
  10.5 34.4 %all-to-all-start = ((f32[128,24,128]{2,1,0:T(8,128)}), f32[128,24,128]{2,1,0:T(8,128)S(1)}, u32[]{:S(2)}, u32[]{:S(2)}) async-start(f32[128,24,128]{2,1,0:T(8,128)} %bitcast.17), calls=%async_computation | async-start | bytes 3145728 | tf_op jit(solution)/shard_map/all_to_all | solution.py:664
  44.8 18.2 %copy-start = (bf16[4,128,128]{2,1,0:T(8,128)(2,1)S(1)}, bf16[4,128,128]{2,1,0:T(8,128)(2,1)}, u32[]{:S(2)}) copy-start(bf16[4,128,128]{2,1,0:T(8,128)(2,1)} %constant.30.clone.refs_5_.refs_4_) | copy-start | bytes 393220
  48.2 35.5 %all-to-all-start.2 = ((f32[16,192,128]{2,1,0:T(8,128)}), f32[16,192,128]{2,1,0:T(8,128)S(1)}, u32[]{:S(2)}, u32[]{:S(2)}) async-start(f32[16,192,128]{2,1,0:T(8,128)} %bitcast.16), calls=%async_computation.2 | async-start | bytes 3145728 | tf_op jit(solution)/shard_map/all_to_all | solution.py:669
  53.6 1.4 %collective-permute-start = (f32[4,72,128]{2,1,0:T(8,128)S(1)}, f32[4,72,128]{2,1,0:T(8,128)S(1)}, u32[]{:S(2)}, u32[]{:S(2)}) collective-permute-start(f32[4,72,128]{2,1,0:T(8,128)S(1)} %get-tuple-element.26), channel_id=1, source_target_pairs={{0,1},{1,0},{2,3},{3,2},{4,5},{5,4},{6,7},{7,6},{8,9},{9,8},{10,11... | collective-permute-start | bytes 442376 | tf_op jit(solution)/shard_map/ppermute | solution.py:323
  55.0 5.2 %collective-permute-start.1 = (f32[2,72,128]{2,1,0:T(8,128)S(1)}, f32[2,72,128]{2,1,0:T(8,128)S(1)}, u32[]{:S(2)}, u32[]{:S(2)}) collective-permute-start(f32[2,72,128]{2,1,0:T(8,128)S(1)} %get-tuple-element.27), channel_id=1, source_target_pairs={{0,2},{1,3},{2,0},{3,1},{4,6},{5,7},{6,4},{7,5},{8,10},{9,11},{10,... | collective-permute-start | bytes 221192 | tf_op jit(solution)/shard_map/ppermute | solution.py:323
  55.6 6.0 %collective-permute-start.2 = (f32[2,72,128]{2,1,0:T(8,128)S(1)}, f32[2,72,128]{2,1,0:T(8,128)S(1)}, u32[]{:S(2)}, u32[]{:S(2)}) collective-permute-start(f32[2,72,128]{2,1,0:T(8,128)S(1)} %get-tuple-element.28), channel_id=1, source_target_pairs={{0,4},{1,5},{2,6},{3,7},{4,0},{5,1},{6,2},{7,3},{8,12},{9,13},{10,... | collective-permute-start | bytes 221192 | tf_op jit(solution)/shard_map/ppermute | solution.py:323
  57.3 5.8 %collective-permute-start.3 = (f32[2,72,128]{2,1,0:T(8,128)S(1)}, f32[2,72,128]{2,1,0:T(8,128)S(1)}, u32[]{:S(2)}, u32[]{:S(2)}) collective-permute-start(f32[2,72,128]{2,1,0:T(8,128)S(1)} %get-tuple-element.29), channel_id=1, source_target_pairs={{0,6},{1,7},{2,4},{3,5},{4,2},{5,3},{6,0},{7,1},{8,14},{9,15},{10,... | collective-permute-start | bytes 221192 | tf_op jit(solution)/shard_map/ppermute | solution.py:323
  63.0 18.6 %copy-start.3 = (bf16[128,96]{1,0:T(8,128)(2,1)S(1)}, bf16[128,96]{1,0:T(8,128)(2,1)}, u32[]{:S(2)}) copy-start(bf16[128,96]{1,0:T(8,128)(2,1)} %constant.32.clone.refs_8_) | copy-start | bytes 73732
  66.6 17.0 %copy-start.1 = (f32[8,72,128]{2,1,0:T(8,128)}, f32[8,72,128]{2,1,0:T(8,128)S(1)}, u32[]{:S(2)}) copy-start(f32[8,72,128]{2,1,0:T(8,128)S(1)} %get-tuple-element.32.grads_ref) | copy-start | bytes 884740
  66.6 12.8 %collective-permute-start.9 = (f32[6,72,128]{2,1,0:T(8,128)S(1)}, f32[6,72,128]{2,1,0:T(8,128)S(1)}, u32[]{:S(2)}, u32[]{:S(2)}) collective-permute-start(f32[6,72,128]{2,1,0:T(8,128)S(1)} %get-tuple-element.30.refs_0_), channel_id=1, source_target_pairs={{0,6},{1,7},{2,4},{3,5},{4,2},{5,3},{6,0},{7,1},{8,14},{9,15},{10,... | collective-permute-start | bytes 663560 | tf_op jit(solution)/shard_map/ppermute | solution.py:323
  69.0 10.4 %collective-permute-start.7 = (f32[6,72,128]{2,1,0:T(8,128)S(1)}, f32[6,72,128]{2,1,0:T(8,128)S(1)}, u32[]{:S(2)}, u32[]{:S(2)}) collective-permute-start(f32[6,72,128]{2,1,0:T(8,128)S(1)} %get-tuple-element.30.refs_0_), channel_id=1, source_target_pairs={{0,4},{1,5},{2,6},{3,7},{4,0},{5,1},{6,2},{7,3},{8,12},{9,13},{10,... | collective-permute-start | bytes 663560 | tf_op jit(solution)/shard_map/ppermute | solution.py:323
  69.0 11.1 %collective-permute-start.5 = (f32[6,72,128]{2,1,0:T(8,128)S(1)}, f32[6,72,128]{2,1,0:T(8,128)S(1)}, u32[]{:S(2)}, u32[]{:S(2)}) collective-permute-start(f32[6,72,128]{2,1,0:T(8,128)S(1)} %get-tuple-element.30.refs_0_), channel_id=1, source_target_pairs={{0,2},{1,3},{2,0},{3,1},{4,6},{5,7},{6,4},{7,5},{8,10},{9,11},{10,... | collective-permute-start | bytes 663560 | tf_op jit(solution)/shard_map/ppermute | solution.py:323
  70.8 9.3 %collective-permute-start.4 = (f32[6,72,128]{2,1,0:T(8,128)S(1)}, f32[6,72,128]{2,1,0:T(8,128)S(1)}, u32[]{:S(2)}, u32[]{:S(2)}) collective-permute-start(f32[6,72,128]{2,1,0:T(8,128)S(1)} %get-tuple-element.30.refs_0_), channel_id=1, source_target_pairs={{0,1},{1,0},{2,3},{3,2},{4,5},{5,4},{6,7},{7,6},{8,9},{9,8},{10,11... | collective-permute-start | bytes 663560 | tf_op jit(solution)/shard_map/ppermute | solution.py:323
  79.5 1.5 %collective-permute-start.10 = (f32[6,72,128]{2,1,0:T(8,128)S(1)}, f32[6,72,128]{2,1,0:T(8,128)S(1)}, u32[]{:S(2)}, u32[]{:S(2)}) collective-permute-start(f32[6,72,128]{2,1,0:T(8,128)S(1)} %collective-permute-done.9.refs_6_), channel_id=1, source_target_pairs={{0,1},{1,0},{2,3},{3,2},{4,5},{5,4},{6,7},{7,6},{8,9},{9,8},{10,11... | collective-permute-start | bytes 663560 | tf_op jit(solution)/shard_map/ppermute | solution.py:323
  79.5 1.8 %collective-permute-start.8 = (f32[6,72,128]{2,1,0:T(8,128)S(1)}, f32[6,72,128]{2,1,0:T(8,128)S(1)}, u32[]{:S(2)}, u32[]{:S(2)}) collective-permute-start(f32[6,72,128]{2,1,0:T(8,128)S(1)} %collective-permute-done.7.refs_4_), channel_id=1, source_target_pairs={{0,1},{1,0},{2,3},{3,2},{4,5},{5,4},{6,7},{7,6},{8,9},{9,8},{10,11... | collective-permute-start | bytes 663560 | tf_op jit(solution)/shard_map/ppermute | solution.py:323
  80.1 1.5 %collective-permute-start.6 = (f32[6,72,128]{2,1,0:T(8,128)S(1)}, f32[6,72,128]{2,1,0:T(8,128)S(1)}, u32[]{:S(2)}, u32[]{:S(2)}) collective-permute-start(f32[6,72,128]{2,1,0:T(8,128)S(1)} %collective-permute-done.5.refs_2_), channel_id=1, source_target_pairs={{0,1},{1,0},{2,3},{3,2},{4,5},{5,4},{6,7},{7,6},{8,9},{9,8},{10,11... | collective-permute-start | bytes 663560 | tf_op jit(solution)/shard_map/ppermute | solution.py:323
  83.7 32.9 %all-to-all-start.1 = ((f32[16,192,128]{2,1,0:T(8,128)}), f32[16,192,128]{2,1,0:T(8,128)S(1)}, u32[]{:S(2)}, u32[]{:S(2)}) async-start(f32[16,192,128]{2,1,0:T(8,128)} %bitcast.13), calls=%async_computation.1 | async-start | bytes 3145728 | tf_op jit(solution)/shard_map/all_to_all | solution.py:669
  90.9 21.3 %copy-start.2 = (f32[8,72,128]{2,1,0:T(8,128)S(1)}, f32[8,72,128]{2,1,0:T(8,128)}, u32[]{:S(2)}) copy-start(f32[8,72,128]{2,1,0:T(8,128)} %copy-done.1) | copy-start | bytes 884740
  93.2 2.5 %collective-permute-start.11 = (f32[4,6,72,128]{3,2,1,0:T(8,128)S(1)}, f32[4,6,72,128]{3,2,1,0:T(8,128)S(1)}, u32[]{:S(2)}, u32[]{:S(2)}) collective-permute-start(f32[4,6,72,128]{3,2,1,0:T(8,128)S(1)} %get-tuple-element.36), channel_id=1, source_target_pairs={{0,1},{1,0},{2,3},{3,2},{4,5},{5,4},{6,7},{7,6},{8,9},{9,8},{10,11... | collective-permute-start | bytes 2654216 | tf_op jit(solution)/shard_map/ppermute | solution.py:323
  95.7 20.8 %copy-start.5 = (bf16[512,192]{1,0:T(8,128)(2,1)S(1)}, bf16[512,192]{1,0:T(8,128)(2,1)}, u32[]{:S(2)}) copy-start(bf16[512,192]{1,0:T(8,128)(2,1)} %constant.35.clone.zl_ref) | copy-start | bytes 589828
  95.7 20.8 %copy-start.6 = (bf16[256,512]{1,0:T(8,128)(2,1)S(1)}, bf16[256,512]{1,0:T(8,128)(2,1)}, u32[]{:S(2)}) copy-start(bf16[256,512]{1,0:T(8,128)(2,1)} %constant.34.clone.table_ref) | copy-start | bytes 786436
  95.8 8.3 %collective-permute-start.12 = (f32[6,72,128]{2,1,0:T(8,128)S(1)}, f32[6,72,128]{2,1,0:T(8,128)S(1)}, u32[]{:S(2)}, u32[]{:S(2)}) collective-permute-start(f32[6,72,128]{2,1,0:T(8,128)S(1)} %get-tuple-element.38), channel_id=1, source_target_pairs={{0,2},{1,3},{2,0},{3,1},{4,6},{5,7},{6,4},{7,5},{8,10},{9,11},{10,... | collective-permute-start | bytes 663560 | tf_op jit(solution)/shard_map/ppermute | solution.py:323
  96.1 13.5 %collective-permute-start.13 = (f32[6,72,128]{2,1,0:T(8,128)S(1)}, f32[6,72,128]{2,1,0:T(8,128)S(1)}, u32[]{:S(2)}, u32[]{:S(2)}) collective-permute-start(f32[6,72,128]{2,1,0:T(8,128)S(1)} %get-tuple-element.39), channel_id=1, source_target_pairs={{0,4},{1,5},{2,6},{3,7},{4,0},{5,1},{6,2},{7,3},{8,12},{9,13},{10,... | collective-permute-start | bytes 663560 | tf_op jit(solution)/shard_map/ppermute | solution.py:323
  99.3 12.9 %collective-permute-start.14 = (f32[6,72,128]{2,1,0:T(8,128)S(1)}, f32[6,72,128]{2,1,0:T(8,128)S(1)}, u32[]{:S(2)}, u32[]{:S(2)}) collective-permute-start(f32[6,72,128]{2,1,0:T(8,128)S(1)} %get-tuple-element.40), channel_id=1, source_target_pairs={{0,6},{1,7},{2,4},{3,5},{4,2},{5,3},{6,0},{7,1},{8,14},{9,15},{10,... | collective-permute-start | bytes 663560 | tf_op jit(solution)/shard_map/ppermute | solution.py:323
  (1 other events, 16.8 us)

commit v7 on v6

--- a/solution.py
+++ b/solution.py
@@ -439,10 +439,13 @@
     )(keep, cross)
 
 
-def exchange_second(blocks):
+def exchange_cores(blocks):
     keep, cross = blocks
     cross = across(cross, 1)
-    pairs = pair_up(keep, cross)
+    return keep, cross, pair_up(keep, cross)
+
+
+def exchange_chips(keep, cross, pairs):
     return [keep, cross] + [across(pair, 2 * sx + 2) for sx, pair in enumerate(pairs)]
 
 
@@ -678,9 +681,10 @@
     mixed = mix_channels(cotangent, pre_activation, mix)
     got, *_ = lax.optimization_barrier((got, sent_input, mixed))
     blocks = planes(got, k)
-    sent_input, *_ = lax.optimization_barrier((sent_input, blocks[0]))
+    keep, cross, pairs = exchange_cores(blocks)
+    sent_input, *_ = lax.optimization_barrier((sent_input, pairs[0]))
     got_input = exchange_first(sent_input)
-    modes, grads, yb = mode_grad(exchange_second(blocks), weights, k)
+    modes, grads, yb = mode_grad(exchange_chips(keep, cross, pairs), weights, k)
     got_input, *_ = lax.optimization_barrier((got_input, modes))
     sums = reduce_cores(forward(got_input, k))
     back = exchange_first(backward(gather_second(modes), yb, k))

time: 124 us -> 123 us (level)
    ppermute x15, starting transfers between devices: 14.3 us -> 13 us  [across(): return lax.ppermute(block, 'gy', [(i, i ^ sx) for i in range(8)])]
  transfers between devices with their start and end apart: 18 -> 18, of which waited for: 14 -> 14; matrix products, arithmetic and copies ran while one was open for 0% -> 0% of each run, Pallas kernels for 22% -> 23%
where the time goes in v7:
time: 123 us; the launch traced here: 122 us
  Pallas kernels  47 us (38%)
  waiting for transfers between devices  36.8 us (30%)
  starting transfers between devices  36.2 us (29%)
    ppermute x15, waiting for transfers between devices, across(): return lax.ppermute(block, 'gy', [(i, i ^ sx) for i in range(8)])  28.1 us
    ppermute x15, starting transfers between devices, across(): return lax.ppermute(block, 'gy', [(i, i ^ sx) for i in range(8)])  13 us
    all_to_all x2, starting transfers between devices, exchange_first(): return lax.all_to_all(flat, 'gx', 0, 0, tiled=True).reshape(block.shape)  12.7 us
    all_to_all x1, starting transfers between devices, exchange_all(): lax.all_to_all(flat, ('gx', 'gy'), 0, 0, tiled=True).reshape(block.shape)  10.4 us
    pallas_call x1, Pallas kernels, analyse_grad(): pl.pallas_call(analyse_grad_kernel, grid=(2, 2), in_specs=[FIELD, FIELD,...  9.84 us
    all_to_all x1, waiting for transfers between devices, exchange_all(): lax.all_to_all(flat, ('gx', 'gy'), 0, 0, tiled=True).reshape(block.shape)  8.72 us
    pallas_call x1, Pallas kernels, mix_channels(): pl.pallas_call(mix_channels_kernel, grid=(2, 2), in_specs=[FIELD, FIELD,...  8.1 us
    pallas_call x1, Pallas kernels, analyse_input(): pl.pallas_call(analyse_input_kernel, grid=(2, 2), in_specs=[FIELD, whole(...  7.1 us
  transfers between devices with their start and end apart: 18, of which 14 were waited for; matrix products, arithmetic and copies ran while one was open for 0% of the time, Pallas kernels for 23%

profile of v7, /device:TPU:8, one launch (start us, length us, event | category | flops | bytes accessed | tf_op | source)
XLA Modules:
  0.0 121.7 jit_solution(8922790950156456688)
XLA Ops:
  0.6 9.8 %analyse_grad.1 = f32[16,8,3,8,128]{4,3,2,1,0:T(8,128)} custom-call(bf16[2,4,8,64,512]{4,3,2,1,0:T(8,128)(2,1)} %cot_ref.3, bf16[2,4,8,64,512]{4,3,2,1,0:T(8,128)(2,1)} %pre_ref.3, bf16[512,256]{1,0:T(8,128)(2,1)} %constant.24.clone.table_ref, bf16[192,512]{1,0:T(8,128)(2,1)} %constant.25.clone.zl_ref), custom_call_target="tpu_custom_call" | custom-call | flops 4000000000 | bytes 14000000 | tf_op jit(solution)/shard_map/analyse_grad/pallas_call | solution.py:187
  10.5 10.4 %all-to-all-start = ((f32[128,24,128]{2,1,0:T(8,128)}), f32[128,24,128]{2,1,0:T(8,128)S(1)}, u32[]{:S(2)}, u32[]{:S(2)}) async-start(f32[128,24,128]{2,1,0:T(8,128)} %bitcast.17), calls=%async_computation | async-start | bytes 3145728 | tf_op jit(solution)/shard_map/all_to_all | solution.py:667
  20.9 7.1 %analyse_input.1 = (f32[16,8,3,8,128]{4,3,2,1,0:T(8,128)}, bf16[256,256]{1,0:T(8,128)(2,1)}) custom-call(bf16[2,4,8,64,512]{4,3,2,1,0:T(8,128)(2,1)} %field_ref.1, bf16[512,256]{1,0:T(8,128)(2,1)} %constant.24.clone.table_ref, bf16[192,512]{1,0:T(8,128)(2,1)} %constant.25.clone.zl_ref, bf16[32,32]{1,0:T(8,128)(2,1)} %weight_ref.1), custom_call_target="tpu_custom_call" | custom-call | flops 4000000000 | bytes 6000000 | tf_op jit(solution)/shard_map/analyse_input/pallas_call | solution.py:242
  28.0 8.1 %mix_channels.1.mixed_hbm = bf16[2,4,8,64,512]{4,3,2,1,0:T(8,128)(2,1)} custom-call(bf16[2,4,8,64,512]{4,3,2,1,0:T(8,128)(2,1)} %cot_ref.3, bf16[2,4,8,64,512]{4,3,2,1,0:T(8,128)(2,1)} %pre_ref.3, bf16[256,256]{1,0:T(8,128)(2,1)} %get-tuple-element.23.mix_ref), custom_call_target="tpu_custom_call" | custom-call | flops 4000000000 | bytes 12000000 | tf_op jit(solution)/shard_map/mix_channels/pallas_call | solution.py:228
  36.1 8.7 %all-to-all-done = f32[128,24,128]{2,1,0:T(8,128)S(1)} async-done(((f32[128,24,128]{2,1,0:T(8,128)}), f32[128,24,128]{2,1,0:T(8,128)S(1)}, u32[]{:S(2)}, u32[]{:S(2)}) %all-to-all-start) | async-done | bytes 1572896 | tf_op jit(solution)/shard_map/all_to_all | solution.py:667
  44.8 3.3 %planes.1 = (f32[4,72,128]{2,1,0:T(8,128)S(1)}, f32[4,72,128]{2,1,0:T(8,128)S(1)}) custom-call(f32[16,8,3,8,128]{4,3,2,1,0:T(8,128)S(1)} %bitcast.12, bf16[48,256]{1,0:T(8,128)(2,1)S(1)} %copy-done.4, f32[8,3,16,128]{3,2,1,0:T(8,128)} %constant.26.clone.cy_hbm), custom_call_target="tpu_custom_call" | custom-call | flops 1000000000 | bytes 3000000 | tf_op jit(solution)/shard_map/planes/pallas_call | solution.py:409
  48.3 1.4 %collective-permute-done.cross_ref.refs_1_ = f32[4,72,128]{2,1,0:T(8,128)S(1)} collective-permute-done((f32[4,72,128]{2,1,0:T(8,128)S(1)}, f32[4,72,128]{2,1,0:T(8,128)S(1)}, u32[]{:S(2)}, u32[]{:S(2)}) %collective-permute-start) | collective-permute-done | bytes 147488 | tf_op jit(solution)/shard_map/ppermute | solution.py:323
  49.7 5.4 %all-to-all-start.2 = ((f32[16,192,128]{2,1,0:T(8,128)}), f32[16,192,128]{2,1,0:T(8,128)S(1)}, u32[]{:S(2)}, u32[]{:S(2)}) async-start(f32[16,192,128]{2,1,0:T(8,128)} %bitcast.16), calls=%async_computation.2 | async-start | bytes 3145728 | tf_op jit(solution)/shard_map/all_to_all | solution.py:672
  55.7 2.6 %collective-permute-start.3 = (f32[2,72,128]{2,1,0:T(8,128)S(1)}, f32[2,72,128]{2,1,0:T(8,128)S(1)}, u32[]{:S(2)}, u32[]{:S(2)}) collective-permute-start(f32[2,72,128]{2,1,0:T(8,128)S(1)} %get-tuple-element.29), channel_id=1, source_target_pairs={{0,6},{1,7},{2,4},{3,5},{4,2},{5,3},{6,0},{7,1},{8,14},{9,15},{10,... | collective-permute-start | bytes 221192 | tf_op jit(solution)/shard_map/ppermute | solution.py:323
  58.6 3.0 %collective-permute-done.2.refs_3_ = f32[2,72,128]{2,1,0:T(8,128)S(1)} collective-permute-done((f32[2,72,128]{2,1,0:T(8,128)S(1)}, f32[2,72,128]{2,1,0:T(8,128)S(1)}, u32[]{:S(2)}, u32[]{:S(2)}) %collective-permute-start.2) | collective-permute-done | bytes 73760 | tf_op jit(solution)/shard_map/ppermute | solution.py:323
  62.7 3.6 %mode_grad.1 = (f32[6,72,128]{2,1,0:T(8,128)S(1)}, f32[8,72,128]{2,1,0:T(8,128)S(1)}, bf16[1024,256]{1,0:T(8,128)(2,1)S(1)}) custom-call(f32[4,72,128]{2,1,0:T(8,128)S(1)} %get-tuple-element.25.keep_ref.refs_0_, f32[4,72,128]{2,1,0:T(8,128)S(1)} %collective-permute-done.cross_ref.refs_1_, f32[2,72,128]{2,1,0:T(8,128)S(1)} %collective-permute-done.1.refs_2_, ...), custom_call_target="tpu_custom_call" | custom-call | flops 1000000000 | bytes 4000000 | tf_op jit(solution)/shard_map/mode_grad/pallas_call | solution.py:493
  69.3 1.8 %collective-permute-start.5 = (f32[6,72,128]{2,1,0:T(8,128)S(1)}, f32[6,72,128]{2,1,0:T(8,128)S(1)}, u32[]{:S(2)}, u32[]{:S(2)}) collective-permute-start(f32[6,72,128]{2,1,0:T(8,128)S(1)} %get-tuple-element.30.refs_0_), channel_id=1, source_target_pairs={{0,2},{1,3},{2,0},{3,1},{4,6},{5,7},{6,4},{7,5},{8,10},{9,11},{10,... | collective-permute-start | bytes 663560 | tf_op jit(solution)/shard_map/ppermute | solution.py:323
  71.1 8.4 %collective-permute-done.9.refs_6_ = f32[6,72,128]{2,1,0:T(8,128)S(1)} collective-permute-done((f32[6,72,128]{2,1,0:T(8,128)S(1)}, f32[6,72,128]{2,1,0:T(8,128)S(1)}, u32[]{:S(2)}, u32[]{:S(2)}) %collective-permute-start.9) | collective-permute-done | bytes 221216 | tf_op jit(solution)/shard_map/ppermute | solution.py:323
  81.6 2.1 %backward.1 = f32[16,8,3,8,128]{4,3,2,1,0:T(8,128)} custom-call(f32[6,72,128]{2,1,0:T(8,128)S(1)} %get-tuple-element.30.refs_0_, f32[6,72,128]{2,1,0:T(8,128)S(1)} %collective-permute-done.4.refs_1_, f32[6,72,128]{2,1,0:T(8,128)S(1)} %collective-permute-done.5.refs_2_, f32[6,72,128]{2,1,0:T(8,128)S(1)} %collective-permute-done.6.refs_3_, ...), custom_call_target="tpu_custom_call" | custom-call | flops 1000000000 | bytes 4000000 | tf_op jit(solution)/shard_map/backward/pallas_call | solution.py:546
  83.7 7.3 %all-to-all-start.1 = ((f32[16,192,128]{2,1,0:T(8,128)}), f32[16,192,128]{2,1,0:T(8,128)S(1)}, u32[]{:S(2)}, u32[]{:S(2)}) async-start(f32[16,192,128]{2,1,0:T(8,128)} %bitcast.13), calls=%async_computation.1 | async-start | bytes 3145728 | tf_op jit(solution)/shard_map/all_to_all | solution.py:672
  91.0 2.3 %forward.1 = (f32[4,6,72,128]{3,2,1,0:T(8,128)S(1)}, f32[4,6,72,128]{3,2,1,0:T(8,128)S(1)}) custom-call(f32[16,8,3,8,128]{4,3,2,1,0:T(8,128)S(1)} %bitcast.10, bf16[48,256]{1,0:T(8,128)(2,1)S(1)} %copy-done.4, bf16[8,256,1024]{2,1,0:T(8,128)(2,1)} %constant.31.clone.yb_hbm), custom_call_target="tpu_custom_call" | custom-call | flops 1000000000 | bytes 4000000 | tf_op jit(solution)/shard_map/forward/pallas_call | solution.py:291
  93.4 2.4 %collective-permute-done.11.cross_ref = f32[4,6,72,128]{3,2,1,0:T(8,128)S(1)} collective-permute-done((f32[4,6,72,128]{3,2,1,0:T(8,128)S(1)}, f32[4,6,72,128]{3,2,1,0:T(8,128)S(1)}, u32[]{:S(2)}, u32[]{:S(2)}) %collective-permute-start.11) | collective-permute-done | bytes 884768 | tf_op jit(solution)/shard_map/ppermute | solution.py:323
  96.0 2.1 %collective-permute-start.13 = (f32[6,72,128]{2,1,0:T(8,128)S(1)}, f32[6,72,128]{2,1,0:T(8,128)S(1)}, u32[]{:S(2)}, u32[]{:S(2)}) collective-permute-start(f32[6,72,128]{2,1,0:T(8,128)S(1)} %get-tuple-element.39), channel_id=1, source_target_pairs={{0,4},{1,5},{2,6},{3,7},{4,0},{5,1},{6,2},{7,3},{8,12},{9,13},{10,... | collective-permute-start | bytes 663560 | tf_op jit(solution)/shard_map/ppermute | solution.py:323
  98.1 2.6 %collective-permute-start.14 = (f32[6,72,128]{2,1,0:T(8,128)S(1)}, f32[6,72,128]{2,1,0:T(8,128)S(1)}, u32[]{:S(2)}, u32[]{:S(2)}) collective-permute-start(f32[6,72,128]{2,1,0:T(8,128)S(1)} %get-tuple-element.40), channel_id=1, source_target_pairs={{0,6},{1,7},{2,4},{3,5},{4,2},{5,3},{6,0},{7,1},{8,14},{9,15},{10,... | collective-permute-start | bytes 663560 | tf_op jit(solution)/shard_map/ppermute | solution.py:323
  100.7 3.6 %collective-permute-done.12.refs_1_ = f32[6,72,128]{2,1,0:T(8,128)S(1)} collective-permute-done((f32[6,72,128]{2,1,0:T(8,128)S(1)}, f32[6,72,128]{2,1,0:T(8,128)S(1)}, u32[]{:S(2)}, u32[]{:S(2)}) %collective-permute-start.12) | collective-permute-done | bytes 221216 | tf_op jit(solution)/shard_map/ppermute | solution.py:323
  104.2 4.1 %collective-permute-done.13.refs_2_ = f32[6,72,128]{2,1,0:T(8,128)S(1)} collective-permute-done((f32[6,72,128]{2,1,0:T(8,128)S(1)}, f32[6,72,128]{2,1,0:T(8,128)S(1)}, u32[]{:S(2)}, u32[]{:S(2)}) %collective-permute-start.13) | collective-permute-done | bytes 221216 | tf_op jit(solution)/shard_map/ppermute | solution.py:323
  108.4 2.6 %collective-permute-done.14.refs_3_ = f32[6,72,128]{2,1,0:T(8,128)S(1)} collective-permute-done((f32[6,72,128]{2,1,0:T(8,128)S(1)}, f32[6,72,128]{2,1,0:T(8,128)S(1)}, u32[]{:S(2)}, u32[]{:S(2)}) %collective-permute-start.14) | collective-permute-done | bytes 221216 | tf_op jit(solution)/shard_map/ppermute | solution.py:323
  110.9 4.3 %spectral_grad.1 = f32[3,12,24,1024]{3,2,1,0:T(8,128)} custom-call(f32[8,72,128]{2,1,0:T(8,128)S(1)} %copy-done.2, f32[6,72,128]{2,1,0:T(8,128)S(1)} %get-tuple-element.37.refs_0_, f32[6,72,128]{2,1,0:T(8,128)S(1)} %collective-permute-done.12.refs_1_, f32[6,72,128]{2,1,0:T(8,128)S(1)} %collective-permute-done.13.refs_2_, ...), custom_call_target="tpu_custom_call" | custom-call | flops 1000000000 | bytes 4000000 | tf_op jit(solution)/shard_map/spectral_grad/pallas_call | solution.py:586
  115.3 6.2 %synthesise.1 = bf16[2,4,8,64,512]{4,3,2,1,0:T(8,128)(2,1)} custom-call(f32[16,8,3,8,128]{4,3,2,1,0:T(8,128)S(1)} %bitcast.11, bf16[256,512]{1,0:T(8,128)(2,1)S(1)} %copy-done.6, bf16[512,192]{1,0:T(8,128)(2,1)S(1)} %copy-done.5, bf16[2,4,8,64,512]{4,3,2,1,0:T(8,128)(2,1)} %mix_channels.1.mixed_hbm), custom_call_target="tpu_custom_call" | custom-call | flops 4000000000 | bytes 10000000 | tf_op jit(solution)/shard_map/synthesise/pallas_call | solution.py:647
  (37 shorter events, 7.4 us)
Async XLA Ops:
  10.5 34.4 %all-to-all-start = ((f32[128,24,128]{2,1,0:T(8,128)}), f32[128,24,128]{2,1,0:T(8,128)S(1)}, u32[]{:S(2)}, u32[]{:S(2)}) async-start(f32[128,24,128]{2,1,0:T(8,128)} %bitcast.17), calls=%async_computation | async-start | bytes 3145728 | tf_op jit(solution)/shard_map/all_to_all | solution.py:667
  28.0 16.8 %copy-start.4 = (bf16[48,256]{1,0:T(8,128)(2,1)S(1)}, bf16[48,256]{1,0:T(8,128)(2,1)}, u32[]{:S(2)}) copy-start(bf16[48,256]{1,0:T(8,128)(2,1)} %constant.27.clone.xl_ref) | copy-start | bytes 73732
  44.8 17.8 %copy-start = (bf16[4,128,128]{2,1,0:T(8,128)(2,1)S(1)}, bf16[4,128,128]{2,1,0:T(8,128)(2,1)}, u32[]{:S(2)}) copy-start(bf16[4,128,128]{2,1,0:T(8,128)(2,1)} %constant.30.clone.refs_5_.refs_4_) | copy-start | bytes 393220
  48.2 1.5 %collective-permute-start = (f32[4,72,128]{2,1,0:T(8,128)S(1)}, f32[4,72,128]{2,1,0:T(8,128)S(1)}, u32[]{:S(2)}, u32[]{:S(2)}) collective-permute-start(f32[4,72,128]{2,1,0:T(8,128)S(1)} %get-tuple-element.26), channel_id=1, source_target_pairs={{0,1},{1,0},{2,3},{3,2},{4,5},{5,4},{6,7},{7,6},{8,9},{9,8},{10,11... | collective-permute-start | bytes 442376 | tf_op jit(solution)/shard_map/ppermute | solution.py:323
  49.7 34.0 %all-to-all-start.2 = ((f32[16,192,128]{2,1,0:T(8,128)}), f32[16,192,128]{2,1,0:T(8,128)S(1)}, u32[]{:S(2)}, u32[]{:S(2)}) async-start(f32[16,192,128]{2,1,0:T(8,128)} %bitcast.16), calls=%async_computation.2 | async-start | bytes 3145728 | tf_op jit(solution)/shard_map/all_to_all | solution.py:672
  55.1 6.5 %collective-permute-start.2 = (f32[2,72,128]{2,1,0:T(8,128)S(1)}, f32[2,72,128]{2,1,0:T(8,128)S(1)}, u32[]{:S(2)}, u32[]{:S(2)}) collective-permute-start(f32[2,72,128]{2,1,0:T(8,128)S(1)} %get-tuple-element.28), channel_id=1, source_target_pairs={{0,4},{1,5},{2,6},{3,7},{4,0},{5,1},{6,2},{7,3},{8,12},{9,13},{10,... | collective-permute-start | bytes 221192 | tf_op jit(solution)/shard_map/ppermute | solution.py:323
  55.7 6.5 %collective-permute-start.3 = (f32[2,72,128]{2,1,0:T(8,128)S(1)}, f32[2,72,128]{2,1,0:T(8,128)S(1)}, u32[]{:S(2)}, u32[]{:S(2)}) collective-permute-start(f32[2,72,128]{2,1,0:T(8,128)S(1)} %get-tuple-element.29), channel_id=1, source_target_pairs={{0,6},{1,7},{2,4},{3,5},{4,2},{5,3},{6,0},{7,1},{8,14},{9,15},{10,... | collective-permute-start | bytes 221192 | tf_op jit(solution)/shard_map/ppermute | solution.py:323
  58.3 4.4 %collective-permute-start.1 = (f32[2,72,128]{2,1,0:T(8,128)S(1)}, f32[2,72,128]{2,1,0:T(8,128)S(1)}, u32[]{:S(2)}, u32[]{:S(2)}) collective-permute-start(f32[2,72,128]{2,1,0:T(8,128)S(1)} %get-tuple-element.27), channel_id=1, source_target_pairs={{0,2},{1,3},{2,0},{3,1},{4,6},{5,7},{6,4},{7,5},{8,10},{9,11},{10,... | collective-permute-start | bytes 221192 | tf_op jit(solution)/shard_map/ppermute | solution.py:323
  62.7 18.9 %copy-start.3 = (bf16[128,96]{1,0:T(8,128)(2,1)S(1)}, bf16[128,96]{1,0:T(8,128)(2,1)}, u32[]{:S(2)}) copy-start(bf16[128,96]{1,0:T(8,128)(2,1)} %constant.32.clone.refs_8_) | copy-start | bytes 73732
  67.0 12.5 %collective-permute-start.9 = (f32[6,72,128]{2,1,0:T(8,128)S(1)}, f32[6,72,128]{2,1,0:T(8,128)S(1)}, u32[]{:S(2)}, u32[]{:S(2)}) collective-permute-start(f32[6,72,128]{2,1,0:T(8,128)S(1)} %get-tuple-element.30.refs_0_), channel_id=1, source_target_pairs={{0,6},{1,7},{2,4},{3,5},{4,2},{5,3},{6,0},{7,1},{8,14},{9,15},{10,... | collective-permute-start | bytes 663560 | tf_op jit(solution)/shard_map/ppermute | solution.py:323
  68.2 11.2 %collective-permute-start.7 = (f32[6,72,128]{2,1,0:T(8,128)S(1)}, f32[6,72,128]{2,1,0:T(8,128)S(1)}, u32[]{:S(2)}, u32[]{:S(2)}) collective-permute-start(f32[6,72,128]{2,1,0:T(8,128)S(1)} %get-tuple-element.30.refs_0_), channel_id=1, source_target_pairs={{0,4},{1,5},{2,6},{3,7},{4,0},{5,1},{6,2},{7,3},{8,12},{9,13},{10,... | collective-permute-start | bytes 663560 | tf_op jit(solution)/shard_map/ppermute | solution.py:323
  69.3 10.8 %collective-permute-start.5 = (f32[6,72,128]{2,1,0:T(8,128)S(1)}, f32[6,72,128]{2,1,0:T(8,128)S(1)}, u32[]{:S(2)}, u32[]{:S(2)}) collective-permute-start(f32[6,72,128]{2,1,0:T(8,128)S(1)} %get-tuple-element.30.refs_0_), channel_id=1, source_target_pairs={{0,2},{1,3},{2,0},{3,1},{4,6},{5,7},{6,4},{7,5},{8,10},{9,11},{10,... | collective-permute-start | bytes 663560 | tf_op jit(solution)/shard_map/ppermute | solution.py:323
  71.1 9.0 %collective-permute-start.4 = (f32[6,72,128]{2,1,0:T(8,128)S(1)}, f32[6,72,128]{2,1,0:T(8,128)S(1)}, u32[]{:S(2)}, u32[]{:S(2)}) collective-permute-start(f32[6,72,128]{2,1,0:T(8,128)S(1)} %get-tuple-element.30.refs_0_), channel_id=1, source_target_pairs={{0,1},{1,0},{2,3},{3,2},{4,5},{5,4},{6,7},{7,6},{8,9},{9,8},{10,11... | collective-permute-start | bytes 663560 | tf_op jit(solution)/shard_map/ppermute | solution.py:323
  79.5 1.5 %collective-permute-start.10 = (f32[6,72,128]{2,1,0:T(8,128)S(1)}, f32[6,72,128]{2,1,0:T(8,128)S(1)}, u32[]{:S(2)}, u32[]{:S(2)}) collective-permute-start(f32[6,72,128]{2,1,0:T(8,128)S(1)} %collective-permute-done.9.refs_6_), channel_id=1, source_target_pairs={{0,1},{1,0},{2,3},{3,2},{4,5},{5,4},{6,7},{7,6},{8,9},{9,8},{10,11... | collective-permute-start | bytes 663560 | tf_op jit(solution)/shard_map/ppermute | solution.py:323
  79.5 1.8 %collective-permute-start.8 = (f32[6,72,128]{2,1,0:T(8,128)S(1)}, f32[6,72,128]{2,1,0:T(8,128)S(1)}, u32[]{:S(2)}, u32[]{:S(2)}) collective-permute-start(f32[6,72,128]{2,1,0:T(8,128)S(1)} %collective-permute-done.7.refs_4_), channel_id=1, source_target_pairs={{0,1},{1,0},{2,3},{3,2},{4,5},{5,4},{6,7},{7,6},{8,9},{9,8},{10,11... | collective-permute-start | bytes 663560 | tf_op jit(solution)/shard_map/ppermute | solution.py:323
  80.1 1.5 %collective-permute-start.6 = (f32[6,72,128]{2,1,0:T(8,128)S(1)}, f32[6,72,128]{2,1,0:T(8,128)S(1)}, u32[]{:S(2)}, u32[]{:S(2)}) collective-permute-start(f32[6,72,128]{2,1,0:T(8,128)S(1)} %collective-permute-done.5.refs_2_), channel_id=1, source_target_pairs={{0,1},{1,0},{2,3},{3,2},{4,5},{5,4},{6,7},{7,6},{8,9},{9,8},{10,11... | collective-permute-start | bytes 663560 | tf_op jit(solution)/shard_map/ppermute | solution.py:323
  83.7 31.6 %all-to-all-start.1 = ((f32[16,192,128]{2,1,0:T(8,128)}), f32[16,192,128]{2,1,0:T(8,128)S(1)}, u32[]{:S(2)}, u32[]{:S(2)}) async-start(f32[16,192,128]{2,1,0:T(8,128)} %bitcast.13), calls=%async_computation.1 | async-start | bytes 3145728 | tf_op jit(solution)/shard_map/all_to_all | solution.py:672
  90.9 20.0 %copy-start.2 = (f32[8,72,128]{2,1,0:T(8,128)S(1)}, f32[8,72,128]{2,1,0:T(8,128)}, u32[]{:S(2)}) copy-start(f32[8,72,128]{2,1,0:T(8,128)} %copy-done.1) | copy-start | bytes 884740
  93.3 2.5 %collective-permute-start.11 = (f32[4,6,72,128]{3,2,1,0:T(8,128)S(1)}, f32[4,6,72,128]{3,2,1,0:T(8,128)S(1)}, u32[]{:S(2)}, u32[]{:S(2)}) collective-permute-start(f32[4,6,72,128]{3,2,1,0:T(8,128)S(1)} %get-tuple-element.36), channel_id=1, source_target_pairs={{0,1},{1,0},{2,3},{3,2},{4,5},{5,4},{6,7},{7,6},{8,9},{9,8},{10,11... | collective-permute-start | bytes 2654216 | tf_op jit(solution)/shard_map/ppermute | solution.py:323
  95.8 19.5 %copy-start.5 = (bf16[512,192]{1,0:T(8,128)(2,1)S(1)}, bf16[512,192]{1,0:T(8,128)(2,1)}, u32[]{:S(2)}) copy-start(bf16[512,192]{1,0:T(8,128)(2,1)} %constant.35.clone.zl_ref) | copy-start | bytes 589828
  95.8 19.5 %copy-start.6 = (bf16[256,512]{1,0:T(8,128)(2,1)S(1)}, bf16[256,512]{1,0:T(8,128)(2,1)}, u32[]{:S(2)}) copy-start(bf16[256,512]{1,0:T(8,128)(2,1)} %constant.34.clone.table_ref) | copy-start | bytes 786436
  95.9 8.3 %collective-permute-start.12 = (f32[6,72,128]{2,1,0:T(8,128)S(1)}, f32[6,72,128]{2,1,0:T(8,128)S(1)}, u32[]{:S(2)}, u32[]{:S(2)}) collective-permute-start(f32[6,72,128]{2,1,0:T(8,128)S(1)} %get-tuple-element.38), channel_id=1, source_target_pairs={{0,2},{1,3},{2,0},{3,1},{4,6},{5,7},{6,4},{7,5},{8,10},{9,11},{10,... | collective-permute-start | bytes 663560 | tf_op jit(solution)/shard_map/ppermute | solution.py:323
  96.0 12.4 %collective-permute-start.13 = (f32[6,72,128]{2,1,0:T(8,128)S(1)}, f32[6,72,128]{2,1,0:T(8,128)S(1)}, u32[]{:S(2)}, u32[]{:S(2)}) collective-permute-start(f32[6,72,128]{2,1,0:T(8,128)S(1)} %get-tuple-element.39), channel_id=1, source_target_pairs={{0,4},{1,5},{2,6},{3,7},{4,0},{5,1},{6,2},{7,3},{8,12},{9,13},{10,... | collective-permute-start | bytes 663560 | tf_op jit(solution)/shard_map/ppermute | solution.py:323
  98.1 12.9 %collective-permute-start.14 = (f32[6,72,128]{2,1,0:T(8,128)S(1)}, f32[6,72,128]{2,1,0:T(8,128)S(1)}, u32[]{:S(2)}, u32[]{:S(2)}) collective-permute-start(f32[6,72,128]{2,1,0:T(8,128)S(1)} %get-tuple-element.40), channel_id=1, source_target_pairs={{0,6},{1,7},{2,4},{3,5},{4,2},{5,3},{6,0},{7,1},{8,14},{9,15},{10,... | collective-permute-start | bytes 663560 | tf_op jit(solution)/shard_map/ppermute | solution.py:323
  (1 other events, 0.7 us)
